TPU v7x, 256 devices: a whole 4x4x8 slice. The times are simulated.
256 devices in a mesh: seq: 32 (over y, x, core), tp: 8 (over z).
Axes of the slice: x: 4, y: 4, z: 8, core: 2. Of those that a mesh axis runs over, the one named last changes fastest.
Arguments:
- query: bfloat16 [32, 16384, 128], P('tp', 'seq'), may hold values from -12 to 12
- keyval: bfloat16 [2, 4, 16384, 128], P(None, None, 'seq'), may hold values from -6 to 6
- vert_blocks: int32 [32, 8], replicated, may hold values from 0 to 255, as said below
- slash_offsets: int32 [32, 8], replicated, may hold values from 0 to 255, as said below
- counts: int32 [32, 2], replicated, may hold values from 1 to 8, as said below
- out_weight: bfloat16 [4096, 8192], P('tp'), may hold values from -0.75 to 0.75
Outputs:
- projected: bfloat16 [16384, 8192], P(('seq', 'tp'))
Inputs may be any that keep to these rules, and one draw needn't show every extreme that they name: `vert_blocks`: the 8 entries of each head's row are distinct; only the first counts[h, 0] are used. `slash_offsets`: the 8 entries of each head's row are distinct and the first is 0; only the first counts[h, 1] are used. `counts`: each column reaches 8 for some head.
All inputs are finite; a program needn't handle non-finite values.
Results may differ from a plain program's by a relative error of at most 0.017.
Values may be sent and summed in bfloat16 or wider, within the bound.
No kernel may reach another device: no remote copies, remote signals or barrier semaphores. Data moves between devices by JAX's collectives and lax.ppermute only.
A program may use at most 128 MiB of HBM per device.

v0:
```python
import math

import jax
import jax.numpy as jnp
from jax import lax
from jax.sharding import PartitionSpec as P

BLK = 64


def plan_tiles(vertical, slash_list, list_counts, query_blocks):
    slot_count = vertical.shape[0]
    positions = jnp.arange(slot_count, dtype=jnp.int32)
    vert_live = positions < list_counts[0]
    vert_ok = vert_live[None, :] & (vertical[None, :] <= query_blocks[:, None])
    diag_block = query_blocks[:, None] - slash_list[None, :]
    covered = jnp.any(
        (diag_block[:, :, None] == vertical[None, None, :]) & vert_live[None, None, :], axis=2
    )
    diag_ok = (positions < list_counts[1])[None, :] & (diag_block >= 0) & jnp.logical_not(covered)
    tile_index = jnp.concatenate(
        [jnp.broadcast_to(vertical[None, :], diag_block.shape), jnp.maximum(diag_block, 0)], axis=1
    )
    tile_live = jnp.concatenate([vert_ok, diag_ok], axis=1)
    return (tile_index, tile_live)


def allowed_mask(tile_index, tile_live, query_blocks, block_size):
    offsets = jnp.arange(block_size, dtype=jnp.int32)
    query_pos = query_blocks[:, None] * block_size + offsets[None, :]
    key_pos = (tile_index[:, :, None] * block_size + offsets[None, None, :]).reshape(
        tile_index.shape[0], -1
    )
    live_keys = jnp.repeat(tile_live, block_size, axis=1)
    return live_keys[:, None, :] & (key_pos[:, None, :] <= query_pos[:, :, None])


def normalize(scores, allowed):
    masked = jnp.where(allowed, scores, -1e30)
    row_top = jnp.max(masked, axis=2, keepdims=True)
    weights = jnp.where(allowed, jnp.exp(masked - row_top), 0.0)
    row_total = jnp.sum(weights, axis=2, keepdims=True)
    return (weights.astype(jnp.bfloat16), row_total)


def attend_padded(
    queries, query_blocks, key_blocks, value_blocks, vertical, slash_list, list_counts
):
    tile_index, tile_live = plan_tiles(vertical, slash_list, list_counts, query_blocks)
    group_count, block_size, head_size = queries.shape
    key_tile = key_blocks[tile_index].reshape(group_count, -1, head_size)
    value_tile = value_blocks[tile_index].reshape(group_count, -1, head_size)
    scores = jnp.einsum("gqd,gkd->gqk", queries, key_tile, preferred_element_type=jnp.float32) * (
        1.0 / math.sqrt(head_size)
    )
    rounded, row_total = normalize(
        scores, allowed_mask(tile_index, tile_live, query_blocks, block_size)
    )
    summed = jnp.einsum("gqk,gkd->gqd", rounded, value_tile, preferred_element_type=jnp.float32)
    return (summed / row_total).astype(jnp.bfloat16)


def per_device(query, keyval, vert_blocks, slash_offsets, counts, out_weight):
    heads_here, local_rows, head_size = query.shape
    seq_count = lax.axis_size("seq")
    tp_count = lax.axis_size("tp")
    part_count = seq_count // heads_here
    part_rows = local_rows // part_count
    seq_index = lax.axis_index("seq")
    tp_index = lax.axis_index("tp")
    heads_kv = keyval.shape[1]
    pair_count = tp_count // heads_kv
    kv_head = tp_index // pair_count
    head_global = tp_index * heads_here + seq_index // part_count
    part_index = seq_index % part_count
    sendable = query.reshape(heads_here * part_count, part_rows, head_size)
    received = lax.all_to_all(sendable, "seq", split_axis=0, concat_axis=0, tiled=True)
    own_head = lax.dynamic_index_in_dim(keyval, kv_head, 1, keepdims=False)
    all_keys = lax.all_gather(own_head, "seq", axis=1, tiled=True)
    key_blocks = all_keys[0].reshape(-1, BLK, head_size)
    value_blocks = all_keys[1].reshape(-1, BLK, head_size)
    vertical = lax.dynamic_index_in_dim(vert_blocks, head_global, 0, keepdims=False)
    slash_list = lax.dynamic_index_in_dim(slash_offsets, head_global, 0, keepdims=False)
    list_counts = lax.dynamic_index_in_dim(counts, head_global, 0, keepdims=False)
    per_part = part_rows // BLK
    first_blocks = (
        jnp.arange(seq_count, dtype=jnp.int32)[:, None] * local_rows + part_index * part_rows
    ) // BLK
    query_blocks = (first_blocks + jnp.arange(per_part, dtype=jnp.int32)[None, :]).reshape(-1, 8)
    queries = received.reshape(-1, 8, BLK, head_size)

    def one_group(group_pair):
        group_queries, group_blocks = group_pair
        return attend_padded(
            group_queries, group_blocks, key_blocks, value_blocks, vertical, slash_list, list_counts
        )

    attended = lax.map(one_group, (queries, query_blocks)).reshape(seq_count, part_rows, head_size)
    returned = lax.all_to_all(attended, "seq", split_axis=0, concat_axis=0, tiled=True).reshape(
        heads_here, local_rows, head_size
    )
    weight_heads = out_weight.reshape(heads_here, head_size, -1)
    return lax.psum_scatter(
        lax.dot_general(
            returned, weight_heads, (((0, 2), (0, 1)), ((), ())), preferred_element_type=jnp.float32
        ).astype(jnp.bfloat16),
        "tp",
        scatter_dimension=0,
        tiled=True,
    )


def solution(mesh):
    return jax.shard_map(
        per_device,
        mesh=mesh,
        in_specs=(P("tp", "seq", None), P(None, None, "seq", None), P(), P(), P(), P("tp", None)),
        out_specs=P(("seq", "tp"), None),
        check_vma=False,
    )
```

profile of v0, /device:TPU:1, one launch (start us, length us, event | category | flops | bytes accessed | tf_op | source)
XLA Modules:
  0.0 271.3 jit_solution(17942607614153629061)
XLA Ops:
  6.5 1.2 copy-done
  7.8 0.7 constant_dynamic-slice_fusion.1
  8.5 8.7 %all-to-all-start = ((bf16[32,64,128]{2,1,0:T(8,128)(2,1)}), bf16[32,64,128]{2,1,0:T(8,128)(2,1)}, u32[]{:S(2)}, u32[]{:S(2)}) async-start(bf16[32,64,128]{2,1,0:T(8,128)(2,1)} %bitcast.57), calls=%async_computation | async-start | bytes 1048576 | tf_op jit(solution)/shard_map/all_to_all | solution.py:77
  17.3 0.9 dynamic-slice_reduce_fusion.2
  18.1 0.9 dynamic-slice_reduce_fusion
  19.1 53.1 %all-gather.3.cloned.1.call-done = bf16[2,1,16384,128]{3,2,1,0:T(8,128)(2,1)} async-done(((bf16[2,1,512,128]{3,2,1,0:T(8,128)(2,1)}), bf16[2,1,16384,128]{3,2,1,0:T(8,128)(2,1)}) %all-gather.3.cloned.1.call-update) | async-done | bytes 8388624 | tf_op jit(solution)/shard_map/all_gather | solution.py:79
  72.2 5.7 %fusion.18 = (bf16[1,1,16384,128]{3,2,1,0:T(8,128)(2,1)}, bf16[1,1,16384,128]{3,2,1,0:T(8,128)(2,1)}) fusion(bf16[2,1,16384,128]{3,2,1,0:T(8,128)(2,1)} %all-gather.3.cloned.1.call-done), kind=kLoop, calls=%fused_computation.49 | loop fusion | bytes 16777216 | tf_op jit(solution)/shard_map/slice | solution.py:81
  77.9 66.7 %while.10 = (s32[]{:T(128)}, bf16[4,8,64,128]{3,2,1,0:T(8,128)(2,1)}, s32[2]{0:T(128)S(1)}, s32[8]{0:T(128)S(1)}, s32[4,8]{1,0:T(4,128)S(1)}, /*index=5*/s32[8]{...) while((s32[]{:T(128)}, ...), condition=%wide.region_4.5_spmd, body=%wide.region_0.4_spmd.sunk | while | flops 275921824 | bytes 29974864 | solution.py:98
  78.0 0.7 fusion.40
  78.7 1.3 iota_compare_fusion.3
  79.9 0.3 and_reduce_fusion.2
  80.7 3.1 %gather_fusion.1 = bf16[128,64,128]{2,1,0:T(8,128)(2,1)S(1)} fusion(bf16[256,64,128]{2,1,0:T(8,128)(2,1)} %get-tuple-element.192, s32[1024]{0:T(1024)S(1)} %pad_clamp_fusion.2), kind=kCustom, calls=%fused_computation.clone.1 | custom fusion | bytes 4194816 | tf_op jit(solution)/shard_map/while/body/eval_jaxpr/gather | solution.py:51
  84.3 1.8 multiply_select_fusion.2
  86.1 1.0 fusion.41
  87.1 0.3 copy-done.1
  87.4 3.1 %gather_fusion = bf16[128,64,128]{2,1,0:T(8,128)(2,1)S(1)} fusion(bf16[256,64,128]{2,1,0:T(8,128)(2,1)} %get-tuple-element.193, s32[1024]{0:T(1024)S(1)} %pad_clamp_fusion.2), kind=kCustom, calls=%fused_computation.1.clone.1 | custom fusion | bytes 4194816 | tf_op jit(solution)/shard_map/while/body/eval_jaxpr/gather | solution.py:52
  90.6 4.0 %fusion.42 = bf16[4,8,64,128]{3,2,1,0:T(8,128)(2,1)} fusion(bf16[4,8,64,128]{3,2,1,0:T(8,128)(2,1)} %get-tuple-element.175, s32[]{:T(128)} %get-tuple-element.174, bf16[8,1024,128]{2,1,0:T(8,128)(2,1)S(1)} %bitcast.54, f32[8,64,1024]{2,1,0:T(8,128)} %copy-done.1, s32[8,64]{1,0:T(8,128)S(1)} %iota_add_fusion.2, ...), kind=kOutput, calls=%fused_computation.9.clone.1 | convolution fusion | flops 136971776 | bytes 6468096 | tf_op jit(solution)/shard_map/while/body/eval_jaxpr/gqk,gkd->gqd/dot_general | solution.py:59
  94.7 0.7 fusion.40
  95.3 1.3 iota_compare_fusion.3
  96.6 0.3 and_reduce_fusion.2
  97.4 3.1 %gather_fusion.1 = bf16[128,64,128]{2,1,0:T(8,128)(2,1)S(1)} fusion(bf16[256,64,128]{2,1,0:T(8,128)(2,1)} %get-tuple-element.192, s32[1024]{0:T(1024)S(1)} %pad_clamp_fusion.2), kind=kCustom, calls=%fused_computation.clone.1 | custom fusion | bytes 4194816 | tf_op jit(solution)/shard_map/while/body/eval_jaxpr/gather | solution.py:51
  101.0 1.8 multiply_select_fusion.2
  102.7 1.0 fusion.41
  103.8 0.3 copy-done.1
  104.1 3.1 %gather_fusion = bf16[128,64,128]{2,1,0:T(8,128)(2,1)S(1)} fusion(bf16[256,64,128]{2,1,0:T(8,128)(2,1)} %get-tuple-element.193, s32[1024]{0:T(1024)S(1)} %pad_clamp_fusion.2), kind=kCustom, calls=%fused_computation.1.clone.1 | custom fusion | bytes 4194816 | tf_op jit(solution)/shard_map/while/body/eval_jaxpr/gather | solution.py:52
  107.2 4.0 %fusion.42 = bf16[4,8,64,128]{3,2,1,0:T(8,128)(2,1)} fusion(bf16[4,8,64,128]{3,2,1,0:T(8,128)(2,1)} %get-tuple-element.175, s32[]{:T(128)} %get-tuple-element.174, bf16[8,1024,128]{2,1,0:T(8,128)(2,1)S(1)} %bitcast.54, f32[8,64,1024]{2,1,0:T(8,128)} %copy-done.1, s32[8,64]{1,0:T(8,128)S(1)} %iota_add_fusion.2, ...), kind=kOutput, calls=%fused_computation.9.clone.1 | convolution fusion | flops 136971776 | bytes 6468096 | tf_op jit(solution)/shard_map/while/body/eval_jaxpr/gqk,gkd->gqd/dot_general | solution.py:59
  111.3 0.7 fusion.40
  112.0 1.3 iota_compare_fusion.3
  113.3 0.3 and_reduce_fusion.2
  114.1 3.1 %gather_fusion.1 = bf16[128,64,128]{2,1,0:T(8,128)(2,1)S(1)} fusion(bf16[256,64,128]{2,1,0:T(8,128)(2,1)} %get-tuple-element.192, s32[1024]{0:T(1024)S(1)} %pad_clamp_fusion.2), kind=kCustom, calls=%fused_computation.clone.1 | custom fusion | bytes 4194816 | tf_op jit(solution)/shard_map/while/body/eval_jaxpr/gather | solution.py:51
  117.6 1.8 multiply_select_fusion.2
  119.4 1.0 fusion.41
  120.4 0.3 copy-done.1
  120.7 3.1 %gather_fusion = bf16[128,64,128]{2,1,0:T(8,128)(2,1)S(1)} fusion(bf16[256,64,128]{2,1,0:T(8,128)(2,1)} %get-tuple-element.193, s32[1024]{0:T(1024)S(1)} %pad_clamp_fusion.2), kind=kCustom, calls=%fused_computation.1.clone.1 | custom fusion | bytes 4194816 | tf_op jit(solution)/shard_map/while/body/eval_jaxpr/gather | solution.py:52
  123.9 4.0 %fusion.42 = bf16[4,8,64,128]{3,2,1,0:T(8,128)(2,1)} fusion(bf16[4,8,64,128]{3,2,1,0:T(8,128)(2,1)} %get-tuple-element.175, s32[]{:T(128)} %get-tuple-element.174, bf16[8,1024,128]{2,1,0:T(8,128)(2,1)S(1)} %bitcast.54, f32[8,64,1024]{2,1,0:T(8,128)} %copy-done.1, s32[8,64]{1,0:T(8,128)S(1)} %iota_add_fusion.2, ...), kind=kOutput, calls=%fused_computation.9.clone.1 | convolution fusion | flops 136971776 | bytes 6468096 | tf_op jit(solution)/shard_map/while/body/eval_jaxpr/gqk,gkd->gqd/dot_general | solution.py:59
  128.0 0.7 fusion.40
  128.7 1.3 iota_compare_fusion.3
  129.9 0.3 and_reduce_fusion.2
  130.5 0.1 and.110
  130.7 3.1 %gather_fusion.1 = bf16[128,64,128]{2,1,0:T(8,128)(2,1)S(1)} fusion(bf16[256,64,128]{2,1,0:T(8,128)(2,1)} %get-tuple-element.192, s32[1024]{0:T(1024)S(1)} %pad_clamp_fusion.2), kind=kCustom, calls=%fused_computation.clone.1 | custom fusion | bytes 4194816 | tf_op jit(solution)/shard_map/while/body/eval_jaxpr/gather | solution.py:51
  134.3 1.8 multiply_select_fusion.2
  136.1 1.0 fusion.41
  137.1 0.3 copy-done.1
  137.4 3.1 %gather_fusion = bf16[128,64,128]{2,1,0:T(8,128)(2,1)S(1)} fusion(bf16[256,64,128]{2,1,0:T(8,128)(2,1)} %get-tuple-element.193, s32[1024]{0:T(1024)S(1)} %pad_clamp_fusion.2), kind=kCustom, calls=%fused_computation.1.clone.1 | custom fusion | bytes 4194816 | tf_op jit(solution)/shard_map/while/body/eval_jaxpr/gather | solution.py:52
  140.6 4.0 %fusion.42 = bf16[4,8,64,128]{3,2,1,0:T(8,128)(2,1)} fusion(bf16[4,8,64,128]{3,2,1,0:T(8,128)(2,1)} %get-tuple-element.175, s32[]{:T(128)} %get-tuple-element.174, bf16[8,1024,128]{2,1,0:T(8,128)(2,1)S(1)} %bitcast.54, f32[8,64,1024]{2,1,0:T(8,128)} %copy-done.1, s32[8,64]{1,0:T(8,128)S(1)} %iota_add_fusion.2, ...), kind=kOutput, calls=%fused_computation.9.clone.1 | convolution fusion | flops 136971776 | bytes 6468096 | tf_op jit(solution)/shard_map/while/body/eval_jaxpr/gqk,gkd->gqd/dot_general | solution.py:59
  144.6 17.0 %all_to_all.10 = bf16[32,64,128]{2,1,0:T(8,128)(2,1)S(1)} all-to-all(bf16[32,64,128]{2,1,0:T(8,128)(2,1)} %bitcast.58), channel_id=1, replica_groups=mesh['seq'=32,'tp'=8] {'seq'}, dimensions={0} | all-to-all | bytes 1048576 | tf_op jit(solution)/shard_map/all_to_all | solution.py:99
  161.6 10.1 %bitcast_convert_fusion = bf16[512,8192]{1,0:T(8,128)(2,1)} fusion(bf16[4,512,128]{2,1,0:T(8,128)(2,1)S(1)} %bitcast.59, bf16[4,128,8192]{2,1,0:T(8,128)(2,1)} %bitcast.60), kind=kOutput, calls=%fused_computation.33 | convolution fusion | flops 4299161600 | bytes 17301504 | tf_op jit(solution)/shard_map/dot_general | solution.py:104
  171.7 92.7 %reduce-scatter.2.cloned.1.call-done = bf16[64,8192]{1,0:T(8,128)(2,1)} async-done(((bf16[512,8192]{1,0:T(8,128)(2,1)}), bf16[64,8192]{1,0:T(8,128)(2,1)}) %reduce-scatter.2.cloned.1.call-update) | async-done | bytes 1048592 | tf_op jit(solution)/shard_map/reduce_scatter | solution.py:103
  (83 shorter events, 4.0 us)
Async XLA Ops:
  6.5 1.2 copy-start
  6.5 65.7 %all-gather.3.cloned.1.call-start = ((), (), s32[]{:S(2)}) async-start(), calls=%async_computation.4 | async-start | bytes 8650752 | tf_op jit(solution)/shard_map/all_gather | solution.py:79
  8.5 69.4 %all-to-all-start = ((bf16[32,64,128]{2,1,0:T(8,128)(2,1)}), bf16[32,64,128]{2,1,0:T(8,128)(2,1)}, u32[]{:S(2)}, u32[]{:S(2)}) async-start(bf16[32,64,128]{2,1,0:T(8,128)(2,1)} %bitcast.57), calls=%async_computation | async-start | bytes 1048576 | tf_op jit(solution)/shard_map/all_to_all | solution.py:77
  17.2 247.3 %reduce-scatter.2.cloned.1.call-start = ((), (), s32[]{:S(2)}) async-start(), calls=%async_computation.3 | async-start | bytes 9437184 | tf_op jit(solution)/shard_map/reduce_scatter | solution.py:103
  86.1 1.4 copy-start.1
  102.7 1.4 copy-start.1
  119.4 1.4 copy-start.1
  136.1 1.4 copy-start.1
Sparse Core Ops, SparseCore 0:
  10.0 62.1 all-gather.2
  171.8 92.5 reduce-scatter.1
where the time goes:
time: 272 us; the launch traced here: 271 us
  waiting for transfers between devices  146 us (54%)
  local copies, waits for them, and re-layouts  40.5 us (15%)
  matrix products  33.2 us (12%)
  blocking collectives  17 us (6%)
  between operations  13.5 us (5%)
  other arithmetic  12.2 us (4%)
  starting transfers between devices  8.7 us (3%)
    reduce_scatter x1, waiting for transfers between devices, per_device(): lax.psum_scatter(lax.dot_general(returned, weight_heads, (((0, 2), (0, 1)...  92.7 us
    all_gather x1, waiting for transfers between devices, per_device(): all_keys = lax.all_gather(own_head, 'seq', axis=1, tiled=True)  53.1 us
    all_to_all x1, blocking collectives, per_device(): lax.all_to_all(attended, 'seq', split_axis=0, concat_axis=0, tiled=True)  17 us
    dot_general x4, matrix products, attend_padded(): jnp.einsum('gqk,gkd->gqd', rounded, value_tile, preferred_element_type=jn...  16.1 us
    gather x4, local copies, waits for them, and re-layouts, attend_padded(): key_tile = key_blocks[tile_index].reshape(group_count, -1, head_size)  12.6 us
    gather x4, local copies, waits for them, and re-layouts, attend_padded(): value_tile = value_blocks[tile_index].reshape(group_count, -1, head_size)  12.5 us
    dot_general x1, matrix products, per_device(): lax.dot_general(returned, weight_heads, (((0, 2), (0, 1)), ((), ())), pre...  10.1 us
    all_to_all x1, starting transfers between devices, per_device(): lax.all_to_all(sendable, 'seq', split_axis=0, concat_axis=0, tiled=True)  8.66 us
  transfers between devices with their start and end apart: 3, of which 2 were waited for; matrix products, arithmetic and copies ran while one was open for 3% of the time, Pallas kernels for 0%

commit v1 on v0

v1 whole, which is shorter than its diff:
```python
import functools
import math

import jax
import jax.numpy as jnp
from jax import lax
from jax.experimental import pallas as pl
from jax.experimental.pallas import tpu as pltpu
from jax.sharding import PartitionSpec as P

BLK = 64
NY, NX, NC = 4, 4, 2
DEAD = 1 << 20
SCALE = math.log2(math.e)


def seq_perm(move):
    pairs = []
    for y in range(NY):
        for x in range(NX):
            for c in range(NC):
                ty, tx, tc = move(y, x, c)
                pairs.append(((y * NX + x) * NC + c, ((ty % NY) * NX + tx % NX) * NC + tc))
    return pairs


A_UP = seq_perm(lambda y, x, c: (y, x + 1, c) if c == 0 else (y + 1, x, c))
A_DOWN = seq_perm(lambda y, x, c: (y, x - 1, c) if c == 0 else (y - 1, x, c))
B_UP = seq_perm(lambda y, x, c: (y + 1, x, c) if c == 0 else (y, x + 1, c))
B_DOWN = seq_perm(lambda y, x, c: (y - 1, x, c) if c == 0 else (y, x - 1, c))
SWAP = seq_perm(lambda y, x, c: (y, x, 1 - c))


def send(a, pairs):
    return lax.ppermute(a, "seq", pairs)


def gather_keyval(own):
    up, down = send(own, A_UP), send(own, A_DOWN)
    far = jnp.stack([send(up[0], A_UP), send(down[1], A_DOWN)])
    line = jnp.stack([own, up, down, far])
    up2, down2 = send(line, B_UP), send(line, B_DOWN)
    far_k, far_v = send(up2[:, 0], B_UP), send(down2[:, 1], B_DOWN)
    mine = [line, up2, down2, far_k, far_v]
    return mine + [send(a, SWAP) for a in mine]


def shard_slots(seq_index):
    shard = jnp.arange(NY * NX * NC, dtype=jnp.int32)

    def parts(i):
        return i // (NX * NC), (i // NC) % NX, i % NC

    ys, xs, cs = parts(shard)
    y0, x0, c0 = parts(seq_index)
    order = jnp.array([0, 2, 3, 1], jnp.int32)
    in_y, in_x = order[(ys - y0) % NY], order[(xs - x0) % NX]
    first = jnp.where(cs == 0, in_x, in_y)
    second = jnp.where(cs == 0, in_y, in_x)
    return (cs != c0) * 16 + second * 4 + first


def attend_kernel(
    slots_ref, vert_ref, diag_ref, q_ref, kpv_ref, kpd_ref,
    l0, u0, d0, fk0, fv0, l1, u1, d1, fk1, fv1,
    o_ref, kbuf, vbuf, sv_ref, pv_ref, od_ref, tot_ref, sems,
):
    heads, rows, width = q_ref.shape
    blocks = rows // BLK
    per = rows // BLK
    copies = ([], [])
    for side, (line, up, down, fk, fv) in enumerate(((l0, u0, d0, fk0, fv0), (l1, u1, d1, fk1, fv1))):
        for which, buf in enumerate((kbuf, vbuf)):
            for j, src in enumerate((line, up, down, (fk, fv)[which])):
                for i in range(4):
                    piece = src.at[i] if j == 3 else src.at[i, which]
                    slot = side * 16 + j * 4 + i
                    copies[which].append(
                        pltpu.make_async_copy(piece, buf.at[slot], sems.at[which, slot])
                    )
    for c in copies[0] + copies[1]:
        c.start()
    for c in copies[0]:
        c.wait()
    for c in copies[1]:
        c.wait()

    def tile(buf, block):
        return buf[slots_ref[block // per], pl.ds(pl.multiple_of((block % per) * BLK, BLK), BLK), :]

    scale = SCALE / math.sqrt(width)
    nt = (((1,), (1,)), ((), ()))

    def one_head(h, carry):
        verts = [vert_ref[h, c] for c in range(8)]
        k_v = jnp.concatenate([tile(kbuf, v) for v in verts], axis=0)
        sv_ref[...] = lax.dot_general(q_ref[h], k_v, nt, preferred_element_type=jnp.float32)
        kpv = kpv_ref[h]
        for b in range(blocks):
            r = slice(b * BLK, (b + 1) * BLK)
            diags = [diag_ref[h * blocks + b, c] for c in range(8)]
            k_d = jnp.concatenate([tile(kbuf, v) for v in diags], axis=0)
            s_d = lax.dot_general(q_ref[h, r, :], k_d, nt, preferred_element_type=jnp.float32)
            s_v = sv_ref[r, :]
            qpos = b * BLK + lax.broadcasted_iota(jnp.int32, (BLK, 1), 0)
            s_d = jnp.where(kpd_ref[h * blocks + b] <= qpos, s_d, -1e30)
            s_v = jnp.where(kpv <= qpos, s_v, -1e30)
            top = jnp.maximum(
                jnp.max(s_d, axis=1, keepdims=True), jnp.max(s_v, axis=1, keepdims=True)
            )
            p_d = jnp.exp2((s_d - top) * scale)
            p_v = jnp.exp2((s_v - top) * scale)
            tot_ref[r, :] = jnp.sum(p_d, axis=1, keepdims=True) + jnp.sum(
                p_v, axis=1, keepdims=True
            )
            pv_ref[r, :] = p_v.astype(jnp.bfloat16)
            v_d = jnp.concatenate([tile(vbuf, v) for v in diags], axis=0)
            od_ref[r, :] = jnp.dot(
                p_d.astype(jnp.bfloat16), v_d, preferred_element_type=jnp.float32
            )
        v_v = jnp.concatenate([tile(vbuf, v) for v in verts], axis=0)
        o_v = jnp.dot(pv_ref[...], v_v, preferred_element_type=jnp.float32)
        o_ref[h] = ((o_v + od_ref[...]) / tot_ref[...]).astype(jnp.bfloat16)
        return carry

    lax.fori_loop(0, heads, one_head, 0)


def attend(query, pieces, slots, vertical, slash, counts, seq_index):
    heads, rows, width = query.shape
    blocks = rows // BLK
    slot = jnp.arange(8, dtype=jnp.int32)
    first = seq_index * blocks
    vert_live = slot[None, :] < counts[:, 0:1]
    diag = first + jnp.arange(blocks, dtype=jnp.int32)[None, :, None] - slash[:, None, :]
    covered = jnp.any(
        (diag[:, :, :, None] == vertical[:, None, None, :]) & vert_live[:, None, None, :], axis=3
    )
    diag_live = (slot < counts[:, 1:2])[:, None, :] & (diag >= 0) & jnp.logical_not(covered)
    within = jnp.arange(BLK, dtype=jnp.int32)
    kpv = jnp.where(
        vert_live[:, :, None], (vertical - first)[:, :, None] * BLK + within, DEAD
    ).reshape(heads, 1, 8 * BLK)
    kpd = jnp.where(
        diag_live[:, :, :, None], (diag - first)[:, :, :, None] * BLK + within, DEAD
    ).reshape(heads * blocks, 1, 8 * BLK)
    diag = jnp.maximum(diag, 0).reshape(heads * blocks, 8)
    smem = pl.BlockSpec(memory_space=pltpu.SMEM)
    vmem = pl.BlockSpec(memory_space=pltpu.VMEM)
    hbm = pl.BlockSpec(memory_space=pl.ANY)
    f32 = jnp.float32
    return pl.pallas_call(
        attend_kernel,
        out_shape=jax.ShapeDtypeStruct((heads, rows, width), jnp.bfloat16),
        in_specs=[smem] * 3 + [vmem] * 3 + [hbm] * len(pieces),
        out_specs=vmem,
        scratch_shapes=[
            pltpu.VMEM((32, rows, width), jnp.bfloat16),
            pltpu.VMEM((32, rows, width), jnp.bfloat16),
            pltpu.VMEM((rows, 8 * BLK), f32),
            pltpu.VMEM((rows, 8 * BLK), jnp.bfloat16),
            pltpu.VMEM((rows, width), f32),
            pltpu.VMEM((rows, 1), f32),
            pltpu.SemaphoreType.DMA((2, 32)),
        ],
        compiler_params=pltpu.CompilerParams(vmem_limit_bytes=24 * 2**20),
        name="attend",
    )(slots, vertical, diag, query, kpv, kpd, *pieces)


def per_device(query, keyval, vert_blocks, slash_offsets, counts, out_weight):
    heads, rows, width = query.shape
    seq_index = lax.axis_index("seq")
    tp_index = lax.axis_index("tp")
    kv_head = tp_index // (lax.axis_size("tp") // keyval.shape[1])
    own = lax.dynamic_index_in_dim(keyval, kv_head, 1, keepdims=False)
    pieces = gather_keyval(own)

    def mine(a):
        return lax.dynamic_slice_in_dim(a, tp_index * heads, heads, 0)

    attended = attend(
        query, pieces, shard_slots(seq_index), mine(vert_blocks), mine(slash_offsets),
        mine(counts), seq_index,
    )
    weight_heads = out_weight.reshape(heads, width, -1)
    partial = lax.dot_general(
        attended, weight_heads, (((0, 2), (0, 1)), ((), ())), preferred_element_type=jnp.float32
    ).astype(jnp.bfloat16)
    return lax.psum_scatter(partial, "tp", scatter_dimension=0, tiled=True)


def solution(mesh):
    return jax.shard_map(
        per_device,
        mesh=mesh,
        in_specs=(P("tp", "seq", None), P(None, None, "seq", None), P(), P(), P(), P("tp", None)),
        out_specs=P(("seq", "tp"), None),
        check_vma=False,
    )
```

time: 272 us -> 196 us (0.72)
  waiting for transfers between devices: 146 us -> 110 us
  local copies, waits for them, and re-layouts: 40.5 us -> 13.4 us
  matrix products: 33.2 us -> 6.64 us
  Pallas kernels: 0 us -> 23.6 us
  starting transfers between devices: 8.7 us -> 27 us
  blocking collectives: 17 us -> 0 us
  other arithmetic: 12.2 us -> 1.32 us
    all_gather x1 -> x0, waiting for transfers between devices: 53.1 us -> none  [per_device(): all_keys = lax.all_gather(own_head, 'seq', axis=1, tiled=True)]
    ppermute x0 -> x13, starting transfers between devices: none -> 27 us  [send(): return lax.ppermute(a, 'seq', pairs)]
    dot_general x9 -> x1, matrix products: 33.2 us -> 6.64 us  [per_device(): lax.dot_general(attended, weight_heads, (((0, 2), (0, 1)), ((), ())), pre...]
    gather x8 -> x0, local copies, waits for them, and re-layouts: 25.1 us -> none  [the longest x4 12.6 us: attend_padded(): key_tile = key_blocks[tile_index].reshape(group_count, -1, head_size)]
    pallas_call x0 -> x1, Pallas kernels: none -> 23.6 us  [attend(): pl.pallas_call(attend_kernel, out_shape=jax.ShapeDtypeStruct((heads, rows...]
    all_to_all x1 -> x0, blocking collectives: 17 us -> none  [per_device(): lax.all_to_all(attended, 'seq', split_axis=0, concat_axis=0, tiled=True)]
    ppermute x0 -> x13, waiting for transfers between devices: none -> 14.8 us  [send(): return lax.ppermute(a, 'seq', pairs)]
    all_to_all x1 -> x0, starting transfers between devices: 8.66 us -> none  [per_device(): lax.all_to_all(sendable, 'seq', split_axis=0, concat_axis=0, tiled=True)]
  transfers between devices with their start and end apart: 3 -> 14, of which waited for: 2 -> 6; matrix products, arithmetic and copies ran while one was open for 3% -> 6% of each run, Pallas kernels for 0% -> 0%
where the time goes in v1:
time: 196 us
  waiting for transfers between devices  110 us (56%)
  starting transfers between devices  27 us (14%)
  Pallas kernels  23.6 us (12%)
  between operations  13.7 us (7%)
  local copies, waits for them, and re-layouts  13.4 us (7%)
  matrix products  6.64 us (3%)
    reduce_scatter x1, waiting for transfers between devices, per_device(): return lax.psum_scatter(partial, 'tp', scatter_dimension=0, tiled=True)  95.5 us
    ppermute x13, starting transfers between devices, send(): return lax.ppermute(a, 'seq', pairs)  27 us
    pallas_call x1, Pallas kernels, attend(): pl.pallas_call(attend_kernel, out_shape=jax.ShapeDtypeStruct((heads, rows...  23.6 us
    ppermute x13, waiting for transfers between devices, send(): return lax.ppermute(a, 'seq', pairs)  14.8 us
    ppermute x5, local copies, waits for them, and re-layouts, send(): return lax.ppermute(a, 'seq', pairs)  6.72 us
    dot_general x1, matrix products, per_device(): lax.dot_general(attended, weight_heads, (((0, 2), (0, 1)), ((), ())), pre...  6.64 us
  transfers between devices with their start and end apart: 14, of which 6 were waited for; matrix products, arithmetic and copies ran while one was open for 6% of the time, Pallas kernels for 0%

profile of v1, /device:TPU:1, one launch (start us, length us, event | category | flops | bytes accessed | tf_op | source)
XLA Modules:
  0.0 196.0 jit_solution(4168767256824196708)
XLA Ops:
  6.5 1.0 dynamic-slice_bitcast_fusion.1
  7.6 3.6 %collective-permute-start.1 = (bf16[2,512,128]{2,1,0:T(8,128)(2,1)S(1)}, bf16[2,512,128]{2,1,0:T(8,128)(2,1)S(1)}, u32[]{:S(2)}, u32[]{:S(2)}) collective-permute-start(bf16[2,512,128]{2,1,0:T(8,128)(2,1)S(1)} %get-tuple-element.6), channel_id=1, source_target_pairs={{0,48},{8,200},{16,0},{24,216},{32,16},{40,232},{48,32},{56,248},{... | collective-permute-start | bytes 786440 | tf_op jit(solution)/shard_map/ppermute | solution.py:35
  11.2 3.3 %collective-permute-done.1 = bf16[2,512,128]{2,1,0:T(8,128)(2,1)S(1)} collective-permute-done((bf16[2,512,128]{2,1,0:T(8,128)(2,1)S(1)}, bf16[2,512,128]{2,1,0:T(8,128)(2,1)S(1)}, u32[]{:S(2)}, u32[]{:S(2)}) %collective-permute-start.1) | collective-permute-done | bytes 262176 | tf_op jit(solution)/shard_map/ppermute | solution.py:35
  14.5 3.2 %collective-permute-start.3 = (bf16[512,128]{1,0:T(8,128)(2,1)S(1)}, bf16[512,128]{1,0:T(8,128)(2,1)S(1)}, u32[]{:S(2)}, u32[]{:S(2)}) collective-permute-start(bf16[512,128]{1,0:T(8,128)(2,1)S(1)} %slice_bitcast_fusion.2), channel_id=1, source_target_pairs={{0,48},{8,200},{16,0},{24,216},{32,16},{40,232},{48,32},{56,248},{... | collective-permute-start | bytes 393224 | tf_op jit(solution)/shard_map/ppermute | solution.py:35
  17.7 0.2 collective-permute-done
  18.0 0.1 collective-permute-start.2
  18.1 0.8 constant_dynamic-slice_fusion
  18.8 0.9 collective-permute-done.3
  19.7 3.4 %collective-permute-done.2 = bf16[512,128]{1,0:T(8,128)(2,1)S(1)} collective-permute-done((bf16[512,128]{1,0:T(8,128)(2,1)S(1)}, bf16[512,128]{1,0:T(8,128)(2,1)S(1)}, u32[]{:S(2)}, u32[]{:S(2)}) %collective-permute-start.2) | collective-permute-done | bytes 131104 | tf_op jit(solution)/shard_map/ppermute | solution.py:35
  23.1 0.1 pad_maximum_fusion
  23.2 1.1 collective-permute-start.4
  24.3 0.1 constant_dynamic-slice_fusion.2
  24.4 1.7 collective-permute-start.5
  26.1 0.8 constant_dynamic-slice_fusion.1
  26.9 0.1 copy.42.vert_ref
  26.9 0.1 copy.31
  27.0 0.1 iota_compare_fusion
  27.1 0.1 subtract_multiply_fusion
  27.2 4.3 %collective-permute-start.8 = (bf16[4,2,512,128]{3,2,0,1:T(8,128)(2,1)S(1)}, bf16[4,2,512,128]{3,2,0,1:T(8,128)(2,1)}, u32[]{:S(2)}, u32[]{:S(2)}) collective-permute-start(bf16[4,2,512,128]{3,2,0,1:T(8,128)(2,1)S(1)} %pad_maximum_fusion), channel_id=1, source_target_pairs={{0,8},{8,0},{16,24},{24,16},{32,40},{40,32},{48,56},{56,48},{64,72... | collective-permute-start | bytes 3145736 | tf_op jit(solution)/shard_map/ppermute | solution.py:35
  31.5 7.0 %collective-permute-done.4 = bf16[4,2,512,128]{3,2,0,1:T(8,128)(2,1)S(1)} collective-permute-done((bf16[4,2,512,128]{3,2,0,1:T(8,128)(2,1)S(1)}, bf16[4,2,512,128]{3,2,0,1:T(8,128)(2,1)S(1)}, u32[]{:S(2)}, u32[]{:S(2)}) %collective-permute-start.4) | collective-permute-done | bytes 1048608 | tf_op jit(solution)/shard_map/ppermute | solution.py:35
  38.5 1.0 copy-done.2
  39.5 0.1 collective-permute-start.6
  39.6 1.9 slice_bitcast_fusion
  41.5 2.7 %collective-permute-start.7 = (bf16[4,512,128]{2,1,0:T(8,128)(2,1)}, bf16[4,512,128]{2,1,0:T(8,128)(2,1)S(1)}, u32[]{:S(2)}, u32[]{:S(2)}) collective-permute-start(bf16[4,512,128]{2,1,0:T(8,128)(2,1)} %slice_bitcast_fusion), channel_id=1, source_target_pairs={{0,192},{8,56},{16,208},{24,8},{32,224},{40,24},{48,240},{56,40},{... | collective-permute-start | bytes 1572872 | tf_op jit(solution)/shard_map/ppermute | solution.py:35
  44.1 5.1 %collective-permute-start.9 = (bf16[4,2,512,128]{3,2,0,1:T(8,128)(2,1)}, bf16[4,2,512,128]{3,2,0,1:T(8,128)(2,1)}, u32[]{:S(2)}, u32[]{:S(2)}) collective-permute-start(bf16[4,2,512,128]{3,2,0,1:T(8,128)(2,1)} %copy-done.2), channel_id=1, source_target_pairs={{0,8},{8,0},{16,24},{24,16},{32,40},{40,32},{48,56},{56,48},{64,72... | collective-permute-start | bytes 3145736 | tf_op jit(solution)/shard_map/ppermute | solution.py:35
  49.3 0.7 and_reduce_fusion
  50.0 0.1 sub.105
  50.1 0.1 broadcast_in_dim.24
  50.2 0.1 broadcast_in_dim.50
  50.3 0.1 add.183
  50.4 0.1 add.185
  50.5 0.1 not_and_fusion
  50.6 0.1 broadcast_in_dim.27
  50.7 0.1 broadcast_in_dim.51
  50.8 0.1 add.188
  50.9 0.1 add.189
  51.1 0.1 fusion.diag_ref
  51.1 3.4 %collective-permute-start.11 = (bf16[4,512,128]{2,1,0:T(8,128)(2,1)S(1)}, bf16[4,512,128]{2,1,0:T(8,128)(2,1)S(1)}, u32[]{:S(2)}, u32[]{:S(2)}) collective-permute-start(bf16[4,512,128]{2,1,0:T(8,128)(2,1)S(1)} %collective-permute-done.6.fk0), channel_id=1, source_target_pairs={{0,8},{8,0},{16,24},{24,16},{32,40},{40,32},{48,56},{56,48},{64,72... | collective-permute-start | bytes 1572872 | tf_op jit(solution)/shard_map/ppermute | solution.py:35
  54.5 1.7 collective-permute-start.12
  56.3 0.1 add_select_fusion.kpd_ref
  56.5 1.3 copy.37.u0
  57.8 1.3 copy.38.d0
  59.2 1.4 copy.39.l1
  60.6 1.4 copy.40.u1
  62.0 1.3 copy.41.d1
  63.4 23.6 %attend.1 = bf16[4,512,128]{2,1,0:T(8,128)(2,1)S(1)} custom-call(s32[32]{0:T(128)S(1)} %fusion.4.slots_ref, s32[4,8]{1,0:T(4,128)S(1)} %copy.42.vert_ref, s32[32,8]{1,0:T(8,128)S(1)} %fusion.diag_ref, bf16[4,512,128]{2,1,0:T(8,128)(2,1)S(1)} %copy-done.1, s32[4,1,512]{2,1,0:T(1,128)S(1)} %add_select_fusion.1.kpv_ref, ...), custom_call_target="tpu_custom_call" | custom-call | tf_op jit(solution)/shard_map/attend/pallas_call | solution.py:152
  87.0 6.6 %bitcast_convert_fusion = bf16[512,8192]{1,0:T(8,128)(2,1)} fusion(bf16[4,512,128]{2,1,0:T(8,128)(2,1)S(1)} %attend.1, bf16[4,128,8192]{2,1,0:T(8,128)(2,1)S(1)} %bitcast.53), kind=kOutput, calls=%fused_computation | convolution fusion | flops 4299161600 | bytes 17301504 | tf_op jit(solution)/shard_map/dot_general | solution.py:187
  93.6 95.5 %reduce-scatter.2.cloned.1.call-done = bf16[64,8192]{1,0:T(8,128)(2,1)} async-done(((bf16[512,8192]{1,0:T(8,128)(2,1)}), bf16[64,8192]{1,0:T(8,128)(2,1)}) %reduce-scatter.2.cloned.1.call-update) | async-done | bytes 1048592 | tf_op jit(solution)/shard_map/reduce_scatter | solution.py:190
  (35 shorter events, 0.4 us)
Async XLA Ops:
  6.5 17.8 %copy-start = (s32[32,8]{0,1:T(8,128)S(1)}, s32[32,8]{0,1:T(8,128)}, u32[]{:S(2)}) copy-start(s32[32,8]{0,1:T(8,128)} %param.9) | copy-start | bytes 3076
  6.5 182.6 %reduce-scatter.2.cloned.1.call-start = ((), (), s32[]{:S(2)}) async-start(), calls=%async_computation.1 | async-start | bytes 9437184 | tf_op jit(solution)/shard_map/reduce_scatter | solution.py:190
  7.6 7.0 %collective-permute-start.1 = (bf16[2,512,128]{2,1,0:T(8,128)(2,1)S(1)}, bf16[2,512,128]{2,1,0:T(8,128)(2,1)S(1)}, u32[]{:S(2)}, u32[]{:S(2)}) collective-permute-start(bf16[2,512,128]{2,1,0:T(8,128)(2,1)S(1)} %get-tuple-element.6), channel_id=1, source_target_pairs={{0,48},{8,200},{16,0},{24,216},{32,16},{40,232},{48,32},{56,248},{... | collective-permute-start | bytes 786440 | tf_op jit(solution)/shard_map/ppermute | solution.py:35
  11.2 6.7 %collective-permute-start = (bf16[2,512,128]{2,1,0:T(8,128)(2,1)S(1)}, bf16[2,512,128]{2,1,0:T(8,128)(2,1)S(1)}, u32[]{:S(2)}, u32[]{:S(2)}) collective-permute-start(bf16[2,512,128]{2,1,0:T(8,128)(2,1)S(1)} %get-tuple-element.6), channel_id=1, source_target_pairs={{0,16},{8,72},{16,32},{24,88},{32,48},{40,104},{48,0},{56,120},{64... | collective-permute-start | bytes 786440 | tf_op jit(solution)/shard_map/ppermute | solution.py:35
  14.5 5.1 %collective-permute-start.3 = (bf16[512,128]{1,0:T(8,128)(2,1)S(1)}, bf16[512,128]{1,0:T(8,128)(2,1)S(1)}, u32[]{:S(2)}, u32[]{:S(2)}) collective-permute-start(bf16[512,128]{1,0:T(8,128)(2,1)S(1)} %slice_bitcast_fusion.2), channel_id=1, source_target_pairs={{0,48},{8,200},{16,0},{24,216},{32,16},{40,232},{48,32},{56,248},{... | collective-permute-start | bytes 393224 | tf_op jit(solution)/shard_map/ppermute | solution.py:35
  18.0 5.1 %collective-permute-start.2 = (bf16[512,128]{1,0:T(8,128)(2,1)S(1)}, bf16[512,128]{1,0:T(8,128)(2,1)S(1)}, u32[]{:S(2)}, u32[]{:S(2)}) collective-permute-start(bf16[512,128]{1,0:T(8,128)(2,1)S(1)} %slice_bitcast_fusion.3), channel_id=1, source_target_pairs={{0,16},{8,72},{16,32},{24,88},{32,48},{40,104},{48,0},{56,120},{64... | collective-permute-start | bytes 393224 | tf_op jit(solution)/shard_map/ppermute | solution.py:35
  23.1 40.3 %copy-start.1 = (bf16[4,512,128]{2,1,0:T(8,128)(2,1)S(1)}, bf16[4,512,128]{2,1,0:T(8,128)(2,1)}, u32[]{:S(2)}) copy-start(bf16[4,512,128]{2,1,0:T(8,128)(2,1)} %q_ref.1) | copy-start | bytes 1572868
  23.2 15.2 %collective-permute-start.4 = (bf16[4,2,512,128]{3,2,0,1:T(8,128)(2,1)S(1)}, bf16[4,2,512,128]{3,2,0,1:T(8,128)(2,1)S(1)}, u32[]{:S(2)}, u32[]{:S(2)}) collective-permute-start(bf16[4,2,512,128]{3,2,0,1:T(8,128)(2,1)S(1)} %pad_maximum_fusion), channel_id=1, source_target_pairs={{0,64},{8,24},{16,80},{24,40},{32,96},{40,56},{48,112},{56,8},{64,... | collective-permute-start | bytes 3145736 | tf_op jit(solution)/shard_map/ppermute | solution.py:35
  24.4 15.2 %collective-permute-start.5 = (bf16[4,2,512,128]{3,2,0,1:T(8,128)(2,1)S(1)}, bf16[4,2,512,128]{3,2,0,1:T(8,128)(2,1)}, u32[]{:S(2)}, u32[]{:S(2)}) collective-permute-start(bf16[4,2,512,128]{3,2,0,1:T(8,128)(2,1)S(1)} %pad_maximum_fusion), channel_id=1, source_target_pairs={{0,192},{8,56},{16,208},{24,8},{32,224},{40,24},{48,240},{56,40},{... | collective-permute-start | bytes 3145736 | tf_op jit(solution)/shard_map/ppermute | solution.py:35
  27.2 32.0 %collective-permute-start.8 = (bf16[4,2,512,128]{3,2,0,1:T(8,128)(2,1)S(1)}, bf16[4,2,512,128]{3,2,0,1:T(8,128)(2,1)}, u32[]{:S(2)}, u32[]{:S(2)}) collective-permute-start(bf16[4,2,512,128]{3,2,0,1:T(8,128)(2,1)S(1)} %pad_maximum_fusion), channel_id=1, source_target_pairs={{0,8},{8,0},{16,24},{24,16},{32,40},{40,32},{48,56},{56,48},{64,72... | collective-permute-start | bytes 3145736 | tf_op jit(solution)/shard_map/ppermute | solution.py:35
  38.5 1.0 copy-start.2
  39.5 11.6 %collective-permute-start.6 = (bf16[4,512,128]{2,1,0:T(8,128)(2,1)S(1)}, bf16[4,512,128]{2,1,0:T(8,128)(2,1)S(1)}, u32[]{:S(2)}, u32[]{:S(2)}) collective-permute-start(bf16[4,512,128]{2,1,0:T(8,128)(2,1)S(1)} %slice_bitcast_fusion.1), channel_id=1, source_target_pairs={{0,64},{8,24},{16,80},{24,40},{32,96},{40,56},{48,112},{56,8},{64,... | collective-permute-start | bytes 1572872 | tf_op jit(solution)/shard_map/ppermute | solution.py:35
  41.5 13.1 %collective-permute-start.7 = (bf16[4,512,128]{2,1,0:T(8,128)(2,1)}, bf16[4,512,128]{2,1,0:T(8,128)(2,1)S(1)}, u32[]{:S(2)}, u32[]{:S(2)}) collective-permute-start(bf16[4,512,128]{2,1,0:T(8,128)(2,1)} %slice_bitcast_fusion), channel_id=1, source_target_pairs={{0,192},{8,56},{16,208},{24,8},{32,224},{40,24},{48,240},{56,40},{... | collective-permute-start | bytes 1572872 | tf_op jit(solution)/shard_map/ppermute | solution.py:35
  44.1 16.5 %collective-permute-start.9 = (bf16[4,2,512,128]{3,2,0,1:T(8,128)(2,1)}, bf16[4,2,512,128]{3,2,0,1:T(8,128)(2,1)}, u32[]{:S(2)}, u32[]{:S(2)}) collective-permute-start(bf16[4,2,512,128]{3,2,0,1:T(8,128)(2,1)} %copy-done.2), channel_id=1, source_target_pairs={{0,8},{8,0},{16,24},{24,16},{32,40},{40,32},{48,56},{56,48},{64,72... | collective-permute-start | bytes 3145736 | tf_op jit(solution)/shard_map/ppermute | solution.py:35
  49.3 12.8 %collective-permute-start.10 = (bf16[4,2,512,128]{3,2,0,1:T(8,128)(2,1)}, bf16[4,2,512,128]{3,2,0,1:T(8,128)(2,1)}, u32[]{:S(2)}, u32[]{:S(2)}) collective-permute-start(bf16[4,2,512,128]{3,2,0,1:T(8,128)(2,1)} %collective-permute-done.5), channel_id=1, source_target_pairs={{0,8},{8,0},{16,24},{24,16},{32,40},{40,32},{48,56},{56,48},{64,72... | collective-permute-start | bytes 3145736 | tf_op jit(solution)/shard_map/ppermute | solution.py:35
  51.1 12.2 %collective-permute-start.11 = (bf16[4,512,128]{2,1,0:T(8,128)(2,1)S(1)}, bf16[4,512,128]{2,1,0:T(8,128)(2,1)S(1)}, u32[]{:S(2)}, u32[]{:S(2)}) collective-permute-start(bf16[4,512,128]{2,1,0:T(8,128)(2,1)S(1)} %collective-permute-done.6.fk0), channel_id=1, source_target_pairs={{0,8},{8,0},{16,24},{24,16},{32,40},{40,32},{48,56},{56,48},{64,72... | collective-permute-start | bytes 1572872 | tf_op jit(solution)/shard_map/ppermute | solution.py:35
  54.5 8.8 %collective-permute-start.12 = (bf16[4,512,128]{2,1,0:T(8,128)(2,1)S(1)}, bf16[4,512,128]{2,1,0:T(8,128)(2,1)S(1)}, u32[]{:S(2)}, u32[]{:S(2)}) collective-permute-start(bf16[4,512,128]{2,1,0:T(8,128)(2,1)S(1)} %collective-permute-done.7.fv0), channel_id=1, source_target_pairs={{0,8},{8,0},{16,24},{24,16},{32,40},{40,32},{48,56},{56,48},{64,72... | collective-permute-start | bytes 1572872 | tf_op jit(solution)/shard_map/ppermute | solution.py:35
  59.1 27.8 %slice-start = ((s8[8388608]{0:T(1024)(128)(4,1)}), s8[4194304]{0:T(1024)(128)(4,1)S(1)}, s32[]{:S(2)}) async-start(s8[8388608]{0:T(1024)(128)(4,1)} %bitcast.51), calls=%async_computation.2 | async-start | bytes 8388608
  63.3 23.6 %slice-start.1 = ((s8[8388608]{0:T(1024)(128)(4,1)}), s8[4194304]{0:T(1024)(128)(4,1)S(1)}, s32[]{:S(2)}) async-start(s8[8388608]{0:T(1024)(128)(4,1)} %bitcast.51), calls=%async_computation.3 | async-start | bytes 8388608
Sparse Core Ops, SparseCore 0:
  93.8 95.3 reduce-scatter.1

commit v2 on v1

--- a/solution.py
+++ b/solution.py
@@ -28,6 +28,13 @@
 A_DOWN = seq_perm(lambda y, x, c: (y, x - 1, c) if c == 0 else (y - 1, x, c))
 B_UP = seq_perm(lambda y, x, c: (y + 1, x, c) if c == 0 else (y, x + 1, c))
 B_DOWN = seq_perm(lambda y, x, c: (y - 1, x, c) if c == 0 else (y, x - 1, c))
+def pair(v, c):
+    return (v ^ 1) if c == 0 else (v + 1 if v % 2 else v - 1)
+
+
+PAIR_X = seq_perm(lambda y, x, c: (y, pair(x, c), c))
+PAIR_Y = seq_perm(lambda y, x, c: (pair(y, c), x, c))
+PAIR_XY = seq_perm(lambda y, x, c: (pair(y, c), pair(x, c), c))
 SWAP = seq_perm(lambda y, x, c: (y, x, 1 - c))
 
 
@@ -38,9 +45,9 @@
 def gather_keyval(own):
     up, down = send(own, A_UP), send(own, A_DOWN)
     far = jnp.stack([send(up[0], A_UP), send(down[1], A_DOWN)])
-    line = jnp.stack([own, up, down, far])
+    line = jnp.stack([own, up, down, far], axis=1)
     up2, down2 = send(line, B_UP), send(line, B_DOWN)
-    far_k, far_v = send(up2[:, 0], B_UP), send(down2[:, 1], B_DOWN)
+    far_k, far_v = send(up2[0], B_UP), send(down2[1], B_DOWN)
     mine = [line, up2, down2, far_k, far_v]
     return mine + [send(a, SWAP) for a in mine]
 
@@ -73,7 +80,7 @@
         for which, buf in enumerate((kbuf, vbuf)):
             for j, src in enumerate((line, up, down, (fk, fv)[which])):
                 for i in range(4):
-                    piece = src.at[i] if j == 3 else src.at[i, which]
+                    piece = src.at[i] if j == 3 else src.at[which, i]
                     slot = side * 16 + j * 4 + i
                     copies[which].append(
                         pltpu.make_async_copy(piece, buf.at[slot], sems.at[which, slot])
@@ -120,7 +127,10 @@
             )
         v_v = jnp.concatenate([tile(vbuf, v) for v in verts], axis=0)
         o_v = jnp.dot(pv_ref[...], v_v, preferred_element_type=jnp.float32)
-        o_ref[h] = ((o_v + od_ref[...]) / tot_ref[...]).astype(jnp.bfloat16)
+        o = ((o_v + od_ref[...]) / tot_ref[...]).astype(jnp.bfloat16)
+        lanes = pl.ds(pl.multiple_of(h * width, width), width)
+        for b in range(blocks):
+            o_ref[b, :, lanes] = o[b * BLK : (b + 1) * BLK]
         return carry
 
     lax.fori_loop(0, heads, one_head, 0)
@@ -151,7 +161,7 @@
     f32 = jnp.float32
     return pl.pallas_call(
         attend_kernel,
-        out_shape=jax.ShapeDtypeStruct((heads, rows, width), jnp.bfloat16),
+        out_shape=jax.ShapeDtypeStruct((blocks, BLK, heads * width), jnp.bfloat16),
         in_specs=[smem] * 3 + [vmem] * 3 + [hbm] * len(pieces),
         out_specs=vmem,
         scratch_shapes=[
@@ -168,13 +178,96 @@
     )(slots, vertical, diag, query, kpv, kpd, *pieces)
 
 
+def ring(n, step):
+    return [(i, (i + step) % n) for i in range(n)]
+
+
+def gather_weight(own):
+    n = lax.axis_size("tp")
+    half = own.shape[0] // 2
+
+    def up(a):
+        return lax.ppermute(a, "tp", ring(n, 1))
+
+    def down(a):
+        return lax.ppermute(a, "tp", ring(n, -1))
+
+    u1, d1 = up(own), down(own)
+    u2, d2 = up(u1), down(d1)
+    u3, d3 = up(u2), down(d2)
+    u4, d4 = up(u3[:half]), down(d3[half:])
+    mine = [own, u1, d1, u2, d2, u3, d3, u4, d4]
+    return mine + [send(a, SWAP) for a in mine]
+
+
+def project_kernel(place_ref, *refs):
+    rows, weights = refs[:4], refs[4:22]
+    o_ref, wbuf, acc, sems = refs[22:]
+    n, group, depth = rows[0].shape
+    cols = weights[0].shape[1]
+    tp, core = place_ref[0], place_ref[1]
+    half = depth // 2
+    copies = []
+    for side in range(2):
+        for i in range(9):
+            dst = wbuf.at[side, i] if i < 7 else wbuf.at[side, 7, pl.ds((i - 7) * half, half)]
+            copies.append(pltpu.make_async_copy(weights[side * 9 + i], dst, sems.at[side * 9 + i]))
+    for c in copies:
+        c.start()
+    steps = (0, -1, 1, -2, 2, -3, 3, 4)
+    for i, step in enumerate(steps):
+        k = lax.rem(tp + step + n, n)
+        a = jnp.concatenate([r[k] for r in rows], axis=0)
+        for side in range(2):
+            copies[side * 9 + i].wait()
+            if i == 7:
+                copies[side * 9 + 8].wait()
+            part = jnp.dot(a, wbuf[side, i], preferred_element_type=jnp.float32)
+            if i == 0:
+                acc[side] = part
+            else:
+                acc[side] += part
+    for side in range(2):
+        col = pl.ds(pl.multiple_of((core if side == 0 else 1 - core) * cols, cols), cols)
+        for r in range(4):
+            o_ref[r, :, col] = acc[side, pl.ds(r * group, group), :].astype(jnp.bfloat16)
+
+
+def project(rows, weights, place):
+    n, group, depth = rows[0].shape
+    cols = weights[0].shape[1]
+    vmem = pl.BlockSpec(memory_space=pltpu.VMEM)
+    hbm = pl.BlockSpec(memory_space=pl.ANY)
+    return pl.pallas_call(
+        project_kernel,
+        out_shape=jax.ShapeDtypeStruct((4, group, 2 * cols), jnp.bfloat16),
+        in_specs=[pl.BlockSpec(memory_space=pltpu.SMEM)] + [vmem] * 4 + [hbm] * len(weights),
+        out_specs=vmem,
+        scratch_shapes=[
+            pltpu.VMEM((2, n, depth, cols), jnp.bfloat16),
+            pltpu.VMEM((2, 4 * group, cols), jnp.float32),
+            pltpu.SemaphoreType.DMA((18,)),
+        ],
+        compiler_params=pltpu.CompilerParams(vmem_limit_bytes=40 * 2**20),
+        name="project",
+    )(place, *rows, *weights)
+
+
 def per_device(query, keyval, vert_blocks, slash_offsets, counts, out_weight):
     heads, rows, width = query.shape
     seq_index = lax.axis_index("seq")
     tp_index = lax.axis_index("tp")
+    core = seq_index % NC
+    x_odd = (seq_index // NC) % 2
+    y_odd = (seq_index // (NC * NX)) % 2
+    block = y_odd * 2 + x_odd
+    cols = out_weight.shape[1] // 8
     kv_head = tp_index // (lax.axis_size("tp") // keyval.shape[1])
     own = lax.dynamic_index_in_dim(keyval, kv_head, 1, keepdims=False)
     pieces = gather_keyval(own)
+    weights = gather_weight(
+        lax.dynamic_slice_in_dim(out_weight, (block * 2 + core) * cols, cols, 1)
+    )
 
     def mine(a):
         return lax.dynamic_slice_in_dim(a, tp_index * heads, heads, 0)
@@ -183,11 +276,15 @@
         query, pieces, shard_slots(seq_index), mine(vert_blocks), mine(slash_offsets),
         mine(counts), seq_index,
     )
-    weight_heads = out_weight.reshape(heads, width, -1)
-    partial = lax.dot_general(
-        attended, weight_heads, (((0, 2), (0, 1)), ((), ())), preferred_element_type=jnp.float32
-    ).astype(jnp.bfloat16)
-    return lax.psum_scatter(partial, "tp", scatter_dimension=0, tiled=True)
+    tokens = lax.all_to_all(attended, "tp", split_axis=0, concat_axis=0, tiled=True)
+    moves = (PAIR_X, PAIR_Y, PAIR_XY)
+    out = project(
+        [tokens] + [send(tokens, m) for m in moves], weights, jnp.stack([tp_index, core])
+    )
+    back = [out[0]] + [send(out[i + 1], m) for i, m in enumerate(moves)]
+    odd_x, odd_y = x_odd == 1, y_odd == 1
+    left = [jnp.where(odd_x, back[i ^ 1], back[i]) for i in range(4)]
+    return jnp.concatenate([jnp.where(odd_y, left[i ^ 2], left[i]) for i in range(4)], axis=1)
 
 
 def solution(mesh):

time: 196 us -> 190 us (0.969)
  waiting for transfers between devices: 110 us -> 79.7 us
  starting transfers between devices: 27 us -> 55.3 us
  between operations: 13.7 us -> 0.3 us
  local copies, waits for them, and re-layouts: 13.4 us -> 22.3 us
  matrix products: 6.64 us -> 0 us
  Pallas kernels: 23.6 us -> 26.8 us
  other arithmetic: 1.32 us -> 4.42 us
    reduce_scatter x1 -> x0, waiting for transfers between devices: 95.5 us -> none  [per_device(): return lax.psum_scatter(partial, 'tp', scatter_dimension=0, tiled=True)]
    ppermute x0 -> x8, waiting for transfers between devices: none -> 47.4 us  [the longest x4 47.4 us: up(): return lax.ppermute(a, 'tp', ring(n, 1))]
    ppermute x0 -> x8, starting transfers between devices: none -> 14.1 us  [the longest x4 10.9 us: down(): return lax.ppermute(a, 'tp', ring(n, -1))]
    unnamed x11 -> x35, local copies, waits for them, and re-layouts: 1.08 us -> 12.9 us
    all_to_all x0 -> x1, waiting for transfers between devices: none -> 11.5 us  [per_device(): lax.all_to_all(attended, 'tp', split_axis=0, concat_axis=0, tiled=True)]
    ppermute x13 -> x28, starting transfers between devices: 27 us -> 35.9 us  [send(): return lax.ppermute(a, 'seq', pairs)]
    ppermute x5 -> x0, local copies, waits for them, and re-layouts: 6.72 us -> none  [send(): return lax.ppermute(a, 'seq', pairs)]
    dot_general x1 -> x0, matrix products: 6.64 us -> none  [per_device(): lax.dot_general(attended, weight_heads, (((0, 2), (0, 1)), ((), ())), pre...]
  transfers between devices with their start and end apart: 14 -> 37, of which waited for: 6 -> 11; matrix products, arithmetic and copies ran while one was open for 6% -> 6% of each run, Pallas kernels for 0% -> 9%
where the time goes in v2:
time: 190 us; the launch traced here: 189 us
  waiting for transfers between devices  79.7 us (42%)
  starting transfers between devices  55.3 us (29%)
  Pallas kernels  26.8 us (14%)
  local copies, waits for them, and re-layouts  22.3 us (12%)
  other arithmetic  4.42 us (2%)
    ppermute x4, waiting for transfers between devices, up(): return lax.ppermute(a, 'tp', ring(n, 1))  47.4 us
    ppermute x28, starting transfers between devices, send(): return lax.ppermute(a, 'seq', pairs)  35.9 us
    ppermute x28, waiting for transfers between devices, send(): return lax.ppermute(a, 'seq', pairs)  20.8 us
    pallas_call x1, Pallas kernels, attend(): pl.pallas_call(attend_kernel, out_shape=jax.ShapeDtypeStruct((blocks, BLK...  17.5 us
    unnamed x35, local copies, waits for them, and re-layouts  12.9 us
    all_to_all x1, waiting for transfers between devices, per_device(): lax.all_to_all(attended, 'tp', split_axis=0, concat_axis=0, tiled=True)  11.5 us
    ppermute x4, starting transfers between devices, down(): return lax.ppermute(a, 'tp', ring(n, -1))  10.9 us
    pallas_call x1, Pallas kernels, project(): pl.pallas_call(project_kernel, out_shape=jax.ShapeDtypeStruct((4, group,...  9.3 us
  transfers between devices with their start and end apart: 37, of which 11 were waited for; matrix products, arithmetic and copies ran while one was open for 6% of the time, Pallas kernels for 9%

profile of v2, /device:TPU:1, one launch (start us, length us, event | category | flops | bytes accessed | tf_op | source)
XLA Modules:
  0.0 188.8 jit_solution(6908604363145832177)
XLA Ops:
  0.0 1.2 copy-done
  1.2 2.2 %collective-permute-start = (bf16[2,512,128]{2,1,0:T(8,128)(2,1)S(1)}, bf16[2,512,128]{2,1,0:T(8,128)(2,1)S(1)}, u32[]{:S(2)}, u32[]{:S(2)}) collective-permute-start(bf16[2,512,128]{2,1,0:T(8,128)(2,1)S(1)} %fusion.11), channel_id=1, source_target_pairs={{0,16},{8,72},{16,32},{24,88},{32,48},{40,104},{48,0},{56,120},{64... | collective-permute-start | bytes 786440 | tf_op jit(solution)/shard_map/ppermute | solution.py:42
  3.5 1.5 collective-permute-start.1
  5.0 4.0 %collective-permute-done = bf16[2,512,128]{2,1,0:T(8,128)(2,1)S(1)} collective-permute-done((bf16[2,512,128]{2,1,0:T(8,128)(2,1)S(1)}, bf16[2,512,128]{2,1,0:T(8,128)(2,1)S(1)}, u32[]{:S(2)}, u32[]{:S(2)}) %collective-permute-start) | collective-permute-done | bytes 262176 | tf_op jit(solution)/shard_map/ppermute | solution.py:42
  9.1 2.7 %collective-permute-start.3 = (bf16[512,128]{1,0:T(8,128)(2,1)S(1)}, bf16[512,128]{1,0:T(8,128)(2,1)S(1)}, u32[]{:S(2)}, u32[]{:S(2)}) collective-permute-start(bf16[512,128]{1,0:T(8,128)(2,1)S(1)} %slice_bitcast_fusion.6), channel_id=1, source_target_pairs={{0,48},{8,200},{16,0},{24,216},{32,16},{40,232},{48,32},{56,248},{... | collective-permute-start | bytes 393224 | tf_op jit(solution)/shard_map/ppermute | solution.py:42
  11.8 1.3 constant_dynamic-slice_fusion.refs_4_
  13.1 1.7 collective-permute-start.16
  14.9 4.0 %collective-permute-start.17 = (bf16[512,1024]{1,0:T(8,128)(2,1)S(1)}, bf16[512,1024]{1,0:T(8,128)(2,1)}, u32[]{:S(2)}, u32[]{:S(2)}) collective-permute-start(bf16[512,1024]{1,0:T(8,128)(2,1)S(1)} %constant_dynamic-slice_fusion.refs_4_), channel_id=1, source_target_pairs={{0,7},{1,0},{2,1},{3,2},{4,3},{5,4},{6,5},{7,6},{8,15},{9,8},{10,9... | collective-permute-start | bytes 3145736 | tf_op jit(solution)/shard_map/ppermute | solution.py:193
  19.0 1.1 pad_maximum_fusion.l0
  21.1 1.8 collective-permute-start.5
  22.8 2.9 %collective-permute-start.24 = (bf16[512,1024]{1,0:T(8,128)(2,1)S(1)}, bf16[512,1024]{1,0:T(8,128)(2,1)}, u32[]{:S(2)}, u32[]{:S(2)}) collective-permute-start(bf16[512,1024]{1,0:T(8,128)(2,1)S(1)} %constant_dynamic-slice_fusion.refs_4_), channel_id=1, source_target_pairs={{0,8},{8,0},{16,24},{24,16},{32,40},{40,32},{48,56},{56,48},{64,72... | collective-permute-start | bytes 3145736 | tf_op jit(solution)/shard_map/ppermute | solution.py:42
  25.9 14.4 %collective-permute-done.16.refs_5_ = bf16[512,1024]{1,0:T(8,128)(2,1)} collective-permute-done((bf16[512,1024]{1,0:T(8,128)(2,1)S(1)}, bf16[512,1024]{1,0:T(8,128)(2,1)}, u32[]{:S(2)}, u32[]{:S(2)}) %collective-permute-start.16) | collective-permute-done | bytes 1048608 | tf_op jit(solution)/shard_map/ppermute | solution.py:190
  40.3 2.7 %collective-permute-start.8 = (bf16[2,4,512,128]{3,2,1,0:T(8,128)(2,1)S(1)}, bf16[2,4,512,128]{3,2,1,0:T(8,128)(2,1)S(1)}, u32[]{:S(2)}, u32[]{:S(2)}) collective-permute-start(bf16[2,4,512,128]{3,2,1,0:T(8,128)(2,1)S(1)} %pad_maximum_fusion.l0), channel_id=1, source_target_pairs={{0,8},{8,0},{16,24},{24,16},{32,40},{40,32},{48,56},{56,48},{64,72... | collective-permute-start | bytes 3145736 | tf_op jit(solution)/shard_map/ppermute | solution.py:42
  43.1 2.7 %collective-permute-start.19 = (bf16[512,1024]{1,0:T(8,128)(2,1)}, bf16[512,1024]{1,0:T(8,128)(2,1)}, u32[]{:S(2)}, u32[]{:S(2)}) collective-permute-start(bf16[512,1024]{1,0:T(8,128)(2,1)} %collective-permute-done.17.refs_6_), channel_id=1, source_target_pairs={{0,7},{1,0},{2,1},{3,2},{4,3},{5,4},{6,5},{7,6},{8,15},{9,8},{10,9... | collective-permute-start | bytes 3145736 | tf_op jit(solution)/shard_map/ppermute | solution.py:193
  45.8 1.1 slice_bitcast_fusion.1
  47.9 1.9 slice_bitcast_fusion
  49.8 1.8 collective-permute-start.7
  52.6 1.1 collective-permute-start.10
  53.7 2.9 %collective-permute-done.6.fk0 = bf16[4,512,128]{2,1,0:T(8,128)(2,1)} collective-permute-done((bf16[4,512,128]{2,1,0:T(8,128)(2,1)S(1)}, bf16[4,512,128]{2,1,0:T(8,128)(2,1)}, u32[]{:S(2)}, u32[]{:S(2)}) %collective-permute-start.6) | collective-permute-done | bytes 524320 | tf_op jit(solution)/shard_map/ppermute | solution.py:42
  56.6 1.4 collective-permute-start.9
  58.0 11.3 %collective-permute-done.18.refs_7_ = bf16[512,1024]{1,0:T(8,128)(2,1)} collective-permute-done((bf16[512,1024]{1,0:T(8,128)(2,1)}, bf16[512,1024]{1,0:T(8,128)(2,1)}, u32[]{:S(2)}, u32[]{:S(2)}) %collective-permute-start.18) | collective-permute-done | bytes 1048608 | tf_op jit(solution)/shard_map/ppermute | solution.py:190
  73.3 3.0 %collective-permute-start.21 = (bf16[512,1024]{1,0:T(8,128)(2,1)}, bf16[512,1024]{1,0:T(8,128)(2,1)}, u32[]{:S(2)}, u32[]{:S(2)}) collective-permute-start(bf16[512,1024]{1,0:T(8,128)(2,1)} %collective-permute-done.19.refs_8_), channel_id=1, source_target_pairs={{0,7},{1,0},{2,1},{3,2},{4,3},{5,4},{6,5},{7,6},{8,15},{9,8},{10,9... | collective-permute-start | bytes 3145736 | tf_op jit(solution)/shard_map/ppermute | solution.py:193
  78.2 16.5 %collective-permute-done.20.refs_9_ = bf16[512,1024]{1,0:T(8,128)(2,1)} collective-permute-done((bf16[512,1024]{1,0:T(8,128)(2,1)}, bf16[512,1024]{1,0:T(8,128)(2,1)}, u32[]{:S(2)}, u32[]{:S(2)}) %collective-permute-start.20) | collective-permute-done | bytes 1048608 | tf_op jit(solution)/shard_map/ppermute | solution.py:190
  94.8 1.7 collective-permute-start.28
  96.6 1.2 copy-done.5
  97.8 1.0 copy-done.6
  98.8 1.0 copy-done.8
  99.9 17.5 %attend.1 = bf16[8,64,512]{2,1,0:T(8,128)(2,1)S(1)} custom-call(s32[32]{0:T(128)S(1)} %fusion.4.slots_ref, s32[4,8]{1,0:T(4,128)S(1)} %copy.24.vert_ref, s32[32,8]{1,0:T(8,128)S(1)} %fusion.diag_ref, bf16[4,512,128]{2,1,0:T(8,128)(2,1)S(1)} %copy-done.6, s32[4,1,512]{2,1,0:T(1,128)S(1)} %add_select_fusion.1.kpv_ref, ...), custom_call_target="tpu_custom_call" | custom-call | tf_op jit(solution)/shard_map/attend/pallas_call | solution.py:162
  118.1 5.3 %all-to-all-start = ((bf16[8,64,512]{2,1,0:T(8,128)(2,1)}), bf16[8,64,512]{2,1,0:T(8,128)(2,1)S(1)}, u32[]{:S(2)}, u32[]{:S(2)}) async-start(bf16[8,64,512]{2,1,0:T(8,128)(2,1)} %copy-done.3), calls=%async_computation | async-start | bytes 1048576 | tf_op jit(solution)/shard_map/all_to_all | solution.py:279
  123.4 1.9 slice.65
  125.3 1.5 collective-permute-start.22
  126.8 1.9 %slice.66 = bf16[256,1024]{1,0:T(8,128)(2,1)} slice(bf16[512,1024]{1,0:T(8,128)(2,1)} %collective-permute-done.21.refs_10_), slice={[256:512], [0:1024]} | slice | bytes 1048576 | tf_op jit(solution)/shard_map/slice | solution.py:198
  128.7 1.2 collective-permute-start.23
  129.9 11.5 %all-to-all-done.refs_0_ = bf16[8,64,512]{2,1,0:T(8,128)(2,1)S(1)} async-done(((bf16[8,64,512]{2,1,0:T(8,128)(2,1)}), bf16[8,64,512]{2,1,0:T(8,128)(2,1)S(1)}, u32[]{:S(2)}, u32[]{:S(2)}) %all-to-all-start) | async-done | bytes 524320 | tf_op jit(solution)/shard_map/all_to_all | solution.py:279
  141.5 2.4 %collective-permute-start.13 = (bf16[8,64,512]{2,1,0:T(8,128)(2,1)S(1)}, bf16[8,64,512]{2,1,0:T(8,128)(2,1)S(1)}, u32[]{:S(2)}, u32[]{:S(2)}) collective-permute-start(bf16[8,64,512]{2,1,0:T(8,128)(2,1)S(1)} %all-to-all-done.refs_0_), channel_id=1, source_target_pairs={{0,16},{8,56},{16,0},{24,40},{32,48},{40,24},{48,32},{56,8},{64,80... | collective-permute-start | bytes 1572872 | tf_op jit(solution)/shard_map/ppermute | solution.py:42
  144.2 5.1 %collective-permute-done.22.refs_11_ = bf16[256,1024]{1,0:T(8,128)(2,1)S(1)} collective-permute-done((bf16[256,1024]{1,0:T(8,128)(2,1)}, bf16[256,1024]{1,0:T(8,128)(2,1)S(1)}, u32[]{:S(2)}, u32[]{:S(2)}) %collective-permute-start.22) | collective-permute-done | bytes 524320 | tf_op jit(solution)/shard_map/ppermute | solution.py:190
  149.3 1.1 collective-permute-start.30
  150.4 2.4 %collective-permute-start.15 = (bf16[8,64,512]{2,1,0:T(8,128)(2,1)S(1)}, bf16[8,64,512]{2,1,0:T(8,128)(2,1)S(1)}, u32[]{:S(2)}, u32[]{:S(2)}) collective-permute-start(bf16[8,64,512]{2,1,0:T(8,128)(2,1)S(1)} %all-to-all-done.refs_0_), channel_id=1, source_target_pairs={{0,80},{8,248},{16,64},{24,232},{32,112},{40,216},{48,96},{56,200}... | collective-permute-start | bytes 1572872 | tf_op jit(solution)/shard_map/ppermute | solution.py:42
  155.1 6.7 %collective-permute-done.15.refs_3_ = bf16[8,64,512]{2,1,0:T(8,128)(2,1)S(1)} collective-permute-done((bf16[8,64,512]{2,1,0:T(8,128)(2,1)S(1)}, bf16[8,64,512]{2,1,0:T(8,128)(2,1)S(1)}, u32[]{:S(2)}, u32[]{:S(2)}) %collective-permute-start.15) | collective-permute-done | bytes 524320 | tf_op jit(solution)/shard_map/ppermute | solution.py:42
  162.8 1.0 copy-done.12
  163.8 1.0 copy-done.2
  164.9 1.0 copy-done.10
  165.9 9.3 %project.1 = bf16[4,64,2048]{2,1,0:T(8,128)(2,1)S(1)} custom-call(s32[2]{0:T(128)S(1)} %pad_add_fusion.place_ref, bf16[8,64,512]{2,1,0:T(8,128)(2,1)S(1)} %copy-done.2, bf16[8,64,512]{2,1,0:T(8,128)(2,1)S(1)} %collective-permute-done.13.refs_1_, bf16[8,64,512]{2,1,0:T(8,128)(2,1)S(1)} %collective-permute-done.14.refs_2_, ...), custom_call_target="tpu_custom_call" | custom-call | tf_op jit(solution)/shard_map/project/pallas_call | solution.py:241
  175.3 2.5 %collective-permute-start.33 = (bf16[64,2048]{1,0:T(8,128)(2,1)S(1)}, bf16[64,2048]{1,0:T(8,128)(2,1)S(1)}, u32[]{:S(2)}, u32[]{:S(2)}) collective-permute-start(bf16[64,2048]{1,0:T(8,128)(2,1)S(1)} %get-tuple-element.11), channel_id=1, source_target_pairs={{0,80},{8,248},{16,64},{24,232},{32,112},{40,216},{48,96},{56,200}... | collective-permute-start | bytes 786440 | tf_op jit(solution)/shard_map/ppermute | solution.py:42
  177.8 2.4 %collective-permute-start.34 = (bf16[64,2048]{1,0:T(8,128)(2,1)S(1)}, bf16[64,2048]{1,0:T(8,128)(2,1)S(1)}, u32[]{:S(2)}, u32[]{:S(2)}) collective-permute-start(bf16[64,2048]{1,0:T(8,128)(2,1)S(1)} %get-tuple-element.10), channel_id=1, source_target_pairs={{0,64},{8,200},{16,80},{24,216},{32,96},{40,232},{48,112},{56,248}... | collective-permute-start | bytes 786440 | tf_op jit(solution)/shard_map/ppermute | solution.py:42
  180.4 3.6 %collective-permute-done.33 = bf16[64,2048]{1,0:T(8,128)(2,1)S(1)} collective-permute-done((bf16[64,2048]{1,0:T(8,128)(2,1)S(1)}, bf16[64,2048]{1,0:T(8,128)(2,1)S(1)}, u32[]{:S(2)}, u32[]{:S(2)}) %collective-permute-start.33) | collective-permute-done | bytes 262176 | tf_op jit(solution)/shard_map/ppermute | solution.py:42
  184.0 2.7 %collective-permute-done.34 = bf16[64,2048]{1,0:T(8,128)(2,1)S(1)} collective-permute-done((bf16[64,2048]{1,0:T(8,128)(2,1)S(1)}, bf16[64,2048]{1,0:T(8,128)(2,1)S(1)}, u32[]{:S(2)}, u32[]{:S(2)}) %collective-permute-start.34) | collective-permute-done | bytes 262176 | tf_op jit(solution)/shard_map/ppermute | solution.py:42
  187.8 1.0 pad_maximum_fusion.1
  (105 shorter events, 15.2 us)
Async XLA Ops:
  0.0 1.2 copy-start
  1.2 7.7 %collective-permute-start = (bf16[2,512,128]{2,1,0:T(8,128)(2,1)S(1)}, bf16[2,512,128]{2,1,0:T(8,128)(2,1)S(1)}, u32[]{:S(2)}, u32[]{:S(2)}) collective-permute-start(bf16[2,512,128]{2,1,0:T(8,128)(2,1)S(1)} %fusion.11), channel_id=1, source_target_pairs={{0,16},{8,72},{16,32},{24,88},{32,48},{40,104},{48,0},{56,120},{64... | collective-permute-start | bytes 786440 | tf_op jit(solution)/shard_map/ppermute | solution.py:42
  3.5 5.6 %collective-permute-start.1 = (bf16[2,512,128]{2,1,0:T(8,128)(2,1)S(1)}, bf16[2,512,128]{2,1,0:T(8,128)(2,1)S(1)}, u32[]{:S(2)}, u32[]{:S(2)}) collective-permute-start(bf16[2,512,128]{2,1,0:T(8,128)(2,1)S(1)} %fusion.11), channel_id=1, source_target_pairs={{0,48},{8,200},{16,0},{24,216},{32,16},{40,232},{48,32},{56,248},{... | collective-permute-start | bytes 786440 | tf_op jit(solution)/shard_map/ppermute | solution.py:42
  9.0 9.9 %collective-permute-start.2 = (bf16[512,128]{1,0:T(8,128)(2,1)S(1)}, bf16[512,128]{1,0:T(8,128)(2,1)S(1)}, u32[]{:S(2)}, u32[]{:S(2)}) collective-permute-start(bf16[512,128]{1,0:T(8,128)(2,1)S(1)} %slice_bitcast_fusion.7), channel_id=1, source_target_pairs={{0,16},{8,72},{16,32},{24,88},{32,48},{40,104},{48,0},{56,120},{64... | collective-permute-start | bytes 393224 | tf_op jit(solution)/shard_map/ppermute | solution.py:42
  9.1 9.9 %copy-start.13 = (bf16[2,512,128]{2,1,0:T(8,128)(2,1)}, bf16[2,512,128]{2,1,0:T(8,128)(2,1)S(1)}, u32[]{:S(2)}) copy-start(bf16[2,512,128]{2,1,0:T(8,128)(2,1)S(1)} %collective-permute-done.1) | copy-start | bytes 786436
  9.1 9.8 %collective-permute-start.3 = (bf16[512,128]{1,0:T(8,128)(2,1)S(1)}, bf16[512,128]{1,0:T(8,128)(2,1)S(1)}, u32[]{:S(2)}, u32[]{:S(2)}) collective-permute-start(bf16[512,128]{1,0:T(8,128)(2,1)S(1)} %slice_bitcast_fusion.6), channel_id=1, source_target_pairs={{0,48},{8,200},{16,0},{24,216},{32,16},{40,232},{48,32},{56,248},{... | collective-permute-start | bytes 393224 | tf_op jit(solution)/shard_map/ppermute | solution.py:42
  13.1 12.6 %copy-start.14 = (s32[32,8]{0,1:T(8,128)S(1)}, s32[32,8]{0,1:T(8,128)}, u32[]{:S(2)}) copy-start(s32[32,8]{0,1:T(8,128)} %param.9) | copy-start | bytes 3076
  13.1 12.7 %copy-start.16 = (s32[32,2]{0,1:T(2,128)S(1)}, s32[32,2]{0,1:T(2,128)}, u32[]{:S(2)}) copy-start(s32[32,2]{0,1:T(2,128)} %param.11) | copy-start | bytes 772
  13.1 29.9 %copy-start.15 = (s32[32,8]{0,1:T(8,128)S(1)}, s32[32,8]{0,1:T(8,128)}, u32[]{:S(2)}) copy-start(s32[32,8]{0,1:T(8,128)} %param.10) | copy-start | bytes 3076
  13.1 27.2 %collective-permute-start.16 = (bf16[512,1024]{1,0:T(8,128)(2,1)S(1)}, bf16[512,1024]{1,0:T(8,128)(2,1)}, u32[]{:S(2)}, u32[]{:S(2)}) collective-permute-start(bf16[512,1024]{1,0:T(8,128)(2,1)S(1)} %constant_dynamic-slice_fusion.refs_4_), channel_id=1, source_target_pairs={{0,1},{1,2},{2,3},{3,4},{4,5},{5,6},{6,7},{7,0},{8,9},{9,10},{10,1... | collective-permute-start | bytes 3145736 | tf_op jit(solution)/shard_map/ppermute | solution.py:190
  14.9 28.2 %collective-permute-start.17 = (bf16[512,1024]{1,0:T(8,128)(2,1)S(1)}, bf16[512,1024]{1,0:T(8,128)(2,1)}, u32[]{:S(2)}, u32[]{:S(2)}) collective-permute-start(bf16[512,1024]{1,0:T(8,128)(2,1)S(1)} %constant_dynamic-slice_fusion.refs_4_), channel_id=1, source_target_pairs={{0,7},{1,0},{2,1},{3,2},{4,3},{5,4},{6,5},{7,6},{8,15},{9,8},{10,9... | collective-permute-start | bytes 3145736 | tf_op jit(solution)/shard_map/ppermute | solution.py:193
  20.1 23.0 %collective-permute-start.4 = (bf16[2,4,512,128]{3,2,1,0:T(8,128)(2,1)S(1)}, bf16[2,4,512,128]{3,2,1,0:T(8,128)(2,1)}, u32[]{:S(2)}, u32[]{:S(2)}) collective-permute-start(bf16[2,4,512,128]{3,2,1,0:T(8,128)(2,1)S(1)} %pad_maximum_fusion.l0), channel_id=1, source_target_pairs={{0,64},{8,24},{16,80},{24,40},{32,96},{40,56},{48,112},{56,8},{64,... | collective-permute-start | bytes 3145736 | tf_op jit(solution)/shard_map/ppermute | solution.py:42
  21.1 25.8 %collective-permute-start.5 = (bf16[2,4,512,128]{3,2,1,0:T(8,128)(2,1)S(1)}, bf16[2,4,512,128]{3,2,1,0:T(8,128)(2,1)}, u32[]{:S(2)}, u32[]{:S(2)}) collective-permute-start(bf16[2,4,512,128]{3,2,1,0:T(8,128)(2,1)S(1)} %pad_maximum_fusion.l0), channel_id=1, source_target_pairs={{0,192},{8,56},{16,208},{24,8},{32,224},{40,24},{48,240},{56,40},{... | collective-permute-start | bytes 3145736 | tf_op jit(solution)/shard_map/ppermute | solution.py:42
  22.8 26.9 %collective-permute-start.24 = (bf16[512,1024]{1,0:T(8,128)(2,1)S(1)}, bf16[512,1024]{1,0:T(8,128)(2,1)}, u32[]{:S(2)}, u32[]{:S(2)}) collective-permute-start(bf16[512,1024]{1,0:T(8,128)(2,1)S(1)} %constant_dynamic-slice_fusion.refs_4_), channel_id=1, source_target_pairs={{0,8},{8,0},{16,24},{24,16},{32,40},{40,32},{48,56},{56,48},{64,72... | collective-permute-start | bytes 3145736 | tf_op jit(solution)/shard_map/ppermute | solution.py:42
  40.3 11.3 %collective-permute-start.8 = (bf16[2,4,512,128]{3,2,1,0:T(8,128)(2,1)S(1)}, bf16[2,4,512,128]{3,2,1,0:T(8,128)(2,1)S(1)}, u32[]{:S(2)}, u32[]{:S(2)}) collective-permute-start(bf16[2,4,512,128]{3,2,1,0:T(8,128)(2,1)S(1)} %pad_maximum_fusion.l0), channel_id=1, source_target_pairs={{0,8},{8,0},{16,24},{24,16},{32,40},{40,32},{48,56},{56,48},{64,72... | collective-permute-start | bytes 3145736 | tf_op jit(solution)/shard_map/ppermute | solution.py:42
  43.0 26.3 %collective-permute-start.18 = (bf16[512,1024]{1,0:T(8,128)(2,1)}, bf16[512,1024]{1,0:T(8,128)(2,1)}, u32[]{:S(2)}, u32[]{:S(2)}) collective-permute-start(bf16[512,1024]{1,0:T(8,128)(2,1)} %collective-permute-done.16.refs_5_), channel_id=1, source_target_pairs={{0,1},{1,2},{2,3},{3,4},{4,5},{5,6},{6,7},{7,0},{8,9},{9,10},{10,1... | collective-permute-start | bytes 3145736 | tf_op jit(solution)/shard_map/ppermute | solution.py:190
  43.1 27.7 %collective-permute-start.19 = (bf16[512,1024]{1,0:T(8,128)(2,1)}, bf16[512,1024]{1,0:T(8,128)(2,1)}, u32[]{:S(2)}, u32[]{:S(2)}) collective-permute-start(bf16[512,1024]{1,0:T(8,128)(2,1)} %collective-permute-done.17.refs_6_), channel_id=1, source_target_pairs={{0,7},{1,0},{2,1},{3,2},{4,3},{5,4},{6,5},{7,6},{8,15},{9,8},{10,9... | collective-permute-start | bytes 3145736 | tf_op jit(solution)/shard_map/ppermute | solution.py:193
  46.9 9.7 %collective-permute-start.6 = (bf16[4,512,128]{2,1,0:T(8,128)(2,1)S(1)}, bf16[4,512,128]{2,1,0:T(8,128)(2,1)}, u32[]{:S(2)}, u32[]{:S(2)}) collective-permute-start(bf16[4,512,128]{2,1,0:T(8,128)(2,1)S(1)} %slice_bitcast_fusion.1), channel_id=1, source_target_pairs={{0,64},{8,24},{16,80},{24,40},{32,96},{40,56},{48,112},{56,8},{64,... | collective-permute-start | bytes 1572872 | tf_op jit(solution)/shard_map/ppermute | solution.py:42
  49.8 20.1 %collective-permute-start.7 = (bf16[4,512,128]{2,1,0:T(8,128)(2,1)}, bf16[4,512,128]{2,1,0:T(8,128)(2,1)}, u32[]{:S(2)}, u32[]{:S(2)}) collective-permute-start(bf16[4,512,128]{2,1,0:T(8,128)(2,1)} %slice_bitcast_fusion), channel_id=1, source_target_pairs={{0,192},{8,56},{16,208},{24,8},{32,224},{40,24},{48,240},{56,40},{... | collective-permute-start | bytes 1572872 | tf_op jit(solution)/shard_map/ppermute | solution.py:42
  52.6 25.1 %collective-permute-start.10 = (bf16[2,4,512,128]{3,2,1,0:T(8,128)(2,1)}, bf16[2,4,512,128]{3,2,1,0:T(8,128)(2,1)}, u32[]{:S(2)}, u32[]{:S(2)}) collective-permute-start(bf16[2,4,512,128]{3,2,1,0:T(8,128)(2,1)} %collective-permute-done.5.d0), channel_id=1, source_target_pairs={{0,8},{8,0},{16,24},{24,16},{32,40},{40,32},{48,56},{56,48},{64,72... | collective-permute-start | bytes 3145736 | tf_op jit(solution)/shard_map/ppermute | solution.py:42
  56.6 21.2 %collective-permute-start.9 = (bf16[2,4,512,128]{3,2,1,0:T(8,128)(2,1)}, bf16[2,4,512,128]{3,2,1,0:T(8,128)(2,1)}, u32[]{:S(2)}, u32[]{:S(2)}) collective-permute-start(bf16[2,4,512,128]{3,2,1,0:T(8,128)(2,1)} %collective-permute-done.4.u0), channel_id=1, source_target_pairs={{0,8},{8,0},{16,24},{24,16},{32,40},{40,32},{48,56},{56,48},{64,72... | collective-permute-start | bytes 3145736 | tf_op jit(solution)/shard_map/ppermute | solution.py:42
  69.3 25.4 %collective-permute-start.20 = (bf16[512,1024]{1,0:T(8,128)(2,1)}, bf16[512,1024]{1,0:T(8,128)(2,1)}, u32[]{:S(2)}, u32[]{:S(2)}) collective-permute-start(bf16[512,1024]{1,0:T(8,128)(2,1)} %collective-permute-done.18.refs_7_), channel_id=1, source_target_pairs={{0,1},{1,2},{2,3},{3,4},{4,5},{5,6},{6,7},{7,0},{8,9},{9,10},{10,1... | collective-permute-start | bytes 3145736 | tf_op jit(solution)/shard_map/ppermute | solution.py:190
  69.8 2.6 %collective-permute-start.11 = (bf16[4,512,128]{2,1,0:T(8,128)(2,1)}, bf16[4,512,128]{2,1,0:T(8,128)(2,1)S(1)}, u32[]{:S(2)}, u32[]{:S(2)}) collective-permute-start(bf16[4,512,128]{2,1,0:T(8,128)(2,1)} %collective-permute-done.6.fk0), channel_id=1, source_target_pairs={{0,8},{8,0},{16,24},{24,16},{32,40},{40,32},{48,56},{56,48},{64,72... | collective-permute-start | bytes 1572872 | tf_op jit(solution)/shard_map/ppermute | solution.py:42
  70.8 6.2 %collective-permute-start.12 = (bf16[4,512,128]{2,1,0:T(8,128)(2,1)}, bf16[4,512,128]{2,1,0:T(8,128)(2,1)}, u32[]{:S(2)}, u32[]{:S(2)}) collective-permute-start(bf16[4,512,128]{2,1,0:T(8,128)(2,1)} %collective-permute-done.7.fv0), channel_id=1, source_target_pairs={{0,8},{8,0},{16,24},{24,16},{32,40},{40,32},{48,56},{56,48},{64,72... | collective-permute-start | bytes 1572872 | tf_op jit(solution)/shard_map/ppermute | solution.py:42
  73.3 52.1 %collective-permute-start.21 = (bf16[512,1024]{1,0:T(8,128)(2,1)}, bf16[512,1024]{1,0:T(8,128)(2,1)}, u32[]{:S(2)}, u32[]{:S(2)}) collective-permute-start(bf16[512,1024]{1,0:T(8,128)(2,1)} %collective-permute-done.19.refs_8_), channel_id=1, source_target_pairs={{0,7},{1,0},{2,1},{3,2},{4,3},{5,4},{6,5},{7,6},{8,15},{9,8},{10,9... | collective-permute-start | bytes 3145736 | tf_op jit(solution)/shard_map/ppermute | solution.py:193
  77.0 51.8 %collective-permute-start.25 = (bf16[512,1024]{1,0:T(8,128)(2,1)}, bf16[512,1024]{1,0:T(8,128)(2,1)}, u32[]{:S(2)}, u32[]{:S(2)}) collective-permute-start(bf16[512,1024]{1,0:T(8,128)(2,1)} %collective-permute-done.16.refs_5_), channel_id=1, source_target_pairs={{0,8},{8,0},{16,24},{24,16},{32,40},{40,32},{48,56},{56,48},{64,72... | collective-permute-start | bytes 3145736 | tf_op jit(solution)/shard_map/ppermute | solution.py:42
  77.7 52.2 %collective-permute-start.26 = (bf16[512,1024]{1,0:T(8,128)(2,1)}, bf16[512,1024]{1,0:T(8,128)(2,1)}, u32[]{:S(2)}, u32[]{:S(2)}) collective-permute-start(bf16[512,1024]{1,0:T(8,128)(2,1)} %collective-permute-done.17.refs_6_), channel_id=1, source_target_pairs={{0,8},{8,0},{16,24},{24,16},{32,40},{40,32},{48,56},{56,48},{64,72... | collective-permute-start | bytes 3145736 | tf_op jit(solution)/shard_map/ppermute | solution.py:42
  77.8 66.1 %collective-permute-start.27 = (bf16[512,1024]{1,0:T(8,128)(2,1)}, bf16[512,1024]{1,0:T(8,128)(2,1)}, u32[]{:S(2)}, u32[]{:S(2)}) collective-permute-start(bf16[512,1024]{1,0:T(8,128)(2,1)} %collective-permute-done.18.refs_7_), channel_id=1, source_target_pairs={{0,8},{8,0},{16,24},{24,16},{32,40},{40,32},{48,56},{56,48},{64,72... | collective-permute-start | bytes 3145736 | tf_op jit(solution)/shard_map/ppermute | solution.py:42
  94.8 49.4 %collective-permute-start.28 = (bf16[512,1024]{1,0:T(8,128)(2,1)}, bf16[512,1024]{1,0:T(8,128)(2,1)}, u32[]{:S(2)}, u32[]{:S(2)}) collective-permute-start(bf16[512,1024]{1,0:T(8,128)(2,1)} %collective-permute-done.19.refs_8_), channel_id=1, source_target_pairs={{0,8},{8,0},{16,24},{24,16},{32,40},{40,32},{48,56},{56,48},{64,72... | collective-permute-start | bytes 3145736 | tf_op jit(solution)/shard_map/ppermute | solution.py:42
  96.5 1.2 copy-start.5
  97.8 1.0 copy-start.6
  98.8 1.0 copy-start.8
  118.1 23.3 %all-to-all-start = ((bf16[8,64,512]{2,1,0:T(8,128)(2,1)}), bf16[8,64,512]{2,1,0:T(8,128)(2,1)S(1)}, u32[]{:S(2)}, u32[]{:S(2)}) async-start(bf16[8,64,512]{2,1,0:T(8,128)(2,1)} %copy-done.3), calls=%async_computation | async-start | bytes 1048576 | tf_op jit(solution)/shard_map/all_to_all | solution.py:279
  125.3 24.0 %collective-permute-start.22 = (bf16[256,1024]{1,0:T(8,128)(2,1)}, bf16[256,1024]{1,0:T(8,128)(2,1)S(1)}, u32[]{:S(2)}, u32[]{:S(2)}) collective-permute-start(bf16[256,1024]{1,0:T(8,128)(2,1)} %slice.65), channel_id=1, source_target_pairs={{0,1},{1,2},{2,3},{3,4},{4,5},{5,6},{6,7},{7,0},{8,9},{9,10},{10,1... | collective-permute-start | bytes 1572872 | tf_op jit(solution)/shard_map/ppermute | solution.py:190
  128.7 21.7 %collective-permute-start.23 = (bf16[256,1024]{1,0:T(8,128)(2,1)}, bf16[256,1024]{1,0:T(8,128)(2,1)}, u32[]{:S(2)}, u32[]{:S(2)}) collective-permute-start(bf16[256,1024]{1,0:T(8,128)(2,1)} %slice.66), channel_id=1, source_target_pairs={{0,7},{1,0},{2,1},{3,2},{4,3},{5,4},{6,5},{7,6},{8,15},{9,8},{10,9... | collective-permute-start | bytes 1572872 | tf_op jit(solution)/shard_map/ppermute | solution.py:193
  141.5 12.2 %collective-permute-start.13 = (bf16[8,64,512]{2,1,0:T(8,128)(2,1)S(1)}, bf16[8,64,512]{2,1,0:T(8,128)(2,1)S(1)}, u32[]{:S(2)}, u32[]{:S(2)}) collective-permute-start(bf16[8,64,512]{2,1,0:T(8,128)(2,1)S(1)} %all-to-all-done.refs_0_), channel_id=1, source_target_pairs={{0,16},{8,56},{16,0},{24,40},{32,48},{40,24},{48,32},{56,8},{64,80... | collective-permute-start | bytes 1572872 | tf_op jit(solution)/shard_map/ppermute | solution.py:42
  143.9 10.6 %collective-permute-start.14 = (bf16[8,64,512]{2,1,0:T(8,128)(2,1)S(1)}, bf16[8,64,512]{2,1,0:T(8,128)(2,1)S(1)}, u32[]{:S(2)}, u32[]{:S(2)}) collective-permute-start(bf16[8,64,512]{2,1,0:T(8,128)(2,1)S(1)} %all-to-all-done.refs_0_), channel_id=1, source_target_pairs={{0,64},{8,200},{16,80},{24,216},{32,96},{40,232},{48,112},{56,248}... | collective-permute-start | bytes 1572872 | tf_op jit(solution)/shard_map/ppermute | solution.py:42
  144.2 17.6 %collective-permute-start.29 = (bf16[512,1024]{1,0:T(8,128)(2,1)}, bf16[512,1024]{1,0:T(8,128)(2,1)S(1)}, u32[]{:S(2)}, u32[]{:S(2)}) collective-permute-start(bf16[512,1024]{1,0:T(8,128)(2,1)} %collective-permute-done.20.refs_9_), channel_id=1, source_target_pairs={{0,8},{8,0},{16,24},{24,16},{32,40},{40,32},{48,56},{56,48},{64,72... | collective-permute-start | bytes 3145736 | tf_op jit(solution)/shard_map/ppermute | solution.py:42
  149.3 12.5 %collective-permute-start.30 = (bf16[512,1024]{1,0:T(8,128)(2,1)}, bf16[512,1024]{1,0:T(8,128)(2,1)S(1)}, u32[]{:S(2)}, u32[]{:S(2)}) collective-permute-start(bf16[512,1024]{1,0:T(8,128)(2,1)} %collective-permute-done.21.refs_10_), channel_id=1, source_target_pairs={{0,8},{8,0},{16,24},{24,16},{32,40},{40,32},{48,56},{56,48},{64,72... | collective-permute-start | bytes 3145736 | tf_op jit(solution)/shard_map/ppermute | solution.py:42
  150.4 11.4 %collective-permute-start.15 = (bf16[8,64,512]{2,1,0:T(8,128)(2,1)S(1)}, bf16[8,64,512]{2,1,0:T(8,128)(2,1)S(1)}, u32[]{:S(2)}, u32[]{:S(2)}) collective-permute-start(bf16[8,64,512]{2,1,0:T(8,128)(2,1)S(1)} %all-to-all-done.refs_0_), channel_id=1, source_target_pairs={{0,80},{8,248},{16,64},{24,232},{32,112},{40,216},{48,96},{56,200}... | collective-permute-start | bytes 1572872 | tf_op jit(solution)/shard_map/ppermute | solution.py:42
  153.7 8.1 %collective-permute-start.31 = (bf16[256,1024]{1,0:T(8,128)(2,1)S(1)}, bf16[256,1024]{1,0:T(8,128)(2,1)S(1)}, u32[]{:S(2)}, u32[]{:S(2)}) collective-permute-start(bf16[256,1024]{1,0:T(8,128)(2,1)S(1)} %collective-permute-done.22.refs_11_), channel_id=1, source_target_pairs={{0,8},{8,0},{16,24},{24,16},{32,40},{40,32},{48,56},{56,48},{64,72... | collective-permute-start | bytes 1572872 | tf_op jit(solution)/shard_map/ppermute | solution.py:42
  154.5 7.3 %collective-permute-start.32 = (bf16[256,1024]{1,0:T(8,128)(2,1)}, bf16[256,1024]{1,0:T(8,128)(2,1)S(1)}, u32[]{:S(2)}, u32[]{:S(2)}) collective-permute-start(bf16[256,1024]{1,0:T(8,128)(2,1)} %collective-permute-done.23.refs_12_), channel_id=1, source_target_pairs={{0,8},{8,0},{16,24},{24,16},{32,40},{40,32},{48,56},{56,48},{64,72... | collective-permute-start | bytes 1572872 | tf_op jit(solution)/shard_map/ppermute | solution.py:42
  162.8 1.0 copy-start.12
  163.8 1.0 copy-start.2
  164.9 1.0 copy-start.10
  175.3 8.7 %collective-permute-start.33 = (bf16[64,2048]{1,0:T(8,128)(2,1)S(1)}, bf16[64,2048]{1,0:T(8,128)(2,1)S(1)}, u32[]{:S(2)}, u32[]{:S(2)}) collective-permute-start(bf16[64,2048]{1,0:T(8,128)(2,1)S(1)} %get-tuple-element.11), channel_id=1, source_target_pairs={{0,80},{8,248},{16,64},{24,232},{32,112},{40,216},{48,96},{56,200}... | collective-permute-start | bytes 786440 | tf_op jit(solution)/shard_map/ppermute | solution.py:42
  177.8 8.9 %collective-permute-start.34 = (bf16[64,2048]{1,0:T(8,128)(2,1)S(1)}, bf16[64,2048]{1,0:T(8,128)(2,1)S(1)}, u32[]{:S(2)}, u32[]{:S(2)}) collective-permute-start(bf16[64,2048]{1,0:T(8,128)(2,1)S(1)} %get-tuple-element.10), channel_id=1, source_target_pairs={{0,64},{8,200},{16,80},{24,216},{32,96},{40,232},{48,112},{56,248}... | collective-permute-start | bytes 786440 | tf_op jit(solution)/shard_map/ppermute | solution.py:42
  180.2 6.5 %collective-permute-start.35 = (bf16[64,2048]{1,0:T(8,128)(2,1)S(1)}, bf16[64,2048]{1,0:T(8,128)(2,1)}, u32[]{:S(2)}, u32[]{:S(2)}) collective-permute-start(bf16[64,2048]{1,0:T(8,128)(2,1)S(1)} %get-tuple-element.9), channel_id=1, source_target_pairs={{0,16},{8,56},{16,0},{24,40},{32,48},{40,24},{48,32},{56,8},{64,80... | collective-permute-start | bytes 786440 | tf_op jit(solution)/shard_map/ppermute | solution.py:42
  (6 other events, 5.2 us)

commit v3 on v2

--- a/solution.py
+++ b/solution.py
@@ -174,6 +174,7 @@
             pltpu.SemaphoreType.DMA((2, 32)),
         ],
         compiler_params=pltpu.CompilerParams(vmem_limit_bytes=24 * 2**20),
+        cost_estimate=pl.CostEstimate(flops=2**31, bytes_accessed=48 * 2**20, transcendentals=2**21),
         name="attend",
     )(slots, vertical, diag, query, kpv, kpd, *pieces)
 
@@ -182,55 +183,53 @@
     return [(i, (i + step) % n) for i in range(n)]
 
 
-def gather_weight(own):
-    n = lax.axis_size("tp")
-    half = own.shape[0] // 2
-
-    def up(a):
-        return lax.ppermute(a, "tp", ring(n, 1))
-
-    def down(a):
-        return lax.ppermute(a, "tp", ring(n, -1))
-
-    u1, d1 = up(own), down(own)
-    u2, d2 = up(u1), down(d1)
-    u3, d3 = up(u2), down(d2)
-    u4, d4 = up(u3[:half]), down(d3[half:])
-    mine = [own, u1, d1, u2, d2, u3, d3, u4, d4]
-    return mine + [send(a, SWAP) for a in mine]
+def after(arrays, dep):
+    count = len(arrays)
+    hbm = pl.BlockSpec(memory_space=pl.ANY)
+    return pl.pallas_call(
+        lambda *refs: None,
+        out_shape=[jax.ShapeDtypeStruct(a.shape, a.dtype) for a in arrays],
+        in_specs=[hbm] * (count + 1),
+        out_specs=[hbm] * count,
+        input_output_aliases={i: i for i in range(count)},
+        name="after",
+    )(*arrays, dep)
+
+
+def up(a):
+    return lax.ppermute(a, "tp", ring(lax.axis_size("tp"), 1))
+
+
+def down(a):
+    return lax.ppermute(a, "tp", ring(lax.axis_size("tp"), -1))
 
 
 def project_kernel(place_ref, *refs):
-    rows, weights = refs[:4], refs[4:22]
-    o_ref, wbuf, acc, sems = refs[22:]
+    rows, weights = refs[:8], refs[8:17]
+    mine_ref, theirs_ref, wbuf, acc, sems = refs[17:]
     n, group, depth = rows[0].shape
-    cols = weights[0].shape[1]
-    tp, core = place_ref[0], place_ref[1]
+    tp = place_ref[0]
     half = depth // 2
     copies = []
-    for side in range(2):
-        for i in range(9):
-            dst = wbuf.at[side, i] if i < 7 else wbuf.at[side, 7, pl.ds((i - 7) * half, half)]
-            copies.append(pltpu.make_async_copy(weights[side * 9 + i], dst, sems.at[side * 9 + i]))
+    for i in range(9):
+        dst = wbuf.at[i] if i < 7 else wbuf.at[7, pl.ds((i - 7) * half, half)]
+        copies.append(pltpu.make_async_copy(weights[i], dst, sems.at[i]))
     for c in copies:
         c.start()
-    steps = (0, -1, 1, -2, 2, -3, 3, 4)
-    for i, step in enumerate(steps):
+    for i, step in enumerate((0, -1, 1, -2, 2, -3, 3, 4)):
         k = lax.rem(tp + step + n, n)
         a = jnp.concatenate([r[k] for r in rows], axis=0)
-        for side in range(2):
-            copies[side * 9 + i].wait()
-            if i == 7:
-                copies[side * 9 + 8].wait()
-            part = jnp.dot(a, wbuf[side, i], preferred_element_type=jnp.float32)
-            if i == 0:
-                acc[side] = part
-            else:
-                acc[side] += part
-    for side in range(2):
-        col = pl.ds(pl.multiple_of((core if side == 0 else 1 - core) * cols, cols), cols)
-        for r in range(4):
-            o_ref[r, :, col] = acc[side, pl.ds(r * group, group), :].astype(jnp.bfloat16)
+        copies[i].wait()
+        if i == 7:
+            copies[8].wait()
+        part = jnp.dot(a, wbuf[i], preferred_element_type=jnp.float32)
+        if i == 0:
+            acc[...] = part
+        else:
+            acc[...] += part
+    for r in range(4):
+        mine_ref[r] = acc[pl.ds(r * group, group), :].astype(jnp.bfloat16)
+        theirs_ref[r] = acc[pl.ds((r + 4) * group, group), :].astype(jnp.bfloat16)
 
 
 def project(rows, weights, place):
@@ -240,15 +239,16 @@
     hbm = pl.BlockSpec(memory_space=pl.ANY)
     return pl.pallas_call(
         project_kernel,
-        out_shape=jax.ShapeDtypeStruct((4, group, 2 * cols), jnp.bfloat16),
-        in_specs=[pl.BlockSpec(memory_space=pltpu.SMEM)] + [vmem] * 4 + [hbm] * len(weights),
-        out_specs=vmem,
+        out_shape=[jax.ShapeDtypeStruct((4, group, cols), jnp.bfloat16)] * 2,
+        in_specs=[pl.BlockSpec(memory_space=pltpu.SMEM)] + [vmem] * 8 + [hbm] * 9,
+        out_specs=[vmem] * 2,
         scratch_shapes=[
-            pltpu.VMEM((2, n, depth, cols), jnp.bfloat16),
-            pltpu.VMEM((2, 4 * group, cols), jnp.float32),
-            pltpu.SemaphoreType.DMA((18,)),
+            pltpu.VMEM((n, depth, cols), jnp.bfloat16),
+            pltpu.VMEM((8 * group, cols), jnp.float32),
+            pltpu.SemaphoreType.DMA((9,)),
         ],
-        compiler_params=pltpu.CompilerParams(vmem_limit_bytes=40 * 2**20),
+        compiler_params=pltpu.CompilerParams(vmem_limit_bytes=32 * 2**20),
+        cost_estimate=pl.CostEstimate(flops=2**32, bytes_accessed=2**24, transcendentals=0),
         name="project",
     )(place, *rows, *weights)
 
@@ -262,12 +262,21 @@
     y_odd = (seq_index // (NC * NX)) % 2
     block = y_odd * 2 + x_odd
     cols = out_weight.shape[1] // 8
+    depth = out_weight.shape[0] // 2
     kv_head = tp_index // (lax.axis_size("tp") // keyval.shape[1])
     own = lax.dynamic_index_in_dim(keyval, kv_head, 1, keepdims=False)
-    pieces = gather_keyval(own)
-    weights = gather_weight(
-        lax.dynamic_slice_in_dim(out_weight, (block * 2 + core) * cols, cols, 1)
-    )
+    w0 = lax.dynamic_slice_in_dim(out_weight, (block * 2 + core) * cols, cols, 1)
+
+    up_a, down_a = send(own, A_UP), send(own, A_DOWN)
+    w_u1, w_d1 = up(w0), down(w0)
+    far = jnp.stack([send(up_a[0], A_UP), send(down_a[1], A_DOWN)])
+    line = jnp.stack([own, up_a, down_a, far], axis=1)
+    up_b, down_b = send(line, B_UP), send(line, B_DOWN)
+    far_k, far_v = send(up_b[0], B_UP), send(down_b[1], B_DOWN)
+    w_u1, w_d1 = after([w_u1, w_d1], down_b)
+    w_u2, w_d2 = up(w_u1), down(w_d1)
+    pieces = [line, up_b, down_b, far_k, far_v]
+    pieces += [send(a, SWAP) for a in pieces]
 
     def mine(a):
         return lax.dynamic_slice_in_dim(a, tp_index * heads, heads, 0)
@@ -276,10 +285,20 @@
         query, pieces, shard_slots(seq_index), mine(vert_blocks), mine(slash_offsets),
         mine(counts), seq_index,
     )
+    w_u2, w_d2 = after([w_u2, w_d2], attended)
+    w_u3, w_d3 = up(w_u2), down(w_d2)
     tokens = lax.all_to_all(attended, "tp", split_axis=0, concat_axis=0, tiled=True)
+    w_u3, w_d3 = after([w_u3, w_d3], tokens)
+    w_u4, w_d4 = up(w_u3[:depth]), down(w_d3[depth:])
     moves = (PAIR_X, PAIR_Y, PAIR_XY)
-    out = project(
-        [tokens] + [send(tokens, m) for m in moves], weights, jnp.stack([tp_index, core])
+    group = [tokens] + [send(tokens, m) for m in moves]
+    group += [send(a, SWAP) for a in group]
+    ours, theirs = project(
+        group, [w0, w_u1, w_d1, w_u2, w_d2, w_u3, w_d3, w_u4, w_d4], jnp.stack([tp_index, core])
+    )
+    other = send(theirs, SWAP)
+    out = jnp.concatenate(
+        [jnp.where(core == 0, ours, other), jnp.where(core == 0, other, ours)], axis=2
     )
     back = [out[0]] + [send(out[i + 1], m) for i, m in enumerate(moves)]
     odd_x, odd_y = x_odd == 1, y_odd == 1

time: 190 us -> 164 us (0.86)
  waiting for transfers between devices: 79.7 us -> 64.9 us
  local copies, waits for them, and re-layouts: 22.3 us -> 13.4 us
    ppermute x8, waiting for transfers between devices: 47.4 us -> 4.45 us  [the longest x4 4.11 us: up(): return lax.ppermute(a, 'tp', ring(lax.axis_size('tp'), 1))]
    all_to_all x1, waiting for transfers between devices: 11.5 us -> 29.2 us  [per_device(): lax.all_to_all(attended, 'tp', split_axis=0, concat_axis=0, tiled=True)]
    ppermute x28 -> x24, waiting for transfers between devices: 20.8 us -> 31.3 us  [send(): return lax.ppermute(a, 'seq', pairs)]
    unnamed x35 -> x23, local copies, waits for them, and re-layouts: 12.9 us -> 4.84 us
    pallas_call x1 -> x4, Pallas kernels: 9.3 us -> 8.15 us  [the longest x1 8.15 us: project(): pl.pallas_call(project_kernel, out_shape=[jax.ShapeDtypeStruct((4, group,...]
    ppermute x28 -> x24, starting transfers between devices: 35.9 us -> 35.9 us  [send(): return lax.ppermute(a, 'seq', pairs)]
  transfers between devices with their start and end apart: 37 -> 33, of which waited for: 11 -> 16; matrix products, arithmetic and copies ran while one was open for 6% -> 6% of each run, Pallas kernels for 9% -> 11%
where the time goes in v3:
time: 164 us; the launch traced here: 163 us
  waiting for transfers between devices  64.9 us (40%)
  starting transfers between devices  54.6 us (33%)
  Pallas kernels  26.5 us (16%)
  local copies, waits for them, and re-layouts  13.4 us (8%)
  other arithmetic  3.48 us (2%)
    ppermute x24, starting transfers between devices, send(): return lax.ppermute(a, 'seq', pairs)  35.9 us
    ppermute x24, waiting for transfers between devices, send(): return lax.ppermute(a, 'seq', pairs)  31.3 us
    all_to_all x1, waiting for transfers between devices, per_device(): lax.all_to_all(attended, 'tp', split_axis=0, concat_axis=0, tiled=True)  29.2 us
    pallas_call x1, Pallas kernels, attend(): pl.pallas_call(attend_kernel, out_shape=jax.ShapeDtypeStruct((blocks, BLK...  18.3 us
    ppermute x4, starting transfers between devices, down(): return lax.ppermute(a, 'tp', ring(lax.axis_size('tp'), -1))  12.5 us
    pallas_call x1, Pallas kernels, project(): pl.pallas_call(project_kernel, out_shape=[jax.ShapeDtypeStruct((4, group,...  8.15 us
    unnamed x23, local copies, waits for them, and re-layouts  4.84 us
    all_to_all x1, starting transfers between devices, per_device(): lax.all_to_all(attended, 'tp', split_axis=0, concat_axis=0, tiled=True)  4.16 us
  transfers between devices with their start and end apart: 33, of which 16 were waited for; matrix products, arithmetic and copies ran while one was open for 6% of the time, Pallas kernels for 11%

profile of v3, /device:TPU:1, one launch (start us, length us, event | category | flops | bytes accessed | tf_op | source)
XLA Modules:
  0.0 163.2 jit_solution(14400036903232015024)
XLA Ops:
  0.0 1.2 copy-done
  1.2 3.6 %collective-permute-start.1 = (bf16[2,512,128]{2,1,0:T(8,128)(2,1)S(1)}, bf16[2,512,128]{2,1,0:T(8,128)(2,1)S(1)}, u32[]{:S(2)}, u32[]{:S(2)}) collective-permute-start(bf16[2,512,128]{2,1,0:T(8,128)(2,1)S(1)} %fusion.19), channel_id=1, source_target_pairs={{0,48},{8,200},{16,0},{24,216},{32,16},{40,232},{48,32},{56,248},{... | collective-permute-start | bytes 786440 | tf_op jit(solution)/shard_map/ppermute | solution.py:42
  4.9 3.3 %collective-permute-done.1 = bf16[2,512,128]{2,1,0:T(8,128)(2,1)S(1)} collective-permute-done((bf16[2,512,128]{2,1,0:T(8,128)(2,1)S(1)}, bf16[2,512,128]{2,1,0:T(8,128)(2,1)S(1)}, u32[]{:S(2)}, u32[]{:S(2)}) %collective-permute-start.1) | collective-permute-done | bytes 262176 | tf_op jit(solution)/shard_map/ppermute | solution.py:42
  8.2 3.2 %collective-permute-start.3 = (bf16[512,128]{1,0:T(8,128)(2,1)S(1)}, bf16[512,128]{1,0:T(8,128)(2,1)S(1)}, u32[]{:S(2)}, u32[]{:S(2)}) collective-permute-start(bf16[512,128]{1,0:T(8,128)(2,1)S(1)} %slice_bitcast_fusion.2), channel_id=1, source_target_pairs={{0,48},{8,200},{16,0},{24,216},{32,16},{40,232},{48,32},{56,248},{... | collective-permute-start | bytes 393224 | tf_op jit(solution)/shard_map/ppermute | solution.py:42
  11.7 2.3 %constant_dynamic-slice_fusion.refs_8_ = bf16[512,1024]{1,0:T(8,128)(2,1)} fusion(bf16[512,8192]{1,0:T(8,128)(2,1)} %param.12, s32[]{:T(128)S(6)} %select_n.232), kind=kLoop, calls=%fused_computation.63 | loop fusion | bytes 2097156 | tf_op jit(solution)/shard_map/dynamic_slice | solution.py:268
  14.0 1.6 %collective-permute-start.20 = (bf16[512,1024]{1,0:T(8,128)(2,1)}, bf16[512,1024]{1,0:T(8,128)(2,1)}, u32[]{:S(2)}, u32[]{:S(2)}) collective-permute-start(bf16[512,1024]{1,0:T(8,128)(2,1)} %constant_dynamic-slice_fusion.refs_8_), channel_id=1, source_target_pairs={{0,1},{1,2},{2,3},{3,4},{4,5},{5,6},{6,7},{7,0},{8,9},{9,10},{10,1... | collective-permute-start | bytes 3145736 | tf_op jit(solution)/shard_map/ppermute | solution.py:200
  15.7 4.0 %collective-permute-start.21 = (bf16[512,1024]{1,0:T(8,128)(2,1)}, bf16[512,1024]{1,0:T(8,128)(2,1)}, u32[]{:S(2)}, u32[]{:S(2)}) collective-permute-start(bf16[512,1024]{1,0:T(8,128)(2,1)} %constant_dynamic-slice_fusion.refs_8_), channel_id=1, source_target_pairs={{0,7},{1,0},{2,1},{3,2},{4,3},{5,4},{6,5},{7,6},{8,15},{9,8},{10,9... | collective-permute-start | bytes 3145736 | tf_op jit(solution)/shard_map/ppermute | solution.py:204
  19.9 1.1 collective-permute-start.4
  21.1 1.7 %collective-permute-start.5 = (bf16[2,4,512,128]{3,2,1,0:T(8,128)(2,1)S(1)}, bf16[2,4,512,128]{3,2,1,0:T(8,128)(2,1)S(1)}, u32[]{:S(2)}, u32[]{:S(2)}) collective-permute-start(bf16[2,4,512,128]{3,2,1,0:T(8,128)(2,1)S(1)} %pad_maximum_fusion.l0), channel_id=1, source_target_pairs={{0,192},{8,56},{16,208},{24,8},{32,224},{40,24},{48,240},{56,40},{... | collective-permute-start | bytes 3145736 | tf_op jit(solution)/shard_map/ppermute | solution.py:42
  23.1 2.5 %collective-permute-start.8 = (bf16[2,4,512,128]{3,2,1,0:T(8,128)(2,1)S(1)}, bf16[2,4,512,128]{3,2,1,0:T(8,128)(2,1)}, u32[]{:S(2)}, u32[]{:S(2)}) collective-permute-start(bf16[2,4,512,128]{3,2,1,0:T(8,128)(2,1)S(1)} %pad_maximum_fusion.l0), channel_id=1, source_target_pairs={{0,8},{8,0},{16,24},{24,16},{32,40},{40,32},{48,56},{56,48},{64,72... | collective-permute-start | bytes 3145736 | tf_op jit(solution)/shard_map/ppermute | solution.py:42
  25.7 9.5 %collective-permute-done.4.u0 = bf16[2,4,512,128]{3,2,1,0:T(8,128)(2,1)} collective-permute-done((bf16[2,4,512,128]{3,2,1,0:T(8,128)(2,1)S(1)}, bf16[2,4,512,128]{3,2,1,0:T(8,128)(2,1)}, u32[]{:S(2)}, u32[]{:S(2)}) %collective-permute-start.4) | collective-permute-done | bytes 1048608 | tf_op jit(solution)/shard_map/ppermute | solution.py:42
  35.2 2.8 %collective-permute-start.9 = (bf16[2,4,512,128]{3,2,1,0:T(8,128)(2,1)}, bf16[2,4,512,128]{3,2,1,0:T(8,128)(2,1)}, u32[]{:S(2)}, u32[]{:S(2)}) collective-permute-start(bf16[2,4,512,128]{3,2,1,0:T(8,128)(2,1)} %collective-permute-done.4.u0), channel_id=1, source_target_pairs={{0,8},{8,0},{16,24},{24,16},{32,40},{40,32},{48,56},{56,48},{64,72... | collective-permute-start | bytes 3145736 | tf_op jit(solution)/shard_map/ppermute | solution.py:42
  38.0 1.9 %slice_bitcast_fusion.1 = bf16[4,512,128]{2,1,0:T(8,128)(2,1)} fusion(bf16[2,4,512,128]{3,2,1,0:T(8,128)(2,1)} %collective-permute-done.4.u0), kind=kLoop, calls=%fused_computation.9 | loop fusion | bytes 1048576 | tf_op jit(solution)/shard_map/squeeze | solution.py:275
  39.9 0.7 and_reduce_fusion
  40.6 0.8 slice_bitcast_fusion
  41.7 2.7 %collective-permute-start.7 = (bf16[4,512,128]{2,1,0:T(8,128)(2,1)}, bf16[4,512,128]{2,1,0:T(8,128)(2,1)}, u32[]{:S(2)}, u32[]{:S(2)}) collective-permute-start(bf16[4,512,128]{2,1,0:T(8,128)(2,1)} %slice_bitcast_fusion), channel_id=1, source_target_pairs={{0,192},{8,56},{16,208},{24,8},{32,224},{40,24},{48,240},{56,40},{... | collective-permute-start | bytes 1572872 | tf_op jit(solution)/shard_map/ppermute | solution.py:42
  44.4 2.6 %collective-permute-start.10 = (bf16[2,4,512,128]{3,2,1,0:T(8,128)(2,1)S(1)}, bf16[2,4,512,128]{3,2,1,0:T(8,128)(2,1)}, u32[]{:S(2)}, u32[]{:S(2)}) collective-permute-start(bf16[2,4,512,128]{3,2,1,0:T(8,128)(2,1)S(1)} %collective-permute-done.5.d0.refs_2_), channel_id=1, source_target_pairs={{0,8},{8,0},{16,24},{24,16},{32,40},{40,32},{48,56},{56,48},{64,72... | collective-permute-start | bytes 3145736 | tf_op jit(solution)/shard_map/ppermute | solution.py:42
  47.1 2.9 %collective-permute-done.6.fk0 = bf16[4,512,128]{2,1,0:T(8,128)(2,1)} collective-permute-done((bf16[4,512,128]{2,1,0:T(8,128)(2,1)}, bf16[4,512,128]{2,1,0:T(8,128)(2,1)}, u32[]{:S(2)}, u32[]{:S(2)}) %collective-permute-start.6) | collective-permute-done | bytes 524320 | tf_op jit(solution)/shard_map/ppermute | solution.py:42
  50.0 3.2 %collective-permute-start.23 = (bf16[512,1024]{1,0:T(8,128)(2,1)}, bf16[512,1024]{1,0:T(8,128)(2,1)}, u32[]{:S(2)}, u32[]{:S(2)}) collective-permute-start(bf16[512,1024]{1,0:T(8,128)(2,1)} %get-tuple-element.14.refs_10_), channel_id=1, source_target_pairs={{0,7},{1,0},{2,1},{3,2},{4,3},{5,4},{6,5},{7,6},{8,15},{9,8},{10,9... | collective-permute-start | bytes 3145736 | tf_op jit(solution)/shard_map/ppermute | solution.py:204
  54.3 1.2 collective-permute-start.11
  55.7 1.5 collective-permute-done.11.fk1
  57.2 0.7 collective-permute-done.12.fv1
  57.9 1.2 copy-done.2
  59.2 1.0 copy-done.7
  60.2 18.3 %attend.1.refs_2_ = bf16[8,64,512]{2,1,0:T(8,128)(2,1)} custom-call(s32[32]{0:T(128)S(1)} %fusion.11.slots_ref, s32[4,8]{1,0:T(4,128)S(1)} %copy.30.vert_ref, s32[32,8]{1,0:T(8,128)S(1)} %fusion.7.diag_ref, bf16[4,512,128]{2,1,0:T(8,128)(2,1)S(1)} %copy-done.7, s32[4,1,512]{2,1,0:T(1,128)S(1)} %add_select_fusion.1.kpv_ref, ...), custom_call_target="tpu_custom_call" | custom-call | flops 2147483648 | bytes 50331648 | tf_op jit(solution)/shard_map/attend/pallas_call | solution.py:162
  78.7 4.2 %all-to-all-start = ((bf16[8,64,512]{2,1,0:T(8,128)(2,1)}), bf16[8,64,512]{2,1,0:T(8,128)(2,1)}, u32[]{:S(2)}, u32[]{:S(2)}) async-start(bf16[8,64,512]{2,1,0:T(8,128)(2,1)} %attend.1.refs_2_), calls=%async_computation | async-start | bytes 1048576 | tf_op jit(solution)/shard_map/all_to_all | solution.py:290
  82.8 2.7 %collective-permute-start.25 = (bf16[512,1024]{1,0:T(8,128)(2,1)}, bf16[512,1024]{1,0:T(8,128)(2,1)S(1)}, u32[]{:S(2)}, u32[]{:S(2)}) collective-permute-start(bf16[512,1024]{1,0:T(8,128)(2,1)} %get-tuple-element.16.refs_12_), channel_id=1, source_target_pairs={{0,7},{1,0},{2,1},{3,2},{4,3},{5,4},{6,5},{7,6},{8,15},{9,8},{10,9... | collective-permute-start | bytes 3145736 | tf_op jit(solution)/shard_map/ppermute | solution.py:204
  85.5 29.2 %all-to-all-done.refs_2_.refs_0_ = bf16[8,64,512]{2,1,0:T(8,128)(2,1)} async-done(((bf16[8,64,512]{2,1,0:T(8,128)(2,1)}), bf16[8,64,512]{2,1,0:T(8,128)(2,1)}, u32[]{:S(2)}, u32[]{:S(2)}) %all-to-all-start) | async-done | bytes 524320 | tf_op jit(solution)/shard_map/all_to_all | solution.py:290
  114.9 4.2 %collective-permute-start.14 = (bf16[8,64,512]{2,1,0:T(8,128)(2,1)}, bf16[8,64,512]{2,1,0:T(8,128)(2,1)}, u32[]{:S(2)}, u32[]{:S(2)}) collective-permute-start(bf16[8,64,512]{2,1,0:T(8,128)(2,1)} %all-to-all-done.refs_2_.refs_0_), channel_id=1, source_target_pairs={{0,64},{8,200},{16,80},{24,216},{32,96},{40,232},{48,112},{56,248}... | collective-permute-start | bytes 1572872 | tf_op jit(solution)/shard_map/ppermute | solution.py:42
  119.1 0.7 collective-permute-start.15
  119.8 0.7 collective-permute-start.16
  120.8 1.0 copy-done.5
  121.7 1.2 slice.45
  123.1 1.1 slice.46
  124.3 2.6 %collective-permute-start.27 = (bf16[256,1024]{1,0:T(8,128)(2,1)S(1)}, bf16[256,1024]{1,0:T(8,128)(2,1)S(1)}, u32[]{:S(2)}, u32[]{:S(2)}) collective-permute-start(bf16[256,1024]{1,0:T(8,128)(2,1)S(1)} %slice.46), channel_id=1, source_target_pairs={{0,7},{1,0},{2,1},{3,2},{4,3},{5,4},{6,5},{7,6},{8,15},{9,8},{10,9... | collective-permute-start | bytes 1572872 | tf_op jit(solution)/shard_map/ppermute | solution.py:204
  126.9 4.9 %collective-permute-done.14.refs_2_ = bf16[8,64,512]{2,1,0:T(8,128)(2,1)} collective-permute-done((bf16[8,64,512]{2,1,0:T(8,128)(2,1)}, bf16[8,64,512]{2,1,0:T(8,128)(2,1)}, u32[]{:S(2)}, u32[]{:S(2)}) %collective-permute-start.14) | collective-permute-done | bytes 524320 | tf_op jit(solution)/shard_map/ppermute | solution.py:42
  131.8 1.3 collective-permute-start.18
  133.2 3.8 %collective-permute-done.26.refs_15_ = bf16[256,1024]{1,0:T(8,128)(2,1)S(1)} collective-permute-done((bf16[256,1024]{1,0:T(8,128)(2,1)S(1)}, bf16[256,1024]{1,0:T(8,128)(2,1)S(1)}, u32[]{:S(2)}, u32[]{:S(2)}) %collective-permute-start.26) | collective-permute-done | bytes 524320 | tf_op jit(solution)/shard_map/ppermute | solution.py:200
  137.4 8.1 %project.1 = (bf16[4,64,1024]{2,1,0:T(8,128)(2,1)S(1)}, bf16[4,64,1024]{2,1,0:T(8,128)(2,1)S(1)}) custom-call(s32[2]{0:T(128)S(1)} %pad_add_fusion.place_ref, bf16[8,64,512]{2,1,0:T(8,128)(2,1)} %all-to-all-done.refs_2_.refs_0_, bf16[8,64,512]{2,1,0:T(8,128)(2,1)} %collective-permute-done.13.refs_1_, bf16[8,64,512]{2,1,0:T(8,128)(2,1)} %collective-permute-done.14.refs_2_, ...), custom_call_target="tpu_custom_call" | custom-call | flops 4294967296 | bytes 16777216 | tf_op jit(solution)/shard_map/project/pallas_call | solution.py:240
  145.5 2.3 %collective-permute-start.28 = (bf16[4,64,1024]{2,1,0:T(8,128)(2,1)S(1)}, bf16[4,64,1024]{2,1,0:T(8,128)(2,1)S(1)}, u32[]{:S(2)}, u32[]{:S(2)}) collective-permute-start(bf16[4,64,1024]{2,1,0:T(8,128)(2,1)S(1)} %get-tuple-element.20), channel_id=1, source_target_pairs={{0,8},{8,0},{16,24},{24,16},{32,40},{40,32},{48,56},{56,48},{64,72... | collective-permute-start | bytes 1572872 | tf_op jit(solution)/shard_map/ppermute | solution.py:42
  147.8 1.5 collective-permute-done.28
  149.4 0.8 fusion.1
  150.2 2.5 %collective-permute-start.30 = (bf16[64,2048]{1,0:T(8,128)(2,1)}, bf16[64,2048]{1,0:T(8,128)(2,1)S(1)}, u32[]{:S(2)}, u32[]{:S(2)}) collective-permute-start(bf16[64,2048]{1,0:T(8,128)(2,1)} %get-tuple-element.28), channel_id=1, source_target_pairs={{0,64},{8,200},{16,80},{24,216},{32,96},{40,232},{48,112},{56,248}... | collective-permute-start | bytes 786440 | tf_op jit(solution)/shard_map/ppermute | solution.py:42
  152.7 2.3 %collective-permute-start.29 = (bf16[64,2048]{1,0:T(8,128)(2,1)S(1)}, bf16[64,2048]{1,0:T(8,128)(2,1)S(1)}, u32[]{:S(2)}, u32[]{:S(2)}) collective-permute-start(bf16[64,2048]{1,0:T(8,128)(2,1)S(1)} %get-tuple-element.27), channel_id=1, source_target_pairs={{0,80},{8,248},{16,64},{24,232},{32,112},{40,216},{48,96},{56,200}... | collective-permute-start | bytes 786440 | tf_op jit(solution)/shard_map/ppermute | solution.py:42
  155.3 3.9 %collective-permute-done.30 = bf16[64,2048]{1,0:T(8,128)(2,1)S(1)} collective-permute-done((bf16[64,2048]{1,0:T(8,128)(2,1)}, bf16[64,2048]{1,0:T(8,128)(2,1)S(1)}, u32[]{:S(2)}, u32[]{:S(2)}) %collective-permute-start.30) | collective-permute-done | bytes 262176 | tf_op jit(solution)/shard_map/ppermute | solution.py:42
  159.2 2.1 %collective-permute-done.29 = bf16[64,2048]{1,0:T(8,128)(2,1)S(1)} collective-permute-done((bf16[64,2048]{1,0:T(8,128)(2,1)S(1)}, bf16[64,2048]{1,0:T(8,128)(2,1)S(1)}, u32[]{:S(2)}, u32[]{:S(2)}) %collective-permute-start.29) | collective-permute-done | bytes 262176 | tf_op jit(solution)/shard_map/ppermute | solution.py:42
  161.2 0.6 collective-permute-done.31
  162.1 1.0 pad_maximum_fusion.1
  (90 shorter events, 4.6 us)
Async XLA Ops:
  0.0 1.2 copy-start
  1.2 7.0 %collective-permute-start.1 = (bf16[2,512,128]{2,1,0:T(8,128)(2,1)S(1)}, bf16[2,512,128]{2,1,0:T(8,128)(2,1)S(1)}, u32[]{:S(2)}, u32[]{:S(2)}) collective-permute-start(bf16[2,512,128]{2,1,0:T(8,128)(2,1)S(1)} %fusion.19), channel_id=1, source_target_pairs={{0,48},{8,200},{16,0},{24,216},{32,16},{40,232},{48,32},{56,248},{... | collective-permute-start | bytes 786440 | tf_op jit(solution)/shard_map/ppermute | solution.py:42
  4.9 6.7 %collective-permute-start = (bf16[2,512,128]{2,1,0:T(8,128)(2,1)S(1)}, bf16[2,512,128]{2,1,0:T(8,128)(2,1)S(1)}, u32[]{:S(2)}, u32[]{:S(2)}) collective-permute-start(bf16[2,512,128]{2,1,0:T(8,128)(2,1)S(1)} %fusion.19), channel_id=1, source_target_pairs={{0,16},{8,72},{16,32},{24,88},{32,48},{40,104},{48,0},{56,120},{64... | collective-permute-start | bytes 786440 | tf_op jit(solution)/shard_map/ppermute | solution.py:42
  8.2 11.5 %collective-permute-start.3 = (bf16[512,128]{1,0:T(8,128)(2,1)S(1)}, bf16[512,128]{1,0:T(8,128)(2,1)S(1)}, u32[]{:S(2)}, u32[]{:S(2)}) collective-permute-start(bf16[512,128]{1,0:T(8,128)(2,1)S(1)} %slice_bitcast_fusion.2), channel_id=1, source_target_pairs={{0,48},{8,200},{16,0},{24,216},{32,16},{40,232},{48,32},{56,248},{... | collective-permute-start | bytes 393224 | tf_op jit(solution)/shard_map/ppermute | solution.py:42
  11.6 8.1 %collective-permute-start.2 = (bf16[512,128]{1,0:T(8,128)(2,1)S(1)}, bf16[512,128]{1,0:T(8,128)(2,1)S(1)}, u32[]{:S(2)}, u32[]{:S(2)}) collective-permute-start(bf16[512,128]{1,0:T(8,128)(2,1)S(1)} %slice_bitcast_fusion.3), channel_id=1, source_target_pairs={{0,16},{8,72},{16,32},{24,88},{32,48},{40,104},{48,0},{56,120},{64... | collective-permute-start | bytes 393224 | tf_op jit(solution)/shard_map/ppermute | solution.py:42
  14.0 7.0 %copy-start.8 = (s32[32,8]{0,1:T(8,128)S(1)}, s32[32,8]{0,1:T(8,128)}, u32[]{:S(2)}) copy-start(s32[32,8]{0,1:T(8,128)} %param.9) | copy-start | bytes 3076
  14.0 7.0 %copy-start.9 = (s32[32,8]{0,1:T(8,128)S(1)}, s32[32,8]{0,1:T(8,128)}, u32[]{:S(2)}) copy-start(s32[32,8]{0,1:T(8,128)} %param.10) | copy-start | bytes 3076
  14.0 9.0 %copy-start.10 = (s32[32,2]{0,1:T(2,128)S(1)}, s32[32,2]{0,1:T(2,128)}, u32[]{:S(2)}) copy-start(s32[32,2]{0,1:T(2,128)} %param.11) | copy-start | bytes 772
  14.0 27.7 %collective-permute-start.20 = (bf16[512,1024]{1,0:T(8,128)(2,1)}, bf16[512,1024]{1,0:T(8,128)(2,1)}, u32[]{:S(2)}, u32[]{:S(2)}) collective-permute-start(bf16[512,1024]{1,0:T(8,128)(2,1)} %constant_dynamic-slice_fusion.refs_8_), channel_id=1, source_target_pairs={{0,1},{1,2},{2,3},{3,4},{4,5},{5,6},{6,7},{7,0},{8,9},{9,10},{10,1... | collective-permute-start | bytes 3145736 | tf_op jit(solution)/shard_map/ppermute | solution.py:200
  15.7 28.7 %collective-permute-start.21 = (bf16[512,1024]{1,0:T(8,128)(2,1)}, bf16[512,1024]{1,0:T(8,128)(2,1)}, u32[]{:S(2)}, u32[]{:S(2)}) collective-permute-start(bf16[512,1024]{1,0:T(8,128)(2,1)} %constant_dynamic-slice_fusion.refs_8_), channel_id=1, source_target_pairs={{0,7},{1,0},{2,1},{3,2},{4,3},{5,4},{6,5},{7,6},{8,15},{9,8},{10,9... | collective-permute-start | bytes 3145736 | tf_op jit(solution)/shard_map/ppermute | solution.py:204
  19.9 15.3 %collective-permute-start.4 = (bf16[2,4,512,128]{3,2,1,0:T(8,128)(2,1)S(1)}, bf16[2,4,512,128]{3,2,1,0:T(8,128)(2,1)}, u32[]{:S(2)}, u32[]{:S(2)}) collective-permute-start(bf16[2,4,512,128]{3,2,1,0:T(8,128)(2,1)S(1)} %pad_maximum_fusion.l0), channel_id=1, source_target_pairs={{0,64},{8,24},{16,80},{24,40},{32,96},{40,56},{48,112},{56,8},{64,... | collective-permute-start | bytes 3145736 | tf_op jit(solution)/shard_map/ppermute | solution.py:42
  21.1 18.8 %collective-permute-start.5 = (bf16[2,4,512,128]{3,2,1,0:T(8,128)(2,1)S(1)}, bf16[2,4,512,128]{3,2,1,0:T(8,128)(2,1)S(1)}, u32[]{:S(2)}, u32[]{:S(2)}) collective-permute-start(bf16[2,4,512,128]{3,2,1,0:T(8,128)(2,1)S(1)} %pad_maximum_fusion.l0), channel_id=1, source_target_pairs={{0,192},{8,56},{16,208},{24,8},{32,224},{40,24},{48,240},{56,40},{... | collective-permute-start | bytes 3145736 | tf_op jit(solution)/shard_map/ppermute | solution.py:42
  23.1 23.9 %collective-permute-start.8 = (bf16[2,4,512,128]{3,2,1,0:T(8,128)(2,1)S(1)}, bf16[2,4,512,128]{3,2,1,0:T(8,128)(2,1)}, u32[]{:S(2)}, u32[]{:S(2)}) collective-permute-start(bf16[2,4,512,128]{3,2,1,0:T(8,128)(2,1)S(1)} %pad_maximum_fusion.l0), channel_id=1, source_target_pairs={{0,8},{8,0},{16,24},{24,16},{32,40},{40,32},{48,56},{56,48},{64,72... | collective-permute-start | bytes 3145736 | tf_op jit(solution)/shard_map/ppermute | solution.py:42
  35.2 20.2 %collective-permute-start.9 = (bf16[2,4,512,128]{3,2,1,0:T(8,128)(2,1)}, bf16[2,4,512,128]{3,2,1,0:T(8,128)(2,1)}, u32[]{:S(2)}, u32[]{:S(2)}) collective-permute-start(bf16[2,4,512,128]{3,2,1,0:T(8,128)(2,1)} %collective-permute-done.4.u0), channel_id=1, source_target_pairs={{0,8},{8,0},{16,24},{24,16},{32,40},{40,32},{48,56},{56,48},{64,72... | collective-permute-start | bytes 3145736 | tf_op jit(solution)/shard_map/ppermute | solution.py:42
  39.9 7.1 %copy-start.1 = (bf16[2,4,512,128]{3,2,1,0:T(8,128)(2,1)}, bf16[2,4,512,128]{3,2,1,0:T(8,128)(2,1)S(1)}, u32[]{:S(2)}) copy-start(bf16[2,4,512,128]{3,2,1,0:T(8,128)(2,1)S(1)} %collective-permute-done.5.d0.refs_2_) | copy-start | bytes 3145732
  39.9 10.1 %collective-permute-start.6 = (bf16[4,512,128]{2,1,0:T(8,128)(2,1)}, bf16[4,512,128]{2,1,0:T(8,128)(2,1)}, u32[]{:S(2)}, u32[]{:S(2)}) collective-permute-start(bf16[4,512,128]{2,1,0:T(8,128)(2,1)} %slice_bitcast_fusion.1), channel_id=1, source_target_pairs={{0,64},{8,24},{16,80},{24,40},{32,96},{40,56},{48,112},{56,8},{64,... | collective-permute-start | bytes 1572872 | tf_op jit(solution)/shard_map/ppermute | solution.py:42
  41.7 12.5 %collective-permute-start.7 = (bf16[4,512,128]{2,1,0:T(8,128)(2,1)}, bf16[4,512,128]{2,1,0:T(8,128)(2,1)}, u32[]{:S(2)}, u32[]{:S(2)}) collective-permute-start(bf16[4,512,128]{2,1,0:T(8,128)(2,1)} %slice_bitcast_fusion), channel_id=1, source_target_pairs={{0,192},{8,56},{16,208},{24,8},{32,224},{40,24},{48,240},{56,40},{... | collective-permute-start | bytes 1572872 | tf_op jit(solution)/shard_map/ppermute | solution.py:42
  44.4 11.3 %collective-permute-start.10 = (bf16[2,4,512,128]{3,2,1,0:T(8,128)(2,1)S(1)}, bf16[2,4,512,128]{3,2,1,0:T(8,128)(2,1)}, u32[]{:S(2)}, u32[]{:S(2)}) collective-permute-start(bf16[2,4,512,128]{3,2,1,0:T(8,128)(2,1)S(1)} %collective-permute-done.5.d0.refs_2_), channel_id=1, source_target_pairs={{0,8},{8,0},{16,24},{24,16},{32,40},{40,32},{48,56},{56,48},{64,72... | collective-permute-start | bytes 3145736 | tf_op jit(solution)/shard_map/ppermute | solution.py:42
  47.1 31.5 %collective-permute-start.22 = (bf16[512,1024]{1,0:T(8,128)(2,1)}, bf16[512,1024]{1,0:T(8,128)(2,1)}, u32[]{:S(2)}, u32[]{:S(2)}) collective-permute-start(bf16[512,1024]{1,0:T(8,128)(2,1)} %get-tuple-element.13.refs_9_), channel_id=1, source_target_pairs={{0,1},{1,2},{2,3},{3,4},{4,5},{5,6},{6,7},{7,0},{8,9},{9,10},{10,1... | collective-permute-start | bytes 3145736 | tf_op jit(solution)/shard_map/ppermute | solution.py:200
  50.0 28.5 %collective-permute-start.23 = (bf16[512,1024]{1,0:T(8,128)(2,1)}, bf16[512,1024]{1,0:T(8,128)(2,1)}, u32[]{:S(2)}, u32[]{:S(2)}) collective-permute-start(bf16[512,1024]{1,0:T(8,128)(2,1)} %get-tuple-element.14.refs_10_), channel_id=1, source_target_pairs={{0,7},{1,0},{2,1},{3,2},{4,3},{5,4},{6,5},{7,6},{8,15},{9,8},{10,9... | collective-permute-start | bytes 3145736 | tf_op jit(solution)/shard_map/ppermute | solution.py:204
  54.3 2.9 %collective-permute-start.11 = (bf16[4,512,128]{2,1,0:T(8,128)(2,1)}, bf16[4,512,128]{2,1,0:T(8,128)(2,1)S(1)}, u32[]{:S(2)}, u32[]{:S(2)}) collective-permute-start(bf16[4,512,128]{2,1,0:T(8,128)(2,1)} %collective-permute-done.6.fk0), channel_id=1, source_target_pairs={{0,8},{8,0},{16,24},{24,16},{32,40},{40,32},{48,56},{56,48},{64,72... | collective-permute-start | bytes 1572872 | tf_op jit(solution)/shard_map/ppermute | solution.py:42
  55.4 2.5 %collective-permute-start.12 = (bf16[4,512,128]{2,1,0:T(8,128)(2,1)}, bf16[4,512,128]{2,1,0:T(8,128)(2,1)S(1)}, u32[]{:S(2)}, u32[]{:S(2)}) collective-permute-start(bf16[4,512,128]{2,1,0:T(8,128)(2,1)} %collective-permute-done.7.fv0), channel_id=1, source_target_pairs={{0,8},{8,0},{16,24},{24,16},{32,40},{40,32},{48,56},{56,48},{64,72... | collective-permute-start | bytes 1572872 | tf_op jit(solution)/shard_map/ppermute | solution.py:42
  57.9 1.2 copy-start.2
  59.2 1.0 copy-start.7
  78.6 41.2 %collective-permute-start.24 = (bf16[512,1024]{1,0:T(8,128)(2,1)}, bf16[512,1024]{1,0:T(8,128)(2,1)S(1)}, u32[]{:S(2)}, u32[]{:S(2)}) collective-permute-start(bf16[512,1024]{1,0:T(8,128)(2,1)} %get-tuple-element.15.refs_11_), channel_id=1, source_target_pairs={{0,1},{1,2},{2,3},{3,4},{4,5},{5,6},{6,7},{7,0},{8,9},{9,10},{10,1... | collective-permute-start | bytes 3145736 | tf_op jit(solution)/shard_map/ppermute | solution.py:200
  78.7 36.0 %all-to-all-start = ((bf16[8,64,512]{2,1,0:T(8,128)(2,1)}), bf16[8,64,512]{2,1,0:T(8,128)(2,1)}, u32[]{:S(2)}, u32[]{:S(2)}) async-start(bf16[8,64,512]{2,1,0:T(8,128)(2,1)} %attend.1.refs_2_), calls=%async_computation | async-start | bytes 1048576 | tf_op jit(solution)/shard_map/all_to_all | solution.py:290
  82.8 37.7 %collective-permute-start.25 = (bf16[512,1024]{1,0:T(8,128)(2,1)}, bf16[512,1024]{1,0:T(8,128)(2,1)S(1)}, u32[]{:S(2)}, u32[]{:S(2)}) collective-permute-start(bf16[512,1024]{1,0:T(8,128)(2,1)} %get-tuple-element.16.refs_12_), channel_id=1, source_target_pairs={{0,7},{1,0},{2,1},{3,2},{4,3},{5,4},{6,5},{7,6},{8,15},{9,8},{10,9... | collective-permute-start | bytes 3145736 | tf_op jit(solution)/shard_map/ppermute | solution.py:204
  114.7 9.6 %collective-permute-start.13 = (bf16[8,64,512]{2,1,0:T(8,128)(2,1)}, bf16[8,64,512]{2,1,0:T(8,128)(2,1)}, u32[]{:S(2)}, u32[]{:S(2)}) collective-permute-start(bf16[8,64,512]{2,1,0:T(8,128)(2,1)} %all-to-all-done.refs_2_.refs_0_), channel_id=1, source_target_pairs={{0,16},{8,56},{16,0},{24,40},{32,48},{40,24},{48,32},{56,8},{64,80... | collective-permute-start | bytes 1572872 | tf_op jit(solution)/shard_map/ppermute | solution.py:42
  114.9 16.9 %collective-permute-start.14 = (bf16[8,64,512]{2,1,0:T(8,128)(2,1)}, bf16[8,64,512]{2,1,0:T(8,128)(2,1)}, u32[]{:S(2)}, u32[]{:S(2)}) collective-permute-start(bf16[8,64,512]{2,1,0:T(8,128)(2,1)} %all-to-all-done.refs_2_.refs_0_), channel_id=1, source_target_pairs={{0,64},{8,200},{16,80},{24,216},{32,96},{40,232},{48,112},{56,248}... | collective-permute-start | bytes 1572872 | tf_op jit(solution)/shard_map/ppermute | solution.py:42
  119.1 12.7 %collective-permute-start.15 = (bf16[8,64,512]{2,1,0:T(8,128)(2,1)}, bf16[8,64,512]{2,1,0:T(8,128)(2,1)}, u32[]{:S(2)}, u32[]{:S(2)}) collective-permute-start(bf16[8,64,512]{2,1,0:T(8,128)(2,1)} %all-to-all-done.refs_2_.refs_0_), channel_id=1, source_target_pairs={{0,80},{8,248},{16,64},{24,232},{32,112},{40,216},{48,96},{56,200}... | collective-permute-start | bytes 1572872 | tf_op jit(solution)/shard_map/ppermute | solution.py:42
  119.8 1.0 copy-start.3
  119.8 13.3 %collective-permute-start.16 = (bf16[8,64,512]{2,1,0:T(8,128)(2,1)}, bf16[8,64,512]{2,1,0:T(8,128)(2,1)}, u32[]{:S(2)}, u32[]{:S(2)}) collective-permute-start(bf16[8,64,512]{2,1,0:T(8,128)(2,1)} %all-to-all-done.refs_2_.refs_0_), channel_id=1, source_target_pairs={{0,8},{8,0},{16,24},{24,16},{32,40},{40,32},{48,56},{56,48},{64,72... | collective-permute-start | bytes 1572872 | tf_op jit(solution)/shard_map/ppermute | solution.py:42
  120.8 1.0 copy-start.5
  121.7 15.6 %copy-start.4 = (bf16[512,1024]{1,0:T(8,128)(2,1)S(1)}, bf16[512,1024]{1,0:T(8,128)(2,1)}, u32[]{:S(2)}) copy-start(bf16[512,1024]{1,0:T(8,128)(2,1)} %get-tuple-element.17.refs_13_) | copy-start | bytes 3145732
  121.7 15.6 %copy-start.6 = (bf16[512,1024]{1,0:T(8,128)(2,1)S(1)}, bf16[512,1024]{1,0:T(8,128)(2,1)}, u32[]{:S(2)}) copy-start(bf16[512,1024]{1,0:T(8,128)(2,1)} %get-tuple-element.18.refs_14_) | copy-start | bytes 3145732
  123.0 14.1 %collective-permute-start.26 = (bf16[256,1024]{1,0:T(8,128)(2,1)S(1)}, bf16[256,1024]{1,0:T(8,128)(2,1)S(1)}, u32[]{:S(2)}, u32[]{:S(2)}) collective-permute-start(bf16[256,1024]{1,0:T(8,128)(2,1)S(1)} %slice.45), channel_id=1, source_target_pairs={{0,1},{1,2},{2,3},{3,4},{4,5},{5,6},{6,7},{7,0},{8,9},{9,10},{10,1... | collective-permute-start | bytes 1572872 | tf_op jit(solution)/shard_map/ppermute | solution.py:200
  124.3 13.1 %collective-permute-start.27 = (bf16[256,1024]{1,0:T(8,128)(2,1)S(1)}, bf16[256,1024]{1,0:T(8,128)(2,1)S(1)}, u32[]{:S(2)}, u32[]{:S(2)}) collective-permute-start(bf16[256,1024]{1,0:T(8,128)(2,1)S(1)} %slice.46), channel_id=1, source_target_pairs={{0,7},{1,0},{2,1},{3,2},{4,3},{5,4},{6,5},{7,6},{8,15},{9,8},{10,9... | collective-permute-start | bytes 1572872 | tf_op jit(solution)/shard_map/ppermute | solution.py:204
  131.8 5.6 %collective-permute-start.17 = (bf16[8,64,512]{2,1,0:T(8,128)(2,1)}, bf16[8,64,512]{2,1,0:T(8,128)(2,1)S(1)}, u32[]{:S(2)}, u32[]{:S(2)}) collective-permute-start(bf16[8,64,512]{2,1,0:T(8,128)(2,1)} %collective-permute-done.13.refs_1_), channel_id=1, source_target_pairs={{0,8},{8,0},{16,24},{24,16},{32,40},{40,32},{48,56},{56,48},{64,72... | collective-permute-start | bytes 1572872 | tf_op jit(solution)/shard_map/ppermute | solution.py:42
  131.8 5.6 %collective-permute-start.18 = (bf16[8,64,512]{2,1,0:T(8,128)(2,1)}, bf16[8,64,512]{2,1,0:T(8,128)(2,1)S(1)}, u32[]{:S(2)}, u32[]{:S(2)}) collective-permute-start(bf16[8,64,512]{2,1,0:T(8,128)(2,1)} %collective-permute-done.14.refs_2_), channel_id=1, source_target_pairs={{0,8},{8,0},{16,24},{24,16},{32,40},{40,32},{48,56},{56,48},{64,72... | collective-permute-start | bytes 1572872 | tf_op jit(solution)/shard_map/ppermute | solution.py:42
  133.1 4.3 %collective-permute-start.19 = (bf16[8,64,512]{2,1,0:T(8,128)(2,1)}, bf16[8,64,512]{2,1,0:T(8,128)(2,1)S(1)}, u32[]{:S(2)}, u32[]{:S(2)}) collective-permute-start(bf16[8,64,512]{2,1,0:T(8,128)(2,1)} %collective-permute-done.15.refs_3_), channel_id=1, source_target_pairs={{0,8},{8,0},{16,24},{24,16},{32,40},{40,32},{48,56},{56,48},{64,72... | collective-permute-start | bytes 1572872 | tf_op jit(solution)/shard_map/ppermute | solution.py:42
  145.5 3.8 %collective-permute-start.28 = (bf16[4,64,1024]{2,1,0:T(8,128)(2,1)S(1)}, bf16[4,64,1024]{2,1,0:T(8,128)(2,1)S(1)}, u32[]{:S(2)}, u32[]{:S(2)}) collective-permute-start(bf16[4,64,1024]{2,1,0:T(8,128)(2,1)S(1)} %get-tuple-element.20), channel_id=1, source_target_pairs={{0,8},{8,0},{16,24},{24,16},{32,40},{40,32},{48,56},{56,48},{64,72... | collective-permute-start | bytes 1572872 | tf_op jit(solution)/shard_map/ppermute | solution.py:42
  150.2 9.0 %collective-permute-start.30 = (bf16[64,2048]{1,0:T(8,128)(2,1)}, bf16[64,2048]{1,0:T(8,128)(2,1)S(1)}, u32[]{:S(2)}, u32[]{:S(2)}) collective-permute-start(bf16[64,2048]{1,0:T(8,128)(2,1)} %get-tuple-element.28), channel_id=1, source_target_pairs={{0,64},{8,200},{16,80},{24,216},{32,96},{40,232},{48,112},{56,248}... | collective-permute-start | bytes 786440 | tf_op jit(solution)/shard_map/ppermute | solution.py:42
  152.7 8.5 %collective-permute-start.29 = (bf16[64,2048]{1,0:T(8,128)(2,1)S(1)}, bf16[64,2048]{1,0:T(8,128)(2,1)S(1)}, u32[]{:S(2)}, u32[]{:S(2)}) collective-permute-start(bf16[64,2048]{1,0:T(8,128)(2,1)S(1)} %get-tuple-element.27), channel_id=1, source_target_pairs={{0,80},{8,248},{16,64},{24,232},{32,112},{40,216},{48,96},{56,200}... | collective-permute-start | bytes 786440 | tf_op jit(solution)/shard_map/ppermute | solution.py:42
  155.0 6.9 %collective-permute-start.31 = (bf16[64,2048]{1,0:T(8,128)(2,1)S(1)}, bf16[64,2048]{1,0:T(8,128)(2,1)S(1)}, u32[]{:S(2)}, u32[]{:S(2)}) collective-permute-start(bf16[64,2048]{1,0:T(8,128)(2,1)S(1)} %get-tuple-element.26), channel_id=1, source_target_pairs={{0,16},{8,56},{16,0},{24,40},{32,48},{40,24},{48,32},{56,8},{64,80... | collective-permute-start | bytes 786440 | tf_op jit(solution)/shard_map/ppermute | solution.py:42

commit v4 on v3

--- a/solution.py
+++ b/solution.py
@@ -70,7 +70,7 @@
 def attend_kernel(
     slots_ref, vert_ref, diag_ref, q_ref, kpv_ref, kpd_ref,
     l0, u0, d0, fk0, fv0, l1, u1, d1, fk1, fv1,
-    o_ref, kbuf, vbuf, sv_ref, pv_ref, od_ref, tot_ref, sems,
+    o_ref, kbuf, vbuf, sv_ref, sd_ref, pv_ref, pd_ref, tot_ref, sems,
 ):
     heads, rows, width = q_ref.shape
     blocks = rows // BLK
@@ -79,18 +79,18 @@
     for side, (line, up, down, fk, fv) in enumerate(((l0, u0, d0, fk0, fv0), (l1, u1, d1, fk1, fv1))):
         for which, buf in enumerate((kbuf, vbuf)):
             for j, src in enumerate((line, up, down, (fk, fv)[which])):
-                for i in range(4):
-                    piece = src.at[i] if j == 3 else src.at[which, i]
-                    slot = side * 16 + j * 4 + i
-                    copies[which].append(
-                        pltpu.make_async_copy(piece, buf.at[slot], sems.at[which, slot])
+                slot = side * 16 + j * 4
+                copies[which].append(
+                    pltpu.make_async_copy(
+                        src if j == 3 else src.at[which],
+                        buf.at[pl.ds(slot, 4)],
+                        sems.at[which, side * 4 + j],
                     )
+                )
     for c in copies[0] + copies[1]:
         c.start()
     for c in copies[0]:
         c.wait()
-    for c in copies[1]:
-        c.wait()
 
     def tile(buf, block):
         return buf[slots_ref[block // per], pl.ds(pl.multiple_of((block % per) * BLK, BLK), BLK), :]
@@ -98,42 +98,44 @@
     scale = SCALE / math.sqrt(width)
     nt = (((1,), (1,)), ((), ()))
 
-    def one_head(h, carry):
+    def one_head(h):
         verts = [vert_ref[h, c] for c in range(8)]
+        diags = [[diag_ref[h * blocks + b, c] for c in range(8)] for b in range(blocks)]
+        sv, sd, pv, pd, tot = (r.at[h % 2] for r in (sv_ref, sd_ref, pv_ref, pd_ref, tot_ref))
         k_v = jnp.concatenate([tile(kbuf, v) for v in verts], axis=0)
-        sv_ref[...] = lax.dot_general(q_ref[h], k_v, nt, preferred_element_type=jnp.float32)
+        sv[...] = lax.dot_general(q_ref[h], k_v, nt, preferred_element_type=jnp.float32)
+        for b in range(blocks):
+            r = slice(b * BLK, (b + 1) * BLK)
+            k_d = jnp.concatenate([tile(kbuf, v) for v in diags[b]], axis=0)
+            sd[r, :] = lax.dot_general(q_ref[h, r, :], k_d, nt, preferred_element_type=jnp.float32)
         kpv = kpv_ref[h]
         for b in range(blocks):
             r = slice(b * BLK, (b + 1) * BLK)
-            diags = [diag_ref[h * blocks + b, c] for c in range(8)]
-            k_d = jnp.concatenate([tile(kbuf, v) for v in diags], axis=0)
-            s_d = lax.dot_general(q_ref[h, r, :], k_d, nt, preferred_element_type=jnp.float32)
-            s_v = sv_ref[r, :]
             qpos = b * BLK + lax.broadcasted_iota(jnp.int32, (BLK, 1), 0)
-            s_d = jnp.where(kpd_ref[h * blocks + b] <= qpos, s_d, -1e30)
-            s_v = jnp.where(kpv <= qpos, s_v, -1e30)
+            s_d = jnp.where(kpd_ref[h * blocks + b] <= qpos, sd[r, :], -1e30)
+            s_v = jnp.where(kpv <= qpos, sv[r, :], -1e30)
             top = jnp.maximum(
                 jnp.max(s_d, axis=1, keepdims=True), jnp.max(s_v, axis=1, keepdims=True)
             )
             p_d = jnp.exp2((s_d - top) * scale)
             p_v = jnp.exp2((s_v - top) * scale)
-            tot_ref[r, :] = jnp.sum(p_d, axis=1, keepdims=True) + jnp.sum(
-                p_v, axis=1, keepdims=True
-            )
-            pv_ref[r, :] = p_v.astype(jnp.bfloat16)
-            v_d = jnp.concatenate([tile(vbuf, v) for v in diags], axis=0)
-            od_ref[r, :] = jnp.dot(
-                p_d.astype(jnp.bfloat16), v_d, preferred_element_type=jnp.float32
-            )
+            tot[r, :] = jnp.sum(p_d, axis=1, keepdims=True) + jnp.sum(p_v, axis=1, keepdims=True)
+            pv[r, :] = p_v.astype(jnp.bfloat16)
+            pd[r, :] = p_d.astype(jnp.bfloat16)
+        if h == 0:
+            for c in copies[1]:
+                c.wait()
         v_v = jnp.concatenate([tile(vbuf, v) for v in verts], axis=0)
-        o_v = jnp.dot(pv_ref[...], v_v, preferred_element_type=jnp.float32)
-        o = ((o_v + od_ref[...]) / tot_ref[...]).astype(jnp.bfloat16)
-        lanes = pl.ds(pl.multiple_of(h * width, width), width)
+        o_v = jnp.dot(pv[...], v_v, preferred_element_type=jnp.float32)
         for b in range(blocks):
-            o_ref[b, :, lanes] = o[b * BLK : (b + 1) * BLK]
-        return carry
-
-    lax.fori_loop(0, heads, one_head, 0)
+            r = slice(b * BLK, (b + 1) * BLK)
+            v_d = jnp.concatenate([tile(vbuf, v) for v in diags[b]], axis=0)
+            o_d = jnp.dot(pd[r, :], v_d, preferred_element_type=jnp.float32)
+            o = ((o_v[r] + o_d) / tot[r, :]).astype(jnp.bfloat16)
+            o_ref[b, :, h * width : (h + 1) * width] = o
+
+    for h in range(heads):
+        one_head(h)
 
 
 def attend(query, pieces, slots, vertical, slash, counts, seq_index):
@@ -157,7 +159,7 @@
     diag = jnp.maximum(diag, 0).reshape(heads * blocks, 8)
     smem = pl.BlockSpec(memory_space=pltpu.SMEM)
     vmem = pl.BlockSpec(memory_space=pltpu.VMEM)
-    hbm = pl.BlockSpec(memory_space=pl.ANY)
+    hbm = pl.BlockSpec(memory_space=pltpu.HBM)
     f32 = jnp.float32
     return pl.pallas_call(
         attend_kernel,
@@ -167,14 +169,15 @@
         scratch_shapes=[
             pltpu.VMEM((32, rows, width), jnp.bfloat16),
             pltpu.VMEM((32, rows, width), jnp.bfloat16),
-            pltpu.VMEM((rows, 8 * BLK), f32),
-            pltpu.VMEM((rows, 8 * BLK), jnp.bfloat16),
-            pltpu.VMEM((rows, width), f32),
-            pltpu.VMEM((rows, 1), f32),
-            pltpu.SemaphoreType.DMA((2, 32)),
+            pltpu.VMEM((2, rows, 8 * BLK), f32),
+            pltpu.VMEM((2, rows, 8 * BLK), f32),
+            pltpu.VMEM((2, rows, 8 * BLK), jnp.bfloat16),
+            pltpu.VMEM((2, rows, 8 * BLK), jnp.bfloat16),
+            pltpu.VMEM((2, rows, 1), f32),
+            pltpu.SemaphoreType.DMA((2, 8)),
         ],
         compiler_params=pltpu.CompilerParams(vmem_limit_bytes=24 * 2**20),
-        cost_estimate=pl.CostEstimate(flops=2**31, bytes_accessed=48 * 2**20, transcendentals=2**21),
+        cost_estimate=pl.CostEstimate(flops=2**31, bytes_accessed=24 * 2**20, transcendentals=2**21),
         name="attend",
     )(slots, vertical, diag, query, kpv, kpd, *pieces)
 
@@ -185,7 +188,7 @@
 
 def after(arrays, dep):
     count = len(arrays)
-    hbm = pl.BlockSpec(memory_space=pl.ANY)
+    hbm = pl.BlockSpec(memory_space=pltpu.HBM)
     return pl.pallas_call(
         lambda *refs: None,
         out_shape=[jax.ShapeDtypeStruct(a.shape, a.dtype) for a in arrays],
@@ -236,7 +239,7 @@
     n, group, depth = rows[0].shape
     cols = weights[0].shape[1]
     vmem = pl.BlockSpec(memory_space=pltpu.VMEM)
-    hbm = pl.BlockSpec(memory_space=pl.ANY)
+    hbm = pl.BlockSpec(memory_space=pltpu.HBM)
     return pl.pallas_call(
         project_kernel,
         out_shape=[jax.ShapeDtypeStruct((4, group, cols), jnp.bfloat16)] * 2,
@@ -269,14 +272,15 @@
 
     up_a, down_a = send(own, A_UP), send(own, A_DOWN)
     w_u1, w_d1 = up(w0), down(w0)
+    up_a, down_a = after([up_a, down_a], w0)
     far = jnp.stack([send(up_a[0], A_UP), send(down_a[1], A_DOWN)])
     line = jnp.stack([own, up_a, down_a, far], axis=1)
     up_b, down_b = send(line, B_UP), send(line, B_DOWN)
     far_k, far_v = send(up_b[0], B_UP), send(down_b[1], B_DOWN)
-    w_u1, w_d1 = after([w_u1, w_d1], down_b)
-    w_u2, w_d2 = up(w_u1), down(w_d1)
     pieces = [line, up_b, down_b, far_k, far_v]
     pieces += [send(a, SWAP) for a in pieces]
+    w_u1, w_d1 = after([w_u1, w_d1], pieces[5])
+    w_u2, w_d2 = up(w_u1), down(w_d1)
 
     def mine(a):
         return lax.dynamic_slice_in_dim(a, tp_index * heads, heads, 0)

time: 164 us -> 175 us (1.067)
  Pallas kernels: 26.5 us -> 16.5 us
  waiting for transfers between devices: 64.9 us -> 73.4 us
  starting transfers between devices: 54.6 us -> 59.3 us
  local copies, waits for them, and re-layouts: 13.4 us -> 17.8 us
  other arithmetic: 3.48 us -> 6.58 us
    pallas_call x1, Pallas kernels: 18.3 us -> 8.94 us  [attend(): pl.pallas_call(attend_kernel, out_shape=jax.ShapeDtypeStruct((blocks, BLK...]
    ppermute x24, starting transfers between devices: 35.9 us -> 42.7 us  [send(): return lax.ppermute(a, 'seq', pairs)]
    ppermute x24, waiting for transfers between devices: 31.3 us -> 36.3 us  [send(): return lax.ppermute(a, 'seq', pairs)]
    ppermute x4, waiting for transfers between devices: 0.34 us -> 3.79 us  [down(): return lax.ppermute(a, 'tp', ring(lax.axis_size('tp'), -1))]
    unnamed x23 -> x31, local copies, waits for them, and re-layouts: 4.84 us -> 7.06 us
    another operation x2, other arithmetic: 0.16 us -> 2.22 us  [per_device(): line = jnp.stack([own, up_a, down_a, far], axis=1)]
    squeeze x2, local copies, waits for them, and re-layouts: 0.02 us -> 1.92 us  [per_device(): far = jnp.stack([send(up_a[0], A_UP), send(down_a[1], A_DOWN)])]
  transfers between devices with their start and end apart: 33 -> 33, of which waited for: 16 -> 19; matrix products, arithmetic and copies ran while one was open for 6% -> 6% of each run, Pallas kernels for 11% -> 5%
where the time goes in v4:
time: 175 us; the launch traced here: 174 us
  waiting for transfers between devices  73.4 us (42%)
  starting transfers between devices  59.3 us (34%)
  local copies, waits for them, and re-layouts  17.8 us (10%)
  Pallas kernels  16.5 us (9%)
  other arithmetic  6.58 us (4%)
    ppermute x24, starting transfers between devices, send(): return lax.ppermute(a, 'seq', pairs)  42.7 us
    ppermute x24, waiting for transfers between devices, send(): return lax.ppermute(a, 'seq', pairs)  36.3 us
    all_to_all x1, waiting for transfers between devices, per_device(): lax.all_to_all(attended, 'tp', split_axis=0, concat_axis=0, tiled=True)  27.8 us
    ppermute x4, starting transfers between devices, down(): return lax.ppermute(a, 'tp', ring(lax.axis_size('tp'), -1))  11 us
    pallas_call x1, Pallas kernels, attend(): pl.pallas_call(attend_kernel, out_shape=jax.ShapeDtypeStruct((blocks, BLK...  8.94 us
    pallas_call x1, Pallas kernels, project(): pl.pallas_call(project_kernel, out_shape=[jax.ShapeDtypeStruct((4, group,...  7.59 us
    unnamed x31, local copies, waits for them, and re-layouts  7.06 us
    ppermute x4, waiting for transfers between devices, up(): return lax.ppermute(a, 'tp', ring(lax.axis_size('tp'), 1))  5.58 us
  transfers between devices with their start and end apart: 33, of which 19 were waited for; matrix products, arithmetic and copies ran while one was open for 6% of the time, Pallas kernels for 5%

profile of v4, /device:TPU:1, one launch (start us, length us, event | category | flops | bytes accessed | tf_op | source)
XLA Modules:
  0.0 174.0 jit_solution(10290777270211380839)
XLA Ops:
  0.0 1.2 copy-done
  1.2 3.6 %collective-permute-start.1 = (bf16[2,512,128]{2,1,0:T(8,128)(2,1)S(1)}, bf16[2,512,128]{2,1,0:T(8,128)(2,1)S(1)}, u32[]{:S(2)}, u32[]{:S(2)}) collective-permute-start(bf16[2,512,128]{2,1,0:T(8,128)(2,1)S(1)} %fusion.19), channel_id=1, source_target_pairs={{0,48},{8,200},{16,0},{24,216},{32,16},{40,232},{48,32},{56,248},{... | collective-permute-start | bytes 786440 | tf_op jit(solution)/shard_map/ppermute | solution.py:42
  4.9 2.3 %constant_dynamic-slice_fusion.refs_2_.refs_8_ = bf16[512,1024]{1,0:T(8,128)(2,1)} fusion(bf16[512,8192]{1,0:T(8,128)(2,1)} %param.12, s32[]{:T(128)S(6)} %select_n.232), kind=kLoop, calls=%fused_computation.63 | loop fusion | bytes 2097156 | tf_op jit(solution)/shard_map/dynamic_slice | solution.py:271
  7.2 1.1 collective-permute-done.1.refs_1_
  8.2 3.4 %collective-permute-done.refs_0_ = bf16[2,512,128]{2,1,0:T(8,128)(2,1)S(1)} collective-permute-done((bf16[2,512,128]{2,1,0:T(8,128)(2,1)S(1)}, bf16[2,512,128]{2,1,0:T(8,128)(2,1)S(1)}, u32[]{:S(2)}, u32[]{:S(2)}) %collective-permute-start) | collective-permute-done | bytes 262176 | tf_op jit(solution)/shard_map/ppermute | solution.py:42
  14.8 1.1 collective-permute-start.2
  15.8 2.3 %collective-permute-done.3 = bf16[512,128]{1,0:T(8,128)(2,1)S(1)} collective-permute-done((bf16[512,128]{1,0:T(8,128)(2,1)S(1)}, bf16[512,128]{1,0:T(8,128)(2,1)S(1)}, u32[]{:S(2)}, u32[]{:S(2)}) %collective-permute-start.3) | collective-permute-done | bytes 131104 | tf_op jit(solution)/shard_map/ppermute | solution.py:42
  18.2 1.6 collective-permute-done.2
  19.8 2.2 %pad_maximum_fusion.l0 = bf16[2,4,512,128]{3,2,1,0:T(8,128)(2,1)} fusion(bf16[2,1,512,128]{3,2,1,0:T(8,128)(2,1)S(1)} %maximum_bitcast_fusion, bf16[2,1,512,128]{3,2,1,0:T(8,128)(2,1)} %bitcast.47, bf16[2,1,512,128]{3,2,1,0:T(8,128)(2,1)} %bitcast.48, bf16[2,1,512,128]{3,2,1,0:T(8,128)(2,1)S(1)} %constant_dynamic-slice_fusion.1), kind=kLoop, calls=%fused_computation.6 | loop fusion | flops 1572864 | bytes 2097152 | tf_op jit(solution)/shard_map/stack | solution.py:277
  22.0 2.8 %collective-permute-start.5 = (bf16[2,4,512,128]{3,2,1,0:T(8,128)(2,1)}, bf16[2,4,512,128]{3,2,1,0:T(8,128)(2,1)}, u32[]{:S(2)}, u32[]{:S(2)}) collective-permute-start(bf16[2,4,512,128]{3,2,1,0:T(8,128)(2,1)} %pad_maximum_fusion.l0), channel_id=1, source_target_pairs={{0,192},{8,56},{16,208},{24,8},{32,224},{40,24},{48,240},{56,40},{... | collective-permute-start | bytes 3145736 | tf_op jit(solution)/shard_map/ppermute | solution.py:42
  24.8 5.6 %collective-permute-start.21 = (bf16[512,1024]{1,0:T(8,128)(2,1)S(1)}, bf16[512,1024]{1,0:T(8,128)(2,1)}, u32[]{:S(2)}, u32[]{:S(2)}) collective-permute-start(bf16[512,1024]{1,0:T(8,128)(2,1)S(1)} %copy-done.3), channel_id=1, source_target_pairs={{0,7},{1,0},{2,1},{3,2},{4,3},{5,4},{6,5},{7,6},{8,15},{9,8},{10,9... | collective-permute-start | bytes 3145736 | tf_op jit(solution)/shard_map/ppermute | solution.py:207
  30.9 3.6 %collective-permute-start.8 = (bf16[2,4,512,128]{3,2,1,0:T(8,128)(2,1)}, bf16[2,4,512,128]{3,2,1,0:T(8,128)(2,1)S(1)}, u32[]{:S(2)}, u32[]{:S(2)}) collective-permute-start(bf16[2,4,512,128]{3,2,1,0:T(8,128)(2,1)} %pad_maximum_fusion.l0), channel_id=1, source_target_pairs={{0,8},{8,0},{16,24},{24,16},{32,40},{40,32},{48,56},{56,48},{64,72... | collective-permute-start | bytes 3145736 | tf_op jit(solution)/shard_map/ppermute | solution.py:42
  34.4 2.4 %collective-permute-done.5.d0 = bf16[2,4,512,128]{3,2,1,0:T(8,128)(2,1)} collective-permute-done((bf16[2,4,512,128]{3,2,1,0:T(8,128)(2,1)}, bf16[2,4,512,128]{3,2,1,0:T(8,128)(2,1)}, u32[]{:S(2)}, u32[]{:S(2)}) %collective-permute-start.5) | collective-permute-done | bytes 1048608 | tf_op jit(solution)/shard_map/ppermute | solution.py:42
  36.8 1.1 slice_bitcast_fusion
  37.9 3.5 %collective-permute-start.7 = (bf16[4,512,128]{2,1,0:T(8,128)(2,1)S(1)}, bf16[4,512,128]{2,1,0:T(8,128)(2,1)}, u32[]{:S(2)}, u32[]{:S(2)}) collective-permute-start(bf16[4,512,128]{2,1,0:T(8,128)(2,1)S(1)} %slice_bitcast_fusion), channel_id=1, source_target_pairs={{0,192},{8,56},{16,208},{24,8},{32,224},{40,24},{48,240},{56,40},{... | collective-permute-start | bytes 1572872 | tf_op jit(solution)/shard_map/ppermute | solution.py:42
  41.4 4.4 %collective-permute-done.4.u0 = bf16[2,4,512,128]{3,2,1,0:T(8,128)(2,1)} collective-permute-done((bf16[2,4,512,128]{3,2,1,0:T(8,128)(2,1)}, bf16[2,4,512,128]{3,2,1,0:T(8,128)(2,1)}, u32[]{:S(2)}, u32[]{:S(2)}) %collective-permute-start.4) | collective-permute-done | bytes 1048608 | tf_op jit(solution)/shard_map/ppermute | solution.py:42
  45.8 1.9 %slice_bitcast_fusion.1 = bf16[4,512,128]{2,1,0:T(8,128)(2,1)} fusion(bf16[2,4,512,128]{3,2,1,0:T(8,128)(2,1)} %collective-permute-done.4.u0), kind=kLoop, calls=%fused_computation.9 | loop fusion | bytes 1048576 | tf_op jit(solution)/shard_map/squeeze | solution.py:279
  48.6 1.0 collective-permute-done.21.refs_1_
  49.6 4.2 %collective-permute-start.10 = (bf16[2,4,512,128]{3,2,1,0:T(8,128)(2,1)}, bf16[2,4,512,128]{3,2,1,0:T(8,128)(2,1)}, u32[]{:S(2)}, u32[]{:S(2)}) collective-permute-start(bf16[2,4,512,128]{3,2,1,0:T(8,128)(2,1)} %collective-permute-done.5.d0), channel_id=1, source_target_pairs={{0,8},{8,0},{16,24},{24,16},{32,40},{40,32},{48,56},{56,48},{64,72... | collective-permute-start | bytes 3145736 | tf_op jit(solution)/shard_map/ppermute | solution.py:42
  53.7 3.5 %collective-permute-start.9 = (bf16[2,4,512,128]{3,2,1,0:T(8,128)(2,1)}, bf16[2,4,512,128]{3,2,1,0:T(8,128)(2,1)}, u32[]{:S(2)}, u32[]{:S(2)}) collective-permute-start(bf16[2,4,512,128]{3,2,1,0:T(8,128)(2,1)} %collective-permute-done.4.u0), channel_id=1, source_target_pairs={{0,8},{8,0},{16,24},{24,16},{32,40},{40,32},{48,56},{56,48},{64,72... | collective-permute-start | bytes 3145736 | tf_op jit(solution)/shard_map/ppermute | solution.py:42
  58.3 2.7 %collective-permute-start.23 = (bf16[512,1024]{1,0:T(8,128)(2,1)}, bf16[512,1024]{1,0:T(8,128)(2,1)}, u32[]{:S(2)}, u32[]{:S(2)}) collective-permute-start(bf16[512,1024]{1,0:T(8,128)(2,1)} %get-tuple-element.18.refs_10_), channel_id=1, source_target_pairs={{0,7},{1,0},{2,1},{3,2},{4,3},{5,4},{6,5},{7,6},{8,15},{9,8},{10,9... | collective-permute-start | bytes 3145736 | tf_op jit(solution)/shard_map/ppermute | solution.py:207
  62.0 5.1 %collective-permute-start.11 = (bf16[4,512,128]{2,1,0:T(8,128)(2,1)}, bf16[4,512,128]{2,1,0:T(8,128)(2,1)S(1)}, u32[]{:S(2)}, u32[]{:S(2)}) collective-permute-start(bf16[4,512,128]{2,1,0:T(8,128)(2,1)} %collective-permute-done.6.fk0), channel_id=1, source_target_pairs={{0,8},{8,0},{16,24},{24,16},{32,40},{40,32},{48,56},{56,48},{64,72... | collective-permute-start | bytes 1572872 | tf_op jit(solution)/shard_map/ppermute | solution.py:42
  67.4 1.6 collective-permute-done.11.fk1
  68.9 1.2 copy-done.2
  70.2 1.0 copy-done.8
  71.2 8.9 %attend.1.refs_2_ = bf16[8,64,512]{2,1,0:T(8,128)(2,1)} custom-call(s32[32]{0:T(128)S(1)} %fusion.11.slots_ref, s32[4,8]{1,0:T(4,128)S(1)} %copy.26.vert_ref, s32[32,8]{1,0:T(8,128)S(1)} %fusion.7.diag_ref, bf16[4,512,128]{2,1,0:T(8,128)(2,1)S(1)} %copy-done.8, s32[4,1,512]{2,1,0:T(1,128)S(1)} %add_select_fusion.1.kpv_ref, ...), custom_call_target="tpu_custom_call" | custom-call | flops 2147483648 | bytes 25165824 | tf_op jit(solution)/shard_map/attend/pallas_call | solution.py:164
  80.1 3.8 %collective-permute-done.22.refs_0_ = bf16[512,1024]{1,0:T(8,128)(2,1)S(1)} collective-permute-done((bf16[512,1024]{1,0:T(8,128)(2,1)}, bf16[512,1024]{1,0:T(8,128)(2,1)S(1)}, u32[]{:S(2)}, u32[]{:S(2)}) %collective-permute-start.22) | collective-permute-done | bytes 1048608 | tf_op jit(solution)/shard_map/ppermute | solution.py:203
  84.9 4.1 %all-to-all-start = ((bf16[8,64,512]{2,1,0:T(8,128)(2,1)}), bf16[8,64,512]{2,1,0:T(8,128)(2,1)}, u32[]{:S(2)}, u32[]{:S(2)}) async-start(bf16[8,64,512]{2,1,0:T(8,128)(2,1)} %attend.1.refs_2_), calls=%async_computation | async-start | bytes 1048576 | tf_op jit(solution)/shard_map/all_to_all | solution.py:294
  89.1 2.7 %collective-permute-start.25 = (bf16[512,1024]{1,0:T(8,128)(2,1)}, bf16[512,1024]{1,0:T(8,128)(2,1)}, u32[]{:S(2)}, u32[]{:S(2)}) collective-permute-start(bf16[512,1024]{1,0:T(8,128)(2,1)} %get-tuple-element.20.refs_12_), channel_id=1, source_target_pairs={{0,7},{1,0},{2,1},{3,2},{4,3},{5,4},{6,5},{7,6},{8,15},{9,8},{10,9... | collective-permute-start | bytes 3145736 | tf_op jit(solution)/shard_map/ppermute | solution.py:207
  91.8 27.8 %all-to-all-done.refs_2_.refs_0_ = bf16[8,64,512]{2,1,0:T(8,128)(2,1)} async-done(((bf16[8,64,512]{2,1,0:T(8,128)(2,1)}), bf16[8,64,512]{2,1,0:T(8,128)(2,1)}, u32[]{:S(2)}, u32[]{:S(2)}) %all-to-all-start) | async-done | bytes 524320 | tf_op jit(solution)/shard_map/all_to_all | solution.py:294
  119.6 3.7 %collective-permute-start.16 = (bf16[8,64,512]{2,1,0:T(8,128)(2,1)}, bf16[8,64,512]{2,1,0:T(8,128)(2,1)}, u32[]{:S(2)}, u32[]{:S(2)}) collective-permute-start(bf16[8,64,512]{2,1,0:T(8,128)(2,1)} %all-to-all-done.refs_2_.refs_0_), channel_id=1, source_target_pairs={{0,8},{8,0},{16,24},{24,16},{32,40},{40,32},{48,56},{56,48},{64,72... | collective-permute-start | bytes 1572872 | tf_op jit(solution)/shard_map/ppermute | solution.py:42
  123.3 1.6 collective-permute-start.15
  124.8 1.1 collective-permute-start.14
  125.9 2.4 %collective-permute-start.13 = (bf16[8,64,512]{2,1,0:T(8,128)(2,1)}, bf16[8,64,512]{2,1,0:T(8,128)(2,1)}, u32[]{:S(2)}, u32[]{:S(2)}) collective-permute-start(bf16[8,64,512]{2,1,0:T(8,128)(2,1)} %all-to-all-done.refs_2_.refs_0_), channel_id=1, source_target_pairs={{0,16},{8,56},{16,0},{24,40},{32,48},{40,24},{48,32},{56,8},{64,80... | collective-permute-start | bytes 1572872 | tf_op jit(solution)/shard_map/ppermute | solution.py:42
  128.4 1.2 slice.45
  129.6 1.1 slice.46
  130.8 1.4 collective-permute-start.26
  132.2 2.8 %collective-permute-done.15.refs_3_ = bf16[8,64,512]{2,1,0:T(8,128)(2,1)} collective-permute-done((bf16[8,64,512]{2,1,0:T(8,128)(2,1)}, bf16[8,64,512]{2,1,0:T(8,128)(2,1)}, u32[]{:S(2)}, u32[]{:S(2)}) %collective-permute-start.15) | collective-permute-done | bytes 524320 | tf_op jit(solution)/shard_map/ppermute | solution.py:42
  135.0 5.2 %collective-permute-done.14.refs_2_ = bf16[8,64,512]{2,1,0:T(8,128)(2,1)} collective-permute-done((bf16[8,64,512]{2,1,0:T(8,128)(2,1)}, bf16[8,64,512]{2,1,0:T(8,128)(2,1)}, u32[]{:S(2)}, u32[]{:S(2)}) %collective-permute-start.14) | collective-permute-done | bytes 524320 | tf_op jit(solution)/shard_map/ppermute | solution.py:42
  140.8 2.8 %collective-permute-done.27.refs_16_ = bf16[256,1024]{1,0:T(8,128)(2,1)S(1)} collective-permute-done((bf16[256,1024]{1,0:T(8,128)(2,1)S(1)}, bf16[256,1024]{1,0:T(8,128)(2,1)S(1)}, u32[]{:S(2)}, u32[]{:S(2)}) %collective-permute-start.27) | collective-permute-done | bytes 524320 | tf_op jit(solution)/shard_map/ppermute | solution.py:207
  143.6 1.8 %collective-permute-done.26.refs_15_ = bf16[256,1024]{1,0:T(8,128)(2,1)S(1)} collective-permute-done((bf16[256,1024]{1,0:T(8,128)(2,1)S(1)}, bf16[256,1024]{1,0:T(8,128)(2,1)S(1)}, u32[]{:S(2)}, u32[]{:S(2)}) %collective-permute-start.26) | collective-permute-done | bytes 524320 | tf_op jit(solution)/shard_map/ppermute | solution.py:203
  145.4 7.6 %project.1 = (bf16[4,64,1024]{2,1,0:T(8,128)(2,1)S(1)}, bf16[4,64,1024]{2,1,0:T(8,128)(2,1)S(1)}) custom-call(s32[2]{0:T(128)S(1)} %pad_add_fusion.place_ref, bf16[8,64,512]{2,1,0:T(8,128)(2,1)} %all-to-all-done.refs_2_.refs_0_, bf16[8,64,512]{2,1,0:T(8,128)(2,1)} %collective-permute-done.13.refs_1_, bf16[8,64,512]{2,1,0:T(8,128)(2,1)} %collective-permute-done.14.refs_2_, ...), custom_call_target="tpu_custom_call" | custom-call | flops 4294967296 | bytes 16777216 | tf_op jit(solution)/shard_map/project/pallas_call | solution.py:243
  153.1 1.9 %collective-permute-done.28 = bf16[4,64,1024]{2,1,0:T(8,128)(2,1)S(1)} collective-permute-done((bf16[4,64,1024]{2,1,0:T(8,128)(2,1)S(1)}, bf16[4,64,1024]{2,1,0:T(8,128)(2,1)S(1)}, u32[]{:S(2)}, u32[]{:S(2)}) %collective-permute-start.28) | collective-permute-done | bytes 524320 | tf_op jit(solution)/shard_map/ppermute | solution.py:42
  155.8 1.1 broadcast_select_fusion
  157.9 5.6 %collective-permute-start.29 = (bf16[64,2048]{1,0:T(8,128)(2,1)S(1)}, bf16[64,2048]{1,0:T(8,128)(2,1)S(1)}, u32[]{:S(2)}, u32[]{:S(2)}) collective-permute-start(bf16[64,2048]{1,0:T(8,128)(2,1)S(1)} %get-tuple-element.31), channel_id=1, source_target_pairs={{0,80},{8,248},{16,64},{24,232},{32,112},{40,216},{48,96},{56,200}... | collective-permute-start | bytes 786440 | tf_op jit(solution)/shard_map/ppermute | solution.py:42
  164.4 5.9 %collective-permute-done.29 = bf16[64,2048]{1,0:T(8,128)(2,1)S(1)} collective-permute-done((bf16[64,2048]{1,0:T(8,128)(2,1)S(1)}, bf16[64,2048]{1,0:T(8,128)(2,1)S(1)}, u32[]{:S(2)}, u32[]{:S(2)}) %collective-permute-start.29) | collective-permute-done | bytes 262176 | tf_op jit(solution)/shard_map/ppermute | solution.py:42
  170.3 2.4 %collective-permute-done.30 = bf16[64,2048]{1,0:T(8,128)(2,1)S(1)} collective-permute-done((bf16[64,2048]{1,0:T(8,128)(2,1)S(1)}, bf16[64,2048]{1,0:T(8,128)(2,1)S(1)}, u32[]{:S(2)}, u32[]{:S(2)}) %collective-permute-start.30) | collective-permute-done | bytes 262176 | tf_op jit(solution)/shard_map/ppermute | solution.py:42
  172.9 1.0 pad_maximum_fusion.1
  (99 shorter events, 11.4 us)
Async XLA Ops:
  0.0 1.2 copy-start
  1.2 7.0 %collective-permute-start.1 = (bf16[2,512,128]{2,1,0:T(8,128)(2,1)S(1)}, bf16[2,512,128]{2,1,0:T(8,128)(2,1)S(1)}, u32[]{:S(2)}, u32[]{:S(2)}) collective-permute-start(bf16[2,512,128]{2,1,0:T(8,128)(2,1)S(1)} %fusion.19), channel_id=1, source_target_pairs={{0,48},{8,200},{16,0},{24,216},{32,16},{40,232},{48,32},{56,248},{... | collective-permute-start | bytes 786440 | tf_op jit(solution)/shard_map/ppermute | solution.py:42
  4.9 6.7 %collective-permute-start = (bf16[2,512,128]{2,1,0:T(8,128)(2,1)S(1)}, bf16[2,512,128]{2,1,0:T(8,128)(2,1)S(1)}, u32[]{:S(2)}, u32[]{:S(2)}) collective-permute-start(bf16[2,512,128]{2,1,0:T(8,128)(2,1)S(1)} %fusion.19), channel_id=1, source_target_pairs={{0,16},{8,72},{16,32},{24,88},{32,48},{40,104},{48,0},{56,120},{64... | collective-permute-start | bytes 786440 | tf_op jit(solution)/shard_map/ppermute | solution.py:42
  8.2 3.4 %copy-start.9 = (bf16[2,512,128]{2,1,0:T(8,128)(2,1)}, bf16[2,512,128]{2,1,0:T(8,128)(2,1)S(1)}, u32[]{:S(2)}) copy-start(bf16[2,512,128]{2,1,0:T(8,128)(2,1)S(1)} %collective-permute-done.1.refs_1_) | copy-start | bytes 786436
  11.6 0.7 copy-start.10
  12.3 12.4 %copy-start.3 = (bf16[512,1024]{1,0:T(8,128)(2,1)S(1)}, bf16[512,1024]{1,0:T(8,128)(2,1)}, u32[]{:S(2)}) copy-start(bf16[512,1024]{1,0:T(8,128)(2,1)} %constant_dynamic-slice_fusion.refs_2_.refs_8_) | copy-start | bytes 3145732
  12.3 18.0 %copy-start.12 = (s32[32,8]{0,1:T(8,128)S(1)}, s32[32,8]{0,1:T(8,128)}, u32[]{:S(2)}) copy-start(s32[32,8]{0,1:T(8,128)} %param.9) | copy-start | bytes 3076
  12.3 18.2 %copy-start.13 = (s32[32,8]{0,1:T(8,128)S(1)}, s32[32,8]{0,1:T(8,128)}, u32[]{:S(2)}) copy-start(s32[32,8]{0,1:T(8,128)} %param.10) | copy-start | bytes 3076
  12.3 18.4 %copy-start.14 = (s32[32,2]{0,1:T(2,128)S(1)}, s32[32,2]{0,1:T(2,128)}, u32[]{:S(2)}) copy-start(s32[32,2]{0,1:T(2,128)} %param.11) | copy-start | bytes 772
  14.3 3.9 %collective-permute-start.3 = (bf16[512,128]{1,0:T(8,128)(2,1)S(1)}, bf16[512,128]{1,0:T(8,128)(2,1)S(1)}, u32[]{:S(2)}, u32[]{:S(2)}) collective-permute-start(bf16[512,128]{1,0:T(8,128)(2,1)S(1)} %slice_bitcast_fusion.2), channel_id=1, source_target_pairs={{0,48},{8,200},{16,0},{24,216},{32,16},{40,232},{48,32},{56,248},{... | collective-permute-start | bytes 393224 | tf_op jit(solution)/shard_map/ppermute | solution.py:42
  14.8 5.0 %collective-permute-start.2 = (bf16[512,128]{1,0:T(8,128)(2,1)S(1)}, bf16[512,128]{1,0:T(8,128)(2,1)S(1)}, u32[]{:S(2)}, u32[]{:S(2)}) collective-permute-start(bf16[512,128]{1,0:T(8,128)(2,1)S(1)} %slice_bitcast_fusion.3), channel_id=1, source_target_pairs={{0,16},{8,72},{16,32},{24,88},{32,48},{40,104},{48,0},{56,120},{64... | collective-permute-start | bytes 393224 | tf_op jit(solution)/shard_map/ppermute | solution.py:42
  22.0 14.8 %collective-permute-start.5 = (bf16[2,4,512,128]{3,2,1,0:T(8,128)(2,1)}, bf16[2,4,512,128]{3,2,1,0:T(8,128)(2,1)}, u32[]{:S(2)}, u32[]{:S(2)}) collective-permute-start(bf16[2,4,512,128]{3,2,1,0:T(8,128)(2,1)} %pad_maximum_fusion.l0), channel_id=1, source_target_pairs={{0,192},{8,56},{16,208},{24,8},{32,224},{40,24},{48,240},{56,40},{... | collective-permute-start | bytes 3145736 | tf_op jit(solution)/shard_map/ppermute | solution.py:42
  24.8 24.8 %collective-permute-start.21 = (bf16[512,1024]{1,0:T(8,128)(2,1)S(1)}, bf16[512,1024]{1,0:T(8,128)(2,1)}, u32[]{:S(2)}, u32[]{:S(2)}) collective-permute-start(bf16[512,1024]{1,0:T(8,128)(2,1)S(1)} %copy-done.3), channel_id=1, source_target_pairs={{0,7},{1,0},{2,1},{3,2},{4,3},{5,4},{6,5},{7,6},{8,15},{9,8},{10,9... | collective-permute-start | bytes 3145736 | tf_op jit(solution)/shard_map/ppermute | solution.py:207
  30.4 23.4 %collective-permute-start.20 = (bf16[512,1024]{1,0:T(8,128)(2,1)S(1)}, bf16[512,1024]{1,0:T(8,128)(2,1)}, u32[]{:S(2)}, u32[]{:S(2)}) collective-permute-start(bf16[512,1024]{1,0:T(8,128)(2,1)S(1)} %copy-done.3), channel_id=1, source_target_pairs={{0,1},{1,2},{2,3},{3,4},{4,5},{5,6},{6,7},{7,0},{8,9},{9,10},{10,1... | collective-permute-start | bytes 3145736 | tf_op jit(solution)/shard_map/ppermute | solution.py:203
  30.4 15.5 %collective-permute-start.4 = (bf16[2,4,512,128]{3,2,1,0:T(8,128)(2,1)}, bf16[2,4,512,128]{3,2,1,0:T(8,128)(2,1)}, u32[]{:S(2)}, u32[]{:S(2)}) collective-permute-start(bf16[2,4,512,128]{3,2,1,0:T(8,128)(2,1)} %pad_maximum_fusion.l0), channel_id=1, source_target_pairs={{0,64},{8,24},{16,80},{24,40},{32,96},{40,56},{48,112},{56,8},{64,... | collective-permute-start | bytes 3145736 | tf_op jit(solution)/shard_map/ppermute | solution.py:42
  30.9 26.5 %collective-permute-start.8 = (bf16[2,4,512,128]{3,2,1,0:T(8,128)(2,1)}, bf16[2,4,512,128]{3,2,1,0:T(8,128)(2,1)S(1)}, u32[]{:S(2)}, u32[]{:S(2)}) collective-permute-start(bf16[2,4,512,128]{3,2,1,0:T(8,128)(2,1)} %pad_maximum_fusion.l0), channel_id=1, source_target_pairs={{0,8},{8,0},{16,24},{24,16},{32,40},{40,32},{48,56},{56,48},{64,72... | collective-permute-start | bytes 3145736 | tf_op jit(solution)/shard_map/ppermute | solution.py:42
  37.9 19.3 %collective-permute-start.7 = (bf16[4,512,128]{2,1,0:T(8,128)(2,1)S(1)}, bf16[4,512,128]{2,1,0:T(8,128)(2,1)}, u32[]{:S(2)}, u32[]{:S(2)}) collective-permute-start(bf16[4,512,128]{2,1,0:T(8,128)(2,1)S(1)} %slice_bitcast_fusion), channel_id=1, source_target_pairs={{0,192},{8,56},{16,208},{24,8},{32,224},{40,24},{48,240},{56,40},{... | collective-permute-start | bytes 1572872 | tf_op jit(solution)/shard_map/ppermute | solution.py:42
  47.8 10.5 %collective-permute-start.6 = (bf16[4,512,128]{2,1,0:T(8,128)(2,1)}, bf16[4,512,128]{2,1,0:T(8,128)(2,1)}, u32[]{:S(2)}, u32[]{:S(2)}) collective-permute-start(bf16[4,512,128]{2,1,0:T(8,128)(2,1)} %slice_bitcast_fusion.1), channel_id=1, source_target_pairs={{0,64},{8,24},{16,80},{24,40},{32,96},{40,56},{48,112},{56,8},{64,... | collective-permute-start | bytes 1572872 | tf_op jit(solution)/shard_map/ppermute | solution.py:42
  49.6 17.8 %collective-permute-start.10 = (bf16[2,4,512,128]{3,2,1,0:T(8,128)(2,1)}, bf16[2,4,512,128]{3,2,1,0:T(8,128)(2,1)}, u32[]{:S(2)}, u32[]{:S(2)}) collective-permute-start(bf16[2,4,512,128]{3,2,1,0:T(8,128)(2,1)} %collective-permute-done.5.d0), channel_id=1, source_target_pairs={{0,8},{8,0},{16,24},{24,16},{32,40},{40,32},{48,56},{56,48},{64,72... | collective-permute-start | bytes 3145736 | tf_op jit(solution)/shard_map/ppermute | solution.py:42
  53.7 15.2 %collective-permute-start.9 = (bf16[2,4,512,128]{3,2,1,0:T(8,128)(2,1)}, bf16[2,4,512,128]{3,2,1,0:T(8,128)(2,1)}, u32[]{:S(2)}, u32[]{:S(2)}) collective-permute-start(bf16[2,4,512,128]{3,2,1,0:T(8,128)(2,1)} %collective-permute-done.4.u0), channel_id=1, source_target_pairs={{0,8},{8,0},{16,24},{24,16},{32,40},{40,32},{48,56},{56,48},{64,72... | collective-permute-start | bytes 3145736 | tf_op jit(solution)/shard_map/ppermute | solution.py:42
  57.3 4.8 %collective-permute-start.12 = (bf16[4,512,128]{2,1,0:T(8,128)(2,1)}, bf16[4,512,128]{2,1,0:T(8,128)(2,1)}, u32[]{:S(2)}, u32[]{:S(2)}) collective-permute-start(bf16[4,512,128]{2,1,0:T(8,128)(2,1)} %collective-permute-done.7.fv0), channel_id=1, source_target_pairs={{0,8},{8,0},{16,24},{24,16},{32,40},{40,32},{48,56},{56,48},{64,72... | collective-permute-start | bytes 1572872 | tf_op jit(solution)/shard_map/ppermute | solution.py:42
  57.3 1.0 copy-start.1
  58.3 25.6 %collective-permute-start.22 = (bf16[512,1024]{1,0:T(8,128)(2,1)}, bf16[512,1024]{1,0:T(8,128)(2,1)S(1)}, u32[]{:S(2)}, u32[]{:S(2)}) collective-permute-start(bf16[512,1024]{1,0:T(8,128)(2,1)} %get-tuple-element.17.refs_9_), channel_id=1, source_target_pairs={{0,1},{1,2},{2,3},{3,4},{4,5},{5,6},{6,7},{7,0},{8,9},{9,10},{10,1... | collective-permute-start | bytes 3145736 | tf_op jit(solution)/shard_map/ppermute | solution.py:203
  58.3 25.6 %collective-permute-start.23 = (bf16[512,1024]{1,0:T(8,128)(2,1)}, bf16[512,1024]{1,0:T(8,128)(2,1)}, u32[]{:S(2)}, u32[]{:S(2)}) collective-permute-start(bf16[512,1024]{1,0:T(8,128)(2,1)} %get-tuple-element.18.refs_10_), channel_id=1, source_target_pairs={{0,7},{1,0},{2,1},{3,2},{4,3},{5,4},{6,5},{7,6},{8,15},{9,8},{10,9... | collective-permute-start | bytes 3145736 | tf_op jit(solution)/shard_map/ppermute | solution.py:207
  62.0 6.9 %collective-permute-start.11 = (bf16[4,512,128]{2,1,0:T(8,128)(2,1)}, bf16[4,512,128]{2,1,0:T(8,128)(2,1)S(1)}, u32[]{:S(2)}, u32[]{:S(2)}) collective-permute-start(bf16[4,512,128]{2,1,0:T(8,128)(2,1)} %collective-permute-done.6.fk0), channel_id=1, source_target_pairs={{0,8},{8,0},{16,24},{24,16},{32,40},{40,32},{48,56},{56,48},{64,72... | collective-permute-start | bytes 1572872 | tf_op jit(solution)/shard_map/ppermute | solution.py:42
  68.9 1.2 copy-start.2
  70.2 1.0 copy-start.8
  83.9 1.0 copy-start.6
  84.9 41.0 %collective-permute-start.24 = (bf16[512,1024]{1,0:T(8,128)(2,1)}, bf16[512,1024]{1,0:T(8,128)(2,1)S(1)}, u32[]{:S(2)}, u32[]{:S(2)}) collective-permute-start(bf16[512,1024]{1,0:T(8,128)(2,1)} %get-tuple-element.19.refs_11_), channel_id=1, source_target_pairs={{0,1},{1,2},{2,3},{3,4},{4,5},{5,6},{6,7},{7,0},{8,9},{9,10},{10,1... | collective-permute-start | bytes 3145736 | tf_op jit(solution)/shard_map/ppermute | solution.py:203
  84.9 34.6 %all-to-all-start = ((bf16[8,64,512]{2,1,0:T(8,128)(2,1)}), bf16[8,64,512]{2,1,0:T(8,128)(2,1)}, u32[]{:S(2)}, u32[]{:S(2)}) async-start(bf16[8,64,512]{2,1,0:T(8,128)(2,1)} %attend.1.refs_2_), calls=%async_computation | async-start | bytes 1048576 | tf_op jit(solution)/shard_map/all_to_all | solution.py:294
  89.1 39.3 %collective-permute-start.25 = (bf16[512,1024]{1,0:T(8,128)(2,1)}, bf16[512,1024]{1,0:T(8,128)(2,1)}, u32[]{:S(2)}, u32[]{:S(2)}) collective-permute-start(bf16[512,1024]{1,0:T(8,128)(2,1)} %get-tuple-element.20.refs_12_), channel_id=1, source_target_pairs={{0,7},{1,0},{2,1},{3,2},{4,3},{5,4},{6,5},{7,6},{8,15},{9,8},{10,9... | collective-permute-start | bytes 3145736 | tf_op jit(solution)/shard_map/ppermute | solution.py:207
  119.6 11.2 %collective-permute-start.16 = (bf16[8,64,512]{2,1,0:T(8,128)(2,1)}, bf16[8,64,512]{2,1,0:T(8,128)(2,1)}, u32[]{:S(2)}, u32[]{:S(2)}) collective-permute-start(bf16[8,64,512]{2,1,0:T(8,128)(2,1)} %all-to-all-done.refs_2_.refs_0_), channel_id=1, source_target_pairs={{0,8},{8,0},{16,24},{24,16},{32,40},{40,32},{48,56},{56,48},{64,72... | collective-permute-start | bytes 1572872 | tf_op jit(solution)/shard_map/ppermute | solution.py:42
  123.3 11.8 %collective-permute-start.15 = (bf16[8,64,512]{2,1,0:T(8,128)(2,1)}, bf16[8,64,512]{2,1,0:T(8,128)(2,1)}, u32[]{:S(2)}, u32[]{:S(2)}) collective-permute-start(bf16[8,64,512]{2,1,0:T(8,128)(2,1)} %all-to-all-done.refs_2_.refs_0_), channel_id=1, source_target_pairs={{0,80},{8,248},{16,64},{24,232},{32,112},{40,216},{48,96},{56,200}... | collective-permute-start | bytes 1572872 | tf_op jit(solution)/shard_map/ppermute | solution.py:42
  124.8 15.4 %collective-permute-start.14 = (bf16[8,64,512]{2,1,0:T(8,128)(2,1)}, bf16[8,64,512]{2,1,0:T(8,128)(2,1)}, u32[]{:S(2)}, u32[]{:S(2)}) collective-permute-start(bf16[8,64,512]{2,1,0:T(8,128)(2,1)} %all-to-all-done.refs_2_.refs_0_), channel_id=1, source_target_pairs={{0,64},{8,200},{16,80},{24,216},{32,96},{40,232},{48,112},{56,248}... | collective-permute-start | bytes 1572872 | tf_op jit(solution)/shard_map/ppermute | solution.py:42
  125.9 2.4 %copy-start.4 = (bf16[512,1024]{1,0:T(8,128)(2,1)}, bf16[512,1024]{1,0:T(8,128)(2,1)S(1)}, u32[]{:S(2)}) copy-start(bf16[512,1024]{1,0:T(8,128)(2,1)S(1)} %collective-permute-done.24.refs_0_) | copy-start | bytes 3145732
  125.9 14.6 %collective-permute-start.13 = (bf16[8,64,512]{2,1,0:T(8,128)(2,1)}, bf16[8,64,512]{2,1,0:T(8,128)(2,1)}, u32[]{:S(2)}, u32[]{:S(2)}) collective-permute-start(bf16[8,64,512]{2,1,0:T(8,128)(2,1)} %all-to-all-done.refs_2_.refs_0_), channel_id=1, source_target_pairs={{0,16},{8,56},{16,0},{24,40},{32,48},{40,24},{48,32},{56,8},{64,80... | collective-permute-start | bytes 1572872 | tf_op jit(solution)/shard_map/ppermute | solution.py:42
  128.3 17.0 %copy-start.5 = (bf16[512,1024]{1,0:T(8,128)(2,1)S(1)}, bf16[512,1024]{1,0:T(8,128)(2,1)}, u32[]{:S(2)}) copy-start(bf16[512,1024]{1,0:T(8,128)(2,1)} %get-tuple-element.21.refs_13_) | copy-start | bytes 3145732
  128.3 17.0 %copy-start.7 = (bf16[512,1024]{1,0:T(8,128)(2,1)S(1)}, bf16[512,1024]{1,0:T(8,128)(2,1)}, u32[]{:S(2)}) copy-start(bf16[512,1024]{1,0:T(8,128)(2,1)} %get-tuple-element.19.refs_11_) | copy-start | bytes 3145732
  130.7 12.9 %collective-permute-start.27 = (bf16[256,1024]{1,0:T(8,128)(2,1)S(1)}, bf16[256,1024]{1,0:T(8,128)(2,1)S(1)}, u32[]{:S(2)}, u32[]{:S(2)}) collective-permute-start(bf16[256,1024]{1,0:T(8,128)(2,1)S(1)} %slice.46), channel_id=1, source_target_pairs={{0,7},{1,0},{2,1},{3,2},{4,3},{5,4},{6,5},{7,6},{8,15},{9,8},{10,9... | collective-permute-start | bytes 1572872 | tf_op jit(solution)/shard_map/ppermute | solution.py:207
  130.8 14.6 %collective-permute-start.26 = (bf16[256,1024]{1,0:T(8,128)(2,1)S(1)}, bf16[256,1024]{1,0:T(8,128)(2,1)S(1)}, u32[]{:S(2)}, u32[]{:S(2)}) collective-permute-start(bf16[256,1024]{1,0:T(8,128)(2,1)S(1)} %slice.45), channel_id=1, source_target_pairs={{0,1},{1,2},{2,3},{3,4},{4,5},{5,6},{6,7},{7,0},{8,9},{9,10},{10,1... | collective-permute-start | bytes 1572872 | tf_op jit(solution)/shard_map/ppermute | solution.py:203
  135.0 10.3 %collective-permute-start.19 = (bf16[8,64,512]{2,1,0:T(8,128)(2,1)}, bf16[8,64,512]{2,1,0:T(8,128)(2,1)S(1)}, u32[]{:S(2)}, u32[]{:S(2)}) collective-permute-start(bf16[8,64,512]{2,1,0:T(8,128)(2,1)} %collective-permute-done.15.refs_3_), channel_id=1, source_target_pairs={{0,8},{8,0},{16,24},{24,16},{32,40},{40,32},{48,56},{56,48},{64,72... | collective-permute-start | bytes 1572872 | tf_op jit(solution)/shard_map/ppermute | solution.py:42
  140.2 5.1 %collective-permute-start.18 = (bf16[8,64,512]{2,1,0:T(8,128)(2,1)}, bf16[8,64,512]{2,1,0:T(8,128)(2,1)S(1)}, u32[]{:S(2)}, u32[]{:S(2)}) collective-permute-start(bf16[8,64,512]{2,1,0:T(8,128)(2,1)} %collective-permute-done.14.refs_2_), channel_id=1, source_target_pairs={{0,8},{8,0},{16,24},{24,16},{32,40},{40,32},{48,56},{56,48},{64,72... | collective-permute-start | bytes 1572872 | tf_op jit(solution)/shard_map/ppermute | solution.py:42
  140.5 4.8 %collective-permute-start.17 = (bf16[8,64,512]{2,1,0:T(8,128)(2,1)}, bf16[8,64,512]{2,1,0:T(8,128)(2,1)S(1)}, u32[]{:S(2)}, u32[]{:S(2)}) collective-permute-start(bf16[8,64,512]{2,1,0:T(8,128)(2,1)} %collective-permute-done.13.refs_1_), channel_id=1, source_target_pairs={{0,8},{8,0},{16,24},{24,16},{32,40},{40,32},{48,56},{56,48},{64,72... | collective-permute-start | bytes 1572872 | tf_op jit(solution)/shard_map/ppermute | solution.py:42
  153.0 2.0 %collective-permute-start.28 = (bf16[4,64,1024]{2,1,0:T(8,128)(2,1)S(1)}, bf16[4,64,1024]{2,1,0:T(8,128)(2,1)S(1)}, u32[]{:S(2)}, u32[]{:S(2)}) collective-permute-start(bf16[4,64,1024]{2,1,0:T(8,128)(2,1)S(1)} %get-tuple-element.24), channel_id=1, source_target_pairs={{0,8},{8,0},{16,24},{24,16},{32,40},{40,32},{48,56},{56,48},{64,72... | collective-permute-start | bytes 1572872 | tf_op jit(solution)/shard_map/ppermute | solution.py:42
  155.0 0.8 copy-start.11
  157.6 6.8 %collective-permute-start.31 = (bf16[64,2048]{1,0:T(8,128)(2,1)}, bf16[64,2048]{1,0:T(8,128)(2,1)S(1)}, u32[]{:S(2)}, u32[]{:S(2)}) collective-permute-start(bf16[64,2048]{1,0:T(8,128)(2,1)} %get-tuple-element.30), channel_id=1, source_target_pairs={{0,16},{8,56},{16,0},{24,40},{32,48},{40,24},{48,32},{56,8},{64,80... | collective-permute-start | bytes 786440 | tf_op jit(solution)/shard_map/ppermute | solution.py:42
  157.9 12.4 %collective-permute-start.29 = (bf16[64,2048]{1,0:T(8,128)(2,1)S(1)}, bf16[64,2048]{1,0:T(8,128)(2,1)S(1)}, u32[]{:S(2)}, u32[]{:S(2)}) collective-permute-start(bf16[64,2048]{1,0:T(8,128)(2,1)S(1)} %get-tuple-element.31), channel_id=1, source_target_pairs={{0,80},{8,248},{16,64},{24,232},{32,112},{40,216},{48,96},{56,200}... | collective-permute-start | bytes 786440 | tf_op jit(solution)/shard_map/ppermute | solution.py:42
  163.5 9.2 %collective-permute-start.30 = (bf16[64,2048]{1,0:T(8,128)(2,1)S(1)}, bf16[64,2048]{1,0:T(8,128)(2,1)S(1)}, u32[]{:S(2)}, u32[]{:S(2)}) collective-permute-start(bf16[64,2048]{1,0:T(8,128)(2,1)S(1)} %get-tuple-element.32), channel_id=1, source_target_pairs={{0,64},{8,200},{16,80},{24,216},{32,96},{40,232},{48,112},{56,248}... | collective-permute-start | bytes 786440 | tf_op jit(solution)/shard_map/ppermute | solution.py:42
